TPU v7x, 32 devices: a whole 2x2x4 slice. The times are simulated.
32 devices in a mesh: wide: 16 (over z, y, core), narrow: 2 (over x).
Axes of the slice: x: 2, y: 2, z: 4, core: 2. Of those that a mesh axis runs over, the one named last changes fastest.
Arguments:
- tokens: bfloat16 [64, 336, 768], P(('wide', 'narrow')), may hold values from -6 to 6
- skip: bfloat16 [64, 336, 768], P(('wide', 'narrow')), may hold values from -6 to 6
- flags: int32 [64], P(('wide', 'narrow')), may hold values from 0 to 1
- cotangent: bfloat16 [64, 336, 768], P(('wide', 'narrow')), may hold values from -6 to 6
- norm_gains: bfloat16 [2, 2, 768], P(None, None, 'narrow'), may hold values from 0.5 to 1.5
- norm_biases: bfloat16 [2, 2, 768], P(None, None, 'narrow'), may hold values from -2 to 2
- qkv_weight: bfloat16 [2, 768, 2304], P(None, 'narrow'), may hold values from -0.21875 to 0.21875
- out_weight: bfloat16 [2, 768, 768], P(None, 'narrow'), may hold values from -1.25 to 1.25
- out_bias: bfloat16 [2, 768], P(None, 'narrow'), may hold values from -2 to 2
- up_weight: bfloat16 [2, 768, 3072], P(None, 'narrow'), may hold values from -0.21875 to 0.21875
- up_bias: bfloat16 [2, 3072], P(None, 'narrow'), may hold values from -2 to 2
- down_weight: bfloat16 [2, 3072, 768], P(None, 'narrow'), may hold values from -0.109375 to 0.109375
- down_bias: bfloat16 [2, 768], P(None, 'narrow'), may hold values from -2 to 2
- skip_weight: bfloat16 [1536, 768], P('narrow'), may hold values from -0.15625 to 0.15625
- skip_bias: bfloat16 [768], P('narrow'), may hold values from -2 to 2
Outputs:
- output: bfloat16 [64, 336, 768], P(('wide', 'narrow'))
- tokens_grad: float32 [64, 336, 768], P(('wide', 'narrow'))
- skip_grad: float32 [64, 336, 768], P(('wide', 'narrow'))
- norm_gains_grad: float32 [2, 2, 768], P(None, None, 'narrow')
- norm_biases_grad: float32 [2, 2, 768], P(None, None, 'narrow')
- qkv_weight_grad: float32 [2, 768, 2304], P(None, 'narrow')
- out_weight_grad: float32 [2, 768, 768], P(None, 'narrow')
- out_bias_grad: float32 [2, 768], P(None, 'narrow')
- up_weight_grad: float32 [2, 768, 3072], P(None, 'narrow')
- up_bias_grad: float32 [2, 3072], P(None, 'narrow')
- down_weight_grad: float32 [2, 3072, 768], P(None, 'narrow')
- down_bias_grad: float32 [2, 768], P(None, 'narrow')
- skip_weight_grad: float32 [1536, 768], P('narrow')
- skip_bias_grad: float32 [768], P('narrow')
Inputs may be any that keep to these rules, and one draw needn't show every extreme that they name: `flags`: 1 where the item holds 77 caption tokens, 0 where it holds none.
All inputs are finite; a program needn't handle non-finite values.
Results may differ from a plain program's by a relative error of at most 0.02.
Values may be sent and summed in bfloat16 or wider, within the bound.
No kernel may reach another device: no remote copies, remote signals or barrier semaphores. Data moves between devices by JAX's collectives and lax.ppermute only.
A program may use at most 256 MiB of HBM per device.

v0:
```python
import jax
import jax.numpy as jnp
from jax import lax
from jax.sharding import PartitionSpec as P

HEAD_DIM = 64
PATCHES = 256
CAPTION = 77


epsilon = 1e-05
masked_score = -1e30


def row_dot(left, right):
    return lax.dot_general(
        left, right, (((0,), (0,)), ((), ())), preferred_element_type=jnp.float32
    )


def back_dot(left, weight):
    return lax.dot_general(
        left, weight, (((1,), (1,)), ((), ())), preferred_element_type=jnp.float32
    )


def normalize(values):
    centred = values - jnp.mean(values, axis=-1, keepdims=True)
    factor = lax.rsqrt(jnp.mean(centred * centred, axis=-1, keepdims=True) + epsilon)
    return (centred * factor, factor)


def normalize_back(upstream, normed, factor):
    return factor * (
        upstream
        - jnp.mean(upstream, axis=-1, keepdims=True)
        - normed * jnp.mean(upstream * normed, axis=-1, keepdims=True)
    )


def score_block(queries, keys, valid):
    raw = jnp.einsum(
        "nqhd,nkhd->nhqk", queries, keys, preferred_element_type=jnp.float32
    ) * HEAD_DIM ** (-0.5)
    return jnp.where(valid[:, None, None, :], raw, masked_score)


def block_forward(inputs, params, valid):
    gains, shifts, qkv_weight, out_weight, out_bias, up_weight, up_bias, down_weight, down_bias = (
        params[:9]
    )
    batch_items, seq_rows, model_width = inputs.shape
    head_count = model_width // HEAD_DIM
    flat = inputs.reshape(batch_items * seq_rows, model_width)
    normed_one, factor_one = normalize(flat)
    first = (normed_one * gains[0] + shifts[0]).astype(jnp.bfloat16)
    packed = jnp.dot(first, qkv_weight, preferred_element_type=jnp.float32).astype(jnp.bfloat16)
    packed = packed.reshape(batch_items, seq_rows, 3, head_count, HEAD_DIM)
    queries = packed[:, :, 0]
    keys = packed[:, :, 1]
    values = packed[:, :, 2]
    scores = score_block(queries, keys, valid)
    largest = jnp.max(scores, axis=-1, keepdims=True)
    log_total = largest + jnp.log(jnp.sum(jnp.exp(scores - largest), axis=-1, keepdims=True))
    rounded_probs = jnp.exp(scores - log_total).astype(jnp.bfloat16)
    mixed = jnp.einsum("nhqk,nkhd->nqhd", rounded_probs, values, preferred_element_type=jnp.float32)
    mixed = mixed.reshape(batch_items * seq_rows, model_width).astype(jnp.bfloat16)
    middle = flat + jnp.dot(mixed, out_weight, preferred_element_type=jnp.float32) + out_bias
    normed_two, factor_two = normalize(middle)
    second = (normed_two * gains[1] + shifts[1]).astype(jnp.bfloat16)
    hidden_pre = jnp.dot(second, up_weight, preferred_element_type=jnp.float32) + up_bias
    hidden = jax.nn.gelu(hidden_pre, approximate=False).astype(jnp.bfloat16)
    result = middle + jnp.dot(hidden, down_weight, preferred_element_type=jnp.float32) + down_bias
    kept = (
        normed_one,
        factor_one,
        first,
        queries,
        keys,
        values,
        log_total,
        mixed,
        normed_two,
        factor_two,
        second,
        hidden_pre,
        hidden,
    )
    return (result.reshape(inputs.shape), kept)


def block_backward(upstream, params, kept, valid):
    gains, shifts, qkv_weight, out_weight, out_bias, up_weight, up_bias, down_weight, down_bias = (
        params[:9]
    )
    (
        normed_one,
        factor_one,
        first,
        queries,
        keys,
        values,
        log_total,
        mixed,
        normed_two,
        factor_two,
        second,
        hidden_pre,
        hidden,
    ) = kept
    batch_items, seq_rows, head_count, head_size = queries.shape
    model_width = head_count * head_size
    incoming = upstream.reshape(batch_items * seq_rows, model_width)
    rounded_out = incoming.astype(jnp.bfloat16)
    grad_down_weight = row_dot(hidden, rounded_out)
    grad_down_bias = jnp.sum(rounded_out.astype(jnp.float32), axis=0)
    grad_hidden = back_dot(rounded_out, down_weight)
    unused, gelu_back = jax.vjp(lambda before: jax.nn.gelu(before, approximate=False), hidden_pre)
    grad_pre = gelu_back(grad_hidden)[0].astype(jnp.bfloat16)
    grad_up_weight = row_dot(second, grad_pre)
    grad_up_bias = jnp.sum(grad_pre.astype(jnp.float32), axis=0)
    grad_second = back_dot(grad_pre, up_weight)
    gain_two = jnp.sum(grad_second * normed_two, axis=0)
    shift_two = jnp.sum(grad_second, axis=0)
    grad_middle = incoming + normalize_back(grad_second * gains[1], normed_two, factor_two)
    grad_branch = grad_middle.astype(jnp.bfloat16)
    grad_out_weight = row_dot(mixed, grad_branch)
    grad_out_bias = jnp.sum(grad_branch.astype(jnp.float32), axis=0)
    grad_mixed = back_dot(grad_branch, out_weight).astype(jnp.bfloat16)
    grad_mixed = grad_mixed.reshape(batch_items, seq_rows, head_count, head_size)
    scores = score_block(queries, keys, valid)
    probs = jnp.exp(scores - log_total)
    rounded_probs = probs.astype(jnp.bfloat16)
    grad_values = jnp.einsum(
        "nhqk,nqhd->nkhd", rounded_probs, grad_mixed, preferred_element_type=jnp.float32
    )
    grad_probs = jnp.einsum(
        "nqhd,nkhd->nhqk", grad_mixed, values, preferred_element_type=jnp.float32
    )
    grad_scores = probs * (grad_probs - jnp.sum(grad_probs * probs, axis=-1, keepdims=True))
    grad_scores = grad_scores.astype(jnp.bfloat16)
    grad_queries = jnp.einsum(
        "nhqk,nkhd->nqhd", grad_scores, keys, preferred_element_type=jnp.float32
    ) * HEAD_DIM ** (-0.5)
    grad_keys = jnp.einsum(
        "nhqk,nqhd->nkhd", grad_scores, queries, preferred_element_type=jnp.float32
    ) * HEAD_DIM ** (-0.5)
    grad_packed = jnp.stack([grad_queries, grad_keys, grad_values], axis=2)
    grad_packed = grad_packed.reshape(batch_items * seq_rows, 3 * model_width).astype(jnp.bfloat16)
    grad_qkv_weight = row_dot(first, grad_packed)
    grad_first = back_dot(grad_packed, qkv_weight)
    gain_one = jnp.sum(grad_first * normed_one, axis=0)
    shift_one = jnp.sum(grad_first, axis=0)
    grad_inputs = grad_middle + normalize_back(grad_first * gains[0], normed_one, factor_one)
    grads = (
        jnp.stack([gain_one, gain_two]),
        jnp.stack([shift_one, shift_two]),
        grad_qkv_weight,
        grad_out_weight,
        grad_out_bias,
        grad_up_weight,
        grad_up_bias,
        grad_down_weight,
        grad_down_bias,
    )
    return (grad_inputs.reshape(batch_items, seq_rows, model_width), grads)


def on_device(
    tokens,
    skip,
    flags,
    cotangent,
    norm_gains,
    norm_biases,
    qkv_weight,
    out_weight,
    out_bias,
    up_weight,
    up_bias,
    down_weight,
    down_bias,
    skip_weight,
    skip_bias,
):
    batch_items, seq_rows, model_width = tokens.shape
    lengths = PATCHES + 1 + CAPTION * flags
    valid = lax.broadcasted_iota(jnp.int32, (batch_items, seq_rows), 1) < lengths[:, None]
    first_params = (
        lax.all_gather(norm_gains[0], "narrow", axis=1, tiled=True),
        lax.all_gather(norm_biases[0], "narrow", axis=1, tiled=True),
        lax.all_gather(qkv_weight[0], "narrow", axis=0, tiled=True),
        lax.all_gather(out_weight[0], "narrow", axis=0, tiled=True),
        lax.all_gather(out_bias[0], "narrow", axis=0, tiled=True),
        lax.all_gather(up_weight[0], "narrow", axis=0, tiled=True),
        lax.all_gather(up_bias[0], "narrow", axis=0, tiled=True),
        lax.all_gather(down_weight[0], "narrow", axis=0, tiled=True),
        lax.all_gather(down_bias[0], "narrow", axis=0, tiled=True),
    )
    inputs = tokens.astype(jnp.float32)
    middle, first_kept = block_forward(inputs, first_params, valid)
    second_params = (
        lax.all_gather(norm_gains[1], "narrow", axis=1, tiled=True),
        lax.all_gather(norm_biases[1], "narrow", axis=1, tiled=True),
        lax.all_gather(qkv_weight[1], "narrow", axis=0, tiled=True),
        lax.all_gather(out_weight[1], "narrow", axis=0, tiled=True),
        lax.all_gather(out_bias[1], "narrow", axis=0, tiled=True),
        lax.all_gather(up_weight[1], "narrow", axis=0, tiled=True),
        lax.all_gather(up_bias[1], "narrow", axis=0, tiled=True),
        lax.all_gather(down_weight[1], "narrow", axis=0, tiled=True),
        lax.all_gather(down_bias[1], "narrow", axis=0, tiled=True),
        lax.all_gather(skip_weight, "narrow", axis=0, tiled=True),
        lax.all_gather(skip_bias, "narrow", axis=0, tiled=True),
    )
    joined = jnp.concatenate([middle.astype(jnp.bfloat16), skip], axis=-1)
    joined = joined.reshape(batch_items * seq_rows, 2 * model_width)
    entry = (
        jnp.dot(joined, second_params[9], preferred_element_type=jnp.float32) + second_params[10]
    )
    entry = entry.reshape(batch_items, seq_rows, model_width)
    final, second_kept = block_forward(entry, second_params, valid)
    row_valid = valid[:, :, None]
    output = jnp.where(row_valid, final, 0.0).astype(jnp.bfloat16)
    grad_final = jnp.where(row_valid, cotangent.astype(jnp.float32), 0.0)
    second_back = (
        lax.all_gather(norm_gains[1], "narrow", axis=1, tiled=True),
        lax.all_gather(norm_biases[1], "narrow", axis=1, tiled=True),
        lax.all_gather(qkv_weight[1], "narrow", axis=0, tiled=True),
        lax.all_gather(out_weight[1], "narrow", axis=0, tiled=True),
        lax.all_gather(out_bias[1], "narrow", axis=0, tiled=True),
        lax.all_gather(up_weight[1], "narrow", axis=0, tiled=True),
        lax.all_gather(up_bias[1], "narrow", axis=0, tiled=True),
        lax.all_gather(down_weight[1], "narrow", axis=0, tiled=True),
        lax.all_gather(down_bias[1], "narrow", axis=0, tiled=True),
        lax.all_gather(skip_weight, "narrow", axis=0, tiled=True),
        lax.all_gather(skip_bias, "narrow", axis=0, tiled=True),
    )
    unused_second, second_saved = block_forward(entry, second_back, valid)
    grad_entry, second_terms = block_backward(grad_final, second_back, second_saved, valid)
    rounded_entry = grad_entry.reshape(batch_items * seq_rows, model_width).astype(jnp.bfloat16)
    grad_skip_weight = row_dot(joined, rounded_entry)
    grad_skip_bias = jnp.sum(rounded_entry.astype(jnp.float32), axis=0)
    grad_joined = back_dot(rounded_entry, second_back[9]).reshape(
        batch_items, seq_rows, 2 * model_width
    )
    grad_middle = grad_joined[:, :, :model_width]
    skip_grad = grad_joined[:, :, model_width:]
    second_shards = (
        lax.psum_scatter(
            second_terms[0].astype(jnp.bfloat16), "narrow", scatter_dimension=1, tiled=True
        ).astype(jnp.float32),
        lax.psum_scatter(
            second_terms[1].astype(jnp.bfloat16), "narrow", scatter_dimension=1, tiled=True
        ).astype(jnp.float32),
        lax.psum_scatter(
            second_terms[2].astype(jnp.bfloat16), "narrow", scatter_dimension=0, tiled=True
        ).astype(jnp.float32),
        lax.psum_scatter(
            second_terms[3].astype(jnp.bfloat16), "narrow", scatter_dimension=0, tiled=True
        ).astype(jnp.float32),
        lax.psum_scatter(
            second_terms[4].astype(jnp.bfloat16), "narrow", scatter_dimension=0, tiled=True
        ).astype(jnp.float32),
        lax.psum_scatter(
            second_terms[5].astype(jnp.bfloat16), "narrow", scatter_dimension=0, tiled=True
        ).astype(jnp.float32),
        lax.psum_scatter(
            second_terms[6].astype(jnp.bfloat16), "narrow", scatter_dimension=0, tiled=True
        ).astype(jnp.float32),
        lax.psum_scatter(
            second_terms[7].astype(jnp.bfloat16), "narrow", scatter_dimension=0, tiled=True
        ).astype(jnp.float32),
        lax.psum_scatter(
            second_terms[8].astype(jnp.bfloat16), "narrow", scatter_dimension=0, tiled=True
        ).astype(jnp.float32),
        lax.psum_scatter(
            grad_skip_weight.astype(jnp.bfloat16), "narrow", scatter_dimension=0, tiled=True
        ).astype(jnp.float32),
        lax.psum_scatter(
            grad_skip_bias.astype(jnp.bfloat16), "narrow", scatter_dimension=0, tiled=True
        ).astype(jnp.float32),
    )
    first_back = (
        lax.all_gather(norm_gains[0], "narrow", axis=1, tiled=True),
        lax.all_gather(norm_biases[0], "narrow", axis=1, tiled=True),
        lax.all_gather(qkv_weight[0], "narrow", axis=0, tiled=True),
        lax.all_gather(out_weight[0], "narrow", axis=0, tiled=True),
        lax.all_gather(out_bias[0], "narrow", axis=0, tiled=True),
        lax.all_gather(up_weight[0], "narrow", axis=0, tiled=True),
        lax.all_gather(up_bias[0], "narrow", axis=0, tiled=True),
        lax.all_gather(down_weight[0], "narrow", axis=0, tiled=True),
        lax.all_gather(down_bias[0], "narrow", axis=0, tiled=True),
    )
    unused_first, first_saved = block_forward(inputs, first_back, valid)
    tokens_grad, first_terms = block_backward(grad_middle, first_back, first_saved, valid)
    first_shards = (
        lax.psum_scatter(
            first_terms[0].astype(jnp.bfloat16), "narrow", scatter_dimension=1, tiled=True
        ).astype(jnp.float32),
        lax.psum_scatter(
            first_terms[1].astype(jnp.bfloat16), "narrow", scatter_dimension=1, tiled=True
        ).astype(jnp.float32),
        lax.psum_scatter(
            first_terms[2].astype(jnp.bfloat16), "narrow", scatter_dimension=0, tiled=True
        ).astype(jnp.float32),
        lax.psum_scatter(
            first_terms[3].astype(jnp.bfloat16), "narrow", scatter_dimension=0, tiled=True
        ).astype(jnp.float32),
        lax.psum_scatter(
            first_terms[4].astype(jnp.bfloat16), "narrow", scatter_dimension=0, tiled=True
        ).astype(jnp.float32),
        lax.psum_scatter(
            first_terms[5].astype(jnp.bfloat16), "narrow", scatter_dimension=0, tiled=True
        ).astype(jnp.float32),
        lax.psum_scatter(
            first_terms[6].astype(jnp.bfloat16), "narrow", scatter_dimension=0, tiled=True
        ).astype(jnp.float32),
        lax.psum_scatter(
            first_terms[7].astype(jnp.bfloat16), "narrow", scatter_dimension=0, tiled=True
        ).astype(jnp.float32),
        lax.psum_scatter(
            first_terms[8].astype(jnp.bfloat16), "narrow", scatter_dimension=0, tiled=True
        ).astype(jnp.float32),
    )
    summed = (
        lax.psum(first_shards[0].astype(jnp.bfloat16), "wide").astype(jnp.float32),
        lax.psum(first_shards[1].astype(jnp.bfloat16), "wide").astype(jnp.float32),
        lax.psum(first_shards[2].astype(jnp.bfloat16), "wide").astype(jnp.float32),
        lax.psum(first_shards[3].astype(jnp.bfloat16), "wide").astype(jnp.float32),
        lax.psum(first_shards[4].astype(jnp.bfloat16), "wide").astype(jnp.float32),
        lax.psum(first_shards[5].astype(jnp.bfloat16), "wide").astype(jnp.float32),
        lax.psum(first_shards[6].astype(jnp.bfloat16), "wide").astype(jnp.float32),
        lax.psum(first_shards[7].astype(jnp.bfloat16), "wide").astype(jnp.float32),
        lax.psum(first_shards[8].astype(jnp.bfloat16), "wide").astype(jnp.float32),
        lax.psum(second_shards[0].astype(jnp.bfloat16), "wide").astype(jnp.float32),
        lax.psum(second_shards[1].astype(jnp.bfloat16), "wide").astype(jnp.float32),
        lax.psum(second_shards[2].astype(jnp.bfloat16), "wide").astype(jnp.float32),
        lax.psum(second_shards[3].astype(jnp.bfloat16), "wide").astype(jnp.float32),
        lax.psum(second_shards[4].astype(jnp.bfloat16), "wide").astype(jnp.float32),
        lax.psum(second_shards[5].astype(jnp.bfloat16), "wide").astype(jnp.float32),
        lax.psum(second_shards[6].astype(jnp.bfloat16), "wide").astype(jnp.float32),
        lax.psum(second_shards[7].astype(jnp.bfloat16), "wide").astype(jnp.float32),
        lax.psum(second_shards[8].astype(jnp.bfloat16), "wide").astype(jnp.float32),
        lax.psum(second_shards[9].astype(jnp.bfloat16), "wide").astype(jnp.float32),
        lax.psum(second_shards[10].astype(jnp.bfloat16), "wide").astype(jnp.float32),
    )
    inverse = 1.0 / lax.axis_size("wide")
    scaled = [piece * inverse for piece in summed]
    lower = scaled[:9]
    upper = scaled[9:]
    stacked = [jnp.stack([lower[position], upper[position]]) for position in range(9)]
    return (
        output,
        tokens_grad,
        skip_grad,
        stacked[0],
        stacked[1],
        stacked[2],
        stacked[3],
        stacked[4],
        stacked[5],
        stacked[6],
        stacked[7],
        stacked[8],
        upper[9],
        upper[10],
    )


def solution(mesh):
    placed = (
        P(("wide", "narrow"), None, None),
        P(("wide", "narrow"), None, None),
        P(("wide", "narrow")),
        P(("wide", "narrow"), None, None),
        P(None, None, "narrow"),
        P(None, None, "narrow"),
        P(None, "narrow", None),
        P(None, "narrow", None),
        P(None, "narrow"),
        P(None, "narrow", None),
        P(None, "narrow"),
        P(None, "narrow", None),
        P(None, "narrow"),
        P("narrow", None),
        P("narrow"),
    )
    return jax.shard_map(
        on_device,
        mesh=mesh,
        in_specs=placed,
        out_specs=(
            P(("wide", "narrow"), None, None),
            P(("wide", "narrow"), None, None),
            P(("wide", "narrow"), None, None),
            P(None, None, "narrow"),
            P(None, None, "narrow"),
            P(None, "narrow", None),
            P(None, "narrow", None),
            P(None, "narrow"),
            P(None, "narrow", None),
            P(None, "narrow"),
            P(None, "narrow", None),
            P(None, "narrow"),
            P("narrow", None),
            P("narrow"),
        ),
        check_vma=False,
    )
```

profile of v0, /device:TPU:1, one launch (start us, length us, event | category | flops | bytes accessed | tf_op | source)
XLA Modules:
  0.0 1348.5 jit_solution(8273705058748860444)
XLA Ops:
  68.8 7.0 convolution_convert_fusion.7
  75.8 10.3 reshape.348
  86.1 5.8 fusion.109
  111.7 7.9 fusion.53
  125.9 26.6 %all-gather.35.cloned.1.call-done = bf16[1,768,3072]{2,1,0:T(8,128)(2,1)} async-done(((bf16[1,384,3072]{2,1,0:T(8,128)(2,1)}), bf16[1,768,3072]{2,1,0:T(8,128)(2,1)}) %all-gather.35.cloned.1.call-update) | async-done | bytes 4718608 | tf_op jit(solution)/shard_map/all_gather | solution.py:195
  152.6 25.3 %multiply_convert_fusion.3 = (bf16[672,3072]{1,0:T(8,128)(2,1)}, f32[672,3072]{1,0:T(8,128)}, f32[672,3072]{1,0:T(8,128)}) fusion(f32[3072]{0:T(1024)S(1)} %bitcast.257, bf16[1,768,3072]{2,1,0:T(8,128)(2,1)} %all-gather.35.cloned.1.call-done, f32[768]{0:T(1024)S(1)} %get-tuple-element.38, f32[768]{0:T(1024)S(1)} %get-tuple-element.36, ...), kind=kOutput, calls=%fused_computation.33 | convolution fusion | flops 3310239744 | bytes 27453696 | tf_op jit(solution)/shard_map/dot_general | solution.py:71
  177.9 38.8 %all-gather.37.cloned.1.call-done = bf16[1,3072,768]{2,1,0:T(8,128)(2,1)} async-done(((bf16[1,1536,768]{2,1,0:T(8,128)(2,1)}), bf16[1,3072,768]{2,1,0:T(8,128)(2,1)}) %all-gather.37.cloned.1.call-update) | async-done | bytes 4718608 | tf_op jit(solution)/shard_map/all_gather | solution.py:197
  216.7 7.0 add_convert_fusion.5
  225.2 29.0 %all-gather.29.cloned.1.call-done = bf16[1536,768]{1,0:T(8,128)(2,1)} async-done(((bf16[768,768]{1,0:T(8,128)(2,1)}), bf16[1536,768]{1,0:T(8,128)(2,1)}) %all-gather.29.cloned.1.call-update) | async-done | bytes 2359312 | tf_op jit(solution)/shard_map/all_gather | solution.py:212
  258.8 46.1 %all-gather.39.cloned.1.call-done = bf16[1,768,2304]{2,1,0:T(8,128)(2,1)} async-done(((bf16[1,384,2304]{2,1,0:T(8,128)(2,1)}), bf16[1,768,2304]{2,1,0:T(8,128)(2,1)}) %all-gather.39.cloned.1.call-update) | async-done | bytes 3538960 | tf_op jit(solution)/shard_map/all_gather | solution.py:205
  305.0 6.5 convolution_convert_fusion.6
  311.5 10.4 reshape.349
  321.9 5.8 fusion.108
  336.7 5.4 fusion.1
  350.3 7.8 fusion.54
  365.9 28.2 %all-gather.43.cloned.1.call-done = bf16[1,768,3072]{2,1,0:T(8,128)(2,1)} async-done(((bf16[1,384,3072]{2,1,0:T(8,128)(2,1)}), bf16[1,768,3072]{2,1,0:T(8,128)(2,1)}) %all-gather.43.cloned.1.call-update) | async-done | bytes 4718608 | tf_op jit(solution)/shard_map/all_gather | solution.py:208
  394.1 25.8 %multiply_convert_fusion.2 = (bf16[672,3072]{1,0:T(8,128)(2,1)}, f32[672,3072]{1,0:T(8,128)}, f32[672,3072]{1,0:T(8,128)}) fusion(f32[3072]{0:T(1024)S(1)} %bitcast.259, bf16[1,768,3072]{2,1,0:T(8,128)(2,1)} %all-gather.43.cloned.1.call-done, f32[672,768]{1,0:T(8,128)} %copy-done.23, f32[768]{0:T(1024)S(1)} %copy-done.100, f32[768]{0:T(1024)S(1)} %copy-done.82, ...), kind=kOutput, calls=%fused_computation.20 | convolution fusion | flops 3309723648 | bytes 27450624 | tf_op jit(solution)/shard_map/dot_general | solution.py:71
  419.9 38.5 %all-gather.45.cloned.1.call-done = bf16[1,3072,768]{2,1,0:T(8,128)(2,1)} async-done(((bf16[1,1536,768]{2,1,0:T(8,128)(2,1)}), bf16[1,3072,768]{2,1,0:T(8,128)(2,1)}) %all-gather.45.cloned.1.call-update) | async-done | bytes 4718608 | tf_op jit(solution)/shard_map/all_gather | solution.py:210
  458.4 11.8 fusion.121
  485.5 10.3 multiply_reduce_fusion.1
  495.9 8.1 multiply_convert_fusion.1
  521.8 7.6 multiply_reduce_fusion.3
  536.2 11.3 fusion.122
  547.6 7.8 multiply_reduce_fusion.4
  559.9 5.2 convolution_convert_fusion.8
  565.1 7.4 convolution_convert_fusion
  585.7 10.4 multiply_reduce_fusion
  596.1 7.9 multiply_convert_fusion
  613.2 5.4 copy.98
  618.6 8.6 convert_element_type.377
  627.2 7.5 convolution_convert_fusion.1
  635.9 7.9 convolution_convert_fusion.3
  644.4 9.2 convolution_convert_fusion.5
  654.3 9.1 convolution_convert_fusion.4
  664.7 7.8 convolution_convert_fusion.2
  673.2 8.3 fusion.104
  685.4 33.5 %reduce-scatter.22.cloned.1.call-done = bf16[384,2304]{1,0:T(8,128)(2,1)} async-done(((bf16[768,2304]{1,0:T(8,128)(2,1)}), bf16[384,2304]{1,0:T(8,128)(2,1)}) %reduce-scatter.22.cloned.1.call-update) | async-done | bytes 1769488 | tf_op jit(solution)/shard_map/reduce_scatter | solution.py:303
  718.9 62.3 %reduce-scatter.34.cloned.1.call-done = bf16[1536,768]{1,0:T(8,128)(2,1)} async-done(((bf16[3072,768]{1,0:T(8,128)(2,1)}), bf16[1536,768]{1,0:T(8,128)(2,1)}) %reduce-scatter.34.cloned.1.call-update) | async-done | bytes 2359312 | tf_op jit(solution)/shard_map/reduce_scatter | solution.py:318
  781.2 62.8 %reduce-scatter.30.cloned.1.call-done = bf16[384,3072]{1,0:T(8,128)(2,1)} async-done(((bf16[768,3072]{1,0:T(8,128)(2,1)}), bf16[384,3072]{1,0:T(8,128)(2,1)}) %reduce-scatter.30.cloned.1.call-update) | async-done | bytes 2359312 | tf_op jit(solution)/shard_map/reduce_scatter | solution.py:312
  844.0 62.9 %reduce-scatter.32.cloned.1.call-done = bf16[384,3072]{1,0:T(8,128)(2,1)} async-done(((bf16[768,3072]{1,0:T(8,128)(2,1)}), bf16[384,3072]{1,0:T(8,128)(2,1)}) %reduce-scatter.32.cloned.1.call-update) | async-done | bytes 2359312 | tf_op jit(solution)/shard_map/reduce_scatter | solution.py:264
  906.9 62.8 %reduce-scatter.36.cloned.1.call-done = bf16[1536,768]{1,0:T(8,128)(2,1)} async-done(((bf16[3072,768]{1,0:T(8,128)(2,1)}), bf16[1536,768]{1,0:T(8,128)(2,1)}) %reduce-scatter.36.cloned.1.call-update) | async-done | bytes 2359312 | tf_op jit(solution)/shard_map/reduce_scatter | solution.py:270
  977.2 7.7 add_add_fusion
  986.3 5.2 all-reduce.9
  998.2 11.3 reduce-scatter.40.cloned.1.call-done
  1010.5 12.9 reduce-scatter.42.cloned.1.call-done
  1024.3 60.0 %all-reduce.7 = (bf16[2,384]{1,0:T(2,128)(2,1)S(1)}, bf16[2,384]{1,0:T(2,128)(2,1)S(1)}, bf16[2,384]{1,0:T(2,128)(2,1)S(1)}, bf16[2,384]{1,0:T(2,128)(2,1)S(1)},...) all-reduce(bf16[2,384]{1,0:T(2,128)(2,1)S(1)} %copy.110, ...), channel_id=1, replica_groups=mesh['wide'=16,'narrow'=2] {'wide'}, use_global_device_ids=true, to_apply=%region_29.30 | all-reduce | flops 8064 | bytes 32256 | tf_op jit(solution)/shard_map/psum | solution.py:335
  1088.1 223.3 %all-reduce.12.cloned.1.call-done = (bf16[384,2304]{1,0:T(8,128)(2,1)}, bf16[384,2304]{1,0:T(8,128)(2,1)}, bf16[384,768]{1,0:T(8,128)(2,1)}, bf16[384,768]{1,0:T...) async-done(((bf16[384,2304]{1,0:T(8,128)(2,1)}, ...) | async-done | bytes 15335440 | tf_op jit(solution)/shard_map/psum | solution.py:337
  1330.3 5.1 pad_maximum_fusion
  (472 shorter events, 237.4 us)
Async XLA Ops:
  7.2 61.6 %all-gather.31.cloned.1.call-start = ((), (), s32[]{:S(2)}) async-start(), calls=%async_computation.23 | async-start | bytes 5308416 | tf_op jit(solution)/shard_map/all_gather | solution.py:192
  11.4 111.2 %all-gather.33.cloned.1.call-start = ((), (), s32[]{:S(2)}) async-start(), calls=%async_computation.24 | async-start | bytes 1769472 | tf_op jit(solution)/shard_map/all_gather | solution.py:193
  12.6 140.0 %all-gather.35.cloned.1.call-start = ((), (), s32[]{:S(2)}) async-start(), calls=%async_computation.25 | async-start | bytes 7077888 | tf_op jit(solution)/shard_map/all_gather | solution.py:195
  17.5 199.1 %all-gather.37.cloned.1.call-start = ((), (), s32[]{:S(2)}) async-start(), calls=%async_computation.26 | async-start | bytes 7077888 | tf_op jit(solution)/shard_map/all_gather | solution.py:197
  22.6 231.5 %all-gather.29.cloned.1.call-start = ((), (), s32[]{:S(2)}) async-start(), calls=%async_computation.13 | async-start | bytes 3538944 | tf_op jit(solution)/shard_map/all_gather | solution.py:212
  23.2 281.7 %all-gather.39.cloned.1.call-start = ((), (), s32[]{:S(2)}) async-start(), calls=%async_computation.27 | async-start | bytes 5308416 | tf_op jit(solution)/shard_map/all_gather | solution.py:205
  23.8 337.4 %all-gather.41.cloned.1.call-start = ((), (), s32[]{:S(2)}) async-start(), calls=%async_computation.28 | async-start | bytes 1769472 | tf_op jit(solution)/shard_map/all_gather | solution.py:206
  24.6 369.5 %all-gather.43.cloned.1.call-start = ((), (), s32[]{:S(2)}) async-start(), calls=%async_computation.29 | async-start | bytes 7077888 | tf_op jit(solution)/shard_map/all_gather | solution.py:208
  24.7 41.0 %copy-start.31 = (bf16[2,336,768]{2,1,0:T(8,128)(2,1)S(1)}, bf16[2,336,768]{2,1,0:T(8,128)(2,1)}, u32[]{:S(2)}) copy-start(bf16[2,336,768]{2,1,0:T(8,128)(2,1)} %param.18) | copy-start | bytes 3096580
  25.4 433.0 %all-gather.45.cloned.1.call-start = ((), (), s32[]{:S(2)}) async-start(), calls=%async_computation.30 | async-start | bytes 7077888 | tf_op jit(solution)/shard_map/all_gather | solution.py:210
  26.1 659.3 %reduce-scatter.28.cloned.1.call-start = ((), (), s32[]{:S(2)}) async-start(), calls=%async_computation.17 | async-start | bytes 1769472 | tf_op jit(solution)/shard_map/reduce_scatter | solution.py:258
  26.4 39.6 %copy-start.59 = (f32[2,336]{1,0:T(2,128)}, f32[2,336]{1,0:T(2,128)S(1)}, u32[]{:S(2)}) copy-start(f32[2,336]{1,0:T(2,128)S(1)} %broadcast_multiply_fusion.11) | copy-start | bytes 8068
  26.9 41.8 %copy-start.63 = (f32[672]{0:T(1024)}, f32[672]{0:T(1024)S(1)}, u32[]{:S(2)}) copy-start(f32[672]{0:T(1024)S(1)} %div.59) | copy-start | bytes 8068
  26.9 39.1 %copy-start.73 = (f32[2,336]{1,0:T(2,128)}, f32[2,336]{1,0:T(2,128)S(1)}, u32[]{:S(2)}) copy-start(f32[2,336]{1,0:T(2,128)S(1)} %add_rsqrt_fusion.3) | copy-start | bytes 8068
  27.0 41.7 %copy-start.65 = (f32[672]{0:T(1024)}, f32[672]{0:T(1024)S(1)}, u32[]{:S(2)}) copy-start(f32[672]{0:T(1024)S(1)} %rsqrt.41) | copy-start | bytes 8068
  31.4 37.4 %copy-start.67 = (f32[768]{0:T(1024)}, f32[768]{0:T(1024)S(1)}, u32[]{:S(2)}) copy-start(f32[768]{0:T(1024)S(1)} %get-tuple-element.37) | copy-start | bytes 9220
  31.4 121.2 %copy-start.80 = (f32[768]{0:T(1024)}, f32[768]{0:T(1024)S(1)}, u32[]{:S(2)}) copy-start(f32[768]{0:T(1024)S(1)} %get-tuple-element.36) | copy-start | bytes 9220
  34.9 33.8 %copy-start.84 = (f32[768]{0:T(1024)}, f32[768]{0:T(1024)S(1)}, u32[]{:S(2)}) copy-start(f32[768]{0:T(1024)S(1)} %get-tuple-element.39) | copy-start | bytes 9220
  35.0 117.6 %copy-start.98 = (f32[768]{0:T(1024)}, f32[768]{0:T(1024)S(1)}, u32[]{:S(2)}) copy-start(f32[768]{0:T(1024)S(1)} %get-tuple-element.38) | copy-start | bytes 9220
  38.6 178.1 %copy-start.57 = (f32[768]{0:T(1024)}, f32[768]{0:T(1024)S(1)}, u32[]{:S(2)}) copy-start(f32[768]{0:T(1024)S(1)} %convert_reduce_fusion.7) | copy-start | bytes 9220
  42.3 110.3 %copy-start.90 = (f32[1,3072]{1,0:T(1,128)}, f32[1,3072]{1,0:T(1,128)S(1)}, u32[]{:S(2)}) copy-start(f32[1,3072]{1,0:T(1,128)S(1)} %convert_element_type.412) | copy-start | bytes 36868
  54.0 250.9 %copy-start.76 = (f32[768]{0:T(1024)}, f32[768]{0:T(1024)S(1)}, u32[]{:S(2)}) copy-start(f32[768]{0:T(1024)S(1)} %get-tuple-element.33) | copy-start | bytes 9220
  58.2 246.8 %copy-start.102 = (f32[768]{0:T(1024)}, f32[768]{0:T(1024)S(1)}, u32[]{:S(2)}) copy-start(f32[768]{0:T(1024)S(1)} %get-tuple-element.35) | copy-start | bytes 9220
  125.2 91.4 %copy-start.4 = (f32[672,768]{1,0:T(8,128)}, f32[672,768]{1,0:T(8,128)S(1)}, u32[]{:S(2)}) copy-start(f32[672,768]{1,0:T(8,128)S(1)} %bitcast_add_fusion.2) | copy-start | bytes 6193156
  125.5 52.4 %copy-start.69 = (f32[672]{0:T(1024)}, f32[672]{0:T(1024)S(1)}, u32[]{:S(2)}) copy-start(f32[672]{0:T(1024)S(1)} %broadcast_multiply_fusion.10) | copy-start | bytes 8068
  125.9 51.9 %copy-start.86 = (f32[672]{0:T(1024)}, f32[672]{0:T(1024)S(1)}, u32[]{:S(2)}) copy-start(f32[672]{0:T(1024)S(1)} %add_rsqrt_fusion.2) | copy-start | bytes 8068
  258.3 53.1 %copy-start.16 = (f32[672,768]{1,0:T(8,128)}, f32[672,768]{1,0:T(8,128)S(1)}, u32[]{:S(2)}) copy-start(f32[672,768]{1,0:T(8,128)S(1)} %get-tuple-element.109) | copy-start | bytes 6193156
  258.4 53.1 %copy-start.61 = (f32[672]{0:T(1024)}, f32[672]{0:T(1024)S(1)}, u32[]{:S(2)}) copy-start(f32[672]{0:T(1024)S(1)} %broadcast_multiply_fusion.9) | copy-start | bytes 8068
  258.8 52.7 %copy-start.78 = (f32[672]{0:T(1024)}, f32[672]{0:T(1024)S(1)}, u32[]{:S(2)}) copy-start(f32[672]{0:T(1024)S(1)} %add_rsqrt_fusion.1) | copy-start | bytes 8068
  347.0 148.9 %copy-start.55 = (f32[2,12,336]{2,1,0:T(8,128)}, f32[2,12,336]{2,1,0:T(8,128)S(1)}, u32[]{:S(2)}) copy-start(f32[2,12,336]{2,1,0:T(8,128)S(1)} %log_add_fusion) | copy-start | bytes 96772
  361.2 32.9 %copy-start.92 = (f32[1,3072]{1,0:T(1,128)S(1)}, f32[1,3072]{1,0:T(1,128)}, u32[]{:S(2)}) copy-start(f32[1,3072]{1,0:T(1,128)} %convert_element_type.415) | copy-start | bytes 36868
  361.2 32.9 %copy-start.100 = (f32[768]{0:T(1024)S(1)}, f32[768]{0:T(1024)}, u32[]{:S(2)}) copy-start(f32[768]{0:T(1024)} %get-tuple-element.34) | copy-start | bytes 9220
  364.1 110.5 %copy-start.71 = (f32[672]{0:T(1024)}, f32[672]{0:T(1024)S(1)}, u32[]{:S(2)}) copy-start(f32[672]{0:T(1024)S(1)} %broadcast_multiply_fusion.8) | copy-start | bytes 8068
  365.9 108.7 %copy-start.88 = (f32[672]{0:T(1024)}, f32[672]{0:T(1024)S(1)}, u32[]{:S(2)}) copy-start(f32[672]{0:T(1024)S(1)} %add_rsqrt_fusion) | copy-start | bytes 8068
  394.1 64.2 %copy-start.43 = (bf16[672,768]{1,0:T(8,128)(2,1)S(1)}, bf16[672,768]{1,0:T(8,128)(2,1)}, u32[]{:S(2)}) copy-start(bf16[672,768]{1,0:T(8,128)(2,1)} %bitcast_convert_fusion.1) | copy-start | bytes 3096580
  535.6 149.8 %reduce-scatter.26.cloned.1.call-start = ((), (), s32[]{:S(2)}) async-start(), calls=%async_computation.16 | async-start | bytes 1769472 | tf_op jit(solution)/shard_map/reduce_scatter | solution.py:306
  559.8 125.6 %reduce-scatter.38.cloned.1.call-start = ((), (), s32[]{:S(2)}) async-start(), calls=%async_computation.22 | async-start | bytes 3538944 | tf_op jit(solution)/shard_map/reduce_scatter | solution.py:276
  565.1 120.4 %reduce-scatter.24.cloned.1.call-start = ((), (), s32[]{:S(2)}) async-start(), calls=%async_computation.15 | async-start | bytes 5308416 | tf_op jit(solution)/shard_map/reduce_scatter | solution.py:255
  572.6 146.3 %reduce-scatter.22.cloned.1.call-start = ((), (), s32[]{:S(2)}) async-start(), calls=%async_computation.14 | async-start | bytes 5308416 | tf_op jit(solution)/shard_map/reduce_scatter | solution.py:303
  634.7 146.6 %reduce-scatter.34.cloned.1.call-start = ((), (), s32[]{:S(2)}) async-start(), calls=%async_computation.20 | async-start | bytes 7077888 | tf_op jit(solution)/shard_map/reduce_scatter | solution.py:318
  643.8 200.2 %reduce-scatter.30.cloned.1.call-start = ((), (), s32[]{:S(2)}) async-start(), calls=%async_computation.18 | async-start | bytes 7077888 | tf_op jit(solution)/shard_map/reduce_scatter | solution.py:312
  653.6 253.2 %reduce-scatter.32.cloned.1.call-start = ((), (), s32[]{:S(2)}) async-start(), calls=%async_computation.19 | async-start | bytes 7077888 | tf_op jit(solution)/shard_map/reduce_scatter | solution.py:264
  663.5 306.1 %reduce-scatter.36.cloned.1.call-start = ((), (), s32[]{:S(2)}) async-start(), calls=%async_computation.21 | async-start | bytes 7077888 | tf_op jit(solution)/shard_map/reduce_scatter | solution.py:270
  672.5 323.7 %reduce-scatter.44.cloned.1.call-start = ((), (), s32[]{:S(2)}) async-start(), calls=%async_computation.33 | async-start | bytes 294912
  682.5 314.8 %reduce-scatter.46.cloned.1.call-start = ((), (), s32[]{:S(2)}) async-start(), calls=%async_computation.34 | async-start | bytes 294912
  683.4 326.1 %reduce-scatter.40.cloned.1.call-start = ((), (), s32[]{:S(2)}) async-start(), calls=%async_computation.31 | async-start | bytes 294912
  684.4 339.0 %reduce-scatter.42.cloned.1.call-start = ((), (), s32[]{:S(2)}) async-start(), calls=%async_computation.32 | async-start | bytes 294912
  685.3 626.1 %all-reduce.12.cloned.1.call-start = ((), (), s32[]{:S(2)}) async-start(), calls=%async_computation.35 | async-start | bytes 30670848 | tf_op jit(solution)/shard_map/psum | solution.py:337
  (97 other events, 544.0 us)
Sparse Core Ops, SparseCore 0:
  11.5 51.7 all-gather.30
  64.9 22.7 all-gather.32
  89.8 62.7 all-gather.34
  154.0 62.6 all-gather.36
  218.0 36.0 all-gather.28
  255.5 49.3 all-gather.38
  306.5 22.7 all-gather.40
  331.4 62.6 all-gather.42
  395.7 62.6 all-gather.44
  535.7 21.7 reduce-scatter.27
  559.9 21.7 reduce-scatter.25
  584.4 34.6 reduce-scatter.37
  621.4 47.6 reduce-scatter.23
  671.2 47.6 reduce-scatter.21
  721.2 59.9 reduce-scatter.33
  784.0 59.9 reduce-scatter.29
  846.8 59.9 reduce-scatter.31
  909.6 59.9 reduce-scatter.35
  971.9 10.9 reduce-scatter.43
  985.1 11.0 reduce-scatter.45
  998.5 10.9 reduce-scatter.39
  1012.4 10.9 reduce-scatter.41
  1030.5 280.8 all-reduce.11
where the time goes:
time: 1350 us
  waiting for transfers between devices  742 us (55%)
  matrix products  265 us (20%)
  local copies, waits for them, and re-layouts  145 us (11%)
  blocking collectives  104 us (8%)
  other arithmetic  72.6 us (5%)
  between operations  17.4 us (1%)
    psum x1, waiting for transfers between devices, on_device(): lax.psum(second_shards[2].astype(jnp.bfloat16), 'wide').astype(jnp.float32)  223 us
    reduce_scatter x1, waiting for transfers between devices, on_device(): lax.psum_scatter(second_terms[5].astype(jnp.bfloat16), 'narrow', scatter_...  62.9 us
    reduce_scatter x1, waiting for transfers between devices, on_device(): lax.psum_scatter(second_terms[7].astype(jnp.bfloat16), 'narrow', scatter_...  62.8 us
    reduce_scatter x1, waiting for transfers between devices, on_device(): lax.psum_scatter(first_terms[5].astype(jnp.bfloat16), 'narrow', scatter_d...  62.8 us
    reduce_scatter x1, waiting for transfers between devices, on_device(): lax.psum_scatter(first_terms[7].astype(jnp.bfloat16), 'narrow', scatter_d...  62.3 us
    psum x1, blocking collectives, on_device(): lax.psum(second_shards[0].astype(jnp.bfloat16), 'wide').astype(jnp.float32)  60 us
    dot_general x9, matrix products, row_dot(): lax.dot_general(left, right, (((0,), (0,)), ((), ())), preferred_element_...  58.4 us
    dot_general x9, matrix products, back_dot(): lax.dot_general(left, weight, (((1,), (1,)), ((), ())), preferred_element...  57.9 us
  transfers between devices with their start and end apart: 23, of which 14 were waited for; matrix products, arithmetic and copies ran while one was open for 27% of the time, Pallas kernels for 0%

commit v1 on v0

v1 whole, which is shorter than its diff:
```python
import jax
import jax.numpy as jnp
from jax import lax
from jax.sharding import PartitionSpec as P

HEAD_DIM = 64
PATCHES = 256
CAPTION = 77


epsilon = 1e-05
masked_score = -1e30


def row_dot(left, right):
    return lax.dot_general(
        left, right, (((0,), (0,)), ((), ())), preferred_element_type=jnp.float32
    )


def back_dot(left, weight):
    return lax.dot_general(
        left, weight, (((1,), (1,)), ((), ())), preferred_element_type=jnp.float32
    )


def normalize(values):
    centred = values - jnp.mean(values, axis=-1, keepdims=True)
    factor = lax.rsqrt(jnp.mean(centred * centred, axis=-1, keepdims=True) + epsilon)
    return (centred * factor, factor)


def normalize_back(upstream, normed, factor):
    return factor * (
        upstream
        - jnp.mean(upstream, axis=-1, keepdims=True)
        - normed * jnp.mean(upstream * normed, axis=-1, keepdims=True)
    )


def score_block(queries, keys, valid):
    raw = jnp.einsum(
        "nqhd,nkhd->nhqk", queries, keys, preferred_element_type=jnp.float32
    ) * HEAD_DIM ** (-0.5)
    return jnp.where(valid[:, None, None, :], raw, masked_score)


def block_forward(inputs, params, valid):
    gains, shifts, qkv_weight, out_weight, out_bias, up_weight, up_bias, down_weight, down_bias = (
        params[:9]
    )
    batch_items, seq_rows, model_width = inputs.shape
    head_count = model_width // HEAD_DIM
    flat = inputs.reshape(batch_items * seq_rows, model_width)
    normed_one, factor_one = normalize(flat)
    first = (normed_one * gains[0] + shifts[0]).astype(jnp.bfloat16)
    packed = jnp.dot(first, qkv_weight, preferred_element_type=jnp.float32).astype(jnp.bfloat16)
    packed = packed.reshape(batch_items, seq_rows, 3, head_count, HEAD_DIM)
    queries = packed[:, :, 0]
    keys = packed[:, :, 1]
    values = packed[:, :, 2]
    scores = score_block(queries, keys, valid)
    largest = jnp.max(scores, axis=-1, keepdims=True)
    log_total = largest + jnp.log(jnp.sum(jnp.exp(scores - largest), axis=-1, keepdims=True))
    rounded_probs = jnp.exp(scores - log_total).astype(jnp.bfloat16)
    mixed = jnp.einsum("nhqk,nkhd->nqhd", rounded_probs, values, preferred_element_type=jnp.float32)
    mixed = mixed.reshape(batch_items * seq_rows, model_width).astype(jnp.bfloat16)
    middle = flat + jnp.dot(mixed, out_weight, preferred_element_type=jnp.float32) + out_bias
    normed_two, factor_two = normalize(middle)
    second = (normed_two * gains[1] + shifts[1]).astype(jnp.bfloat16)
    hidden_pre = jnp.dot(second, up_weight, preferred_element_type=jnp.float32) + up_bias
    hidden = jax.nn.gelu(hidden_pre, approximate=False).astype(jnp.bfloat16)
    result = middle + jnp.dot(hidden, down_weight, preferred_element_type=jnp.float32) + down_bias
    kept = (
        normed_one,
        factor_one,
        first,
        queries,
        keys,
        values,
        log_total,
        mixed,
        normed_two,
        factor_two,
        second,
        hidden_pre,
        hidden,
    )
    return (result.reshape(inputs.shape), kept)


def block_backward(upstream, params, kept, valid):
    gains, shifts, qkv_weight, out_weight, out_bias, up_weight, up_bias, down_weight, down_bias = (
        params[:9]
    )
    (
        normed_one,
        factor_one,
        first,
        queries,
        keys,
        values,
        log_total,
        mixed,
        normed_two,
        factor_two,
        second,
        hidden_pre,
        hidden,
    ) = kept
    batch_items, seq_rows, head_count, head_size = queries.shape
    model_width = head_count * head_size
    incoming = upstream.reshape(batch_items * seq_rows, model_width)
    rounded_out = incoming.astype(jnp.bfloat16)
    grad_down_weight = row_dot(hidden, rounded_out)
    grad_down_bias = jnp.sum(rounded_out.astype(jnp.float32), axis=0)
    grad_hidden = back_dot(rounded_out, down_weight)
    unused, gelu_back = jax.vjp(lambda before: jax.nn.gelu(before, approximate=False), hidden_pre)
    grad_pre = gelu_back(grad_hidden)[0].astype(jnp.bfloat16)
    grad_up_weight = row_dot(second, grad_pre)
    grad_up_bias = jnp.sum(grad_pre.astype(jnp.float32), axis=0)
    grad_second = back_dot(grad_pre, up_weight)
    gain_two = jnp.sum(grad_second * normed_two, axis=0)
    shift_two = jnp.sum(grad_second, axis=0)
    grad_middle = incoming + normalize_back(grad_second * gains[1], normed_two, factor_two)
    grad_branch = grad_middle.astype(jnp.bfloat16)
    grad_out_weight = row_dot(mixed, grad_branch)
    grad_out_bias = jnp.sum(grad_branch.astype(jnp.float32), axis=0)
    grad_mixed = back_dot(grad_branch, out_weight).astype(jnp.bfloat16)
    grad_mixed = grad_mixed.reshape(batch_items, seq_rows, head_count, head_size)
    scores = score_block(queries, keys, valid)
    probs = jnp.exp(scores - log_total)
    rounded_probs = probs.astype(jnp.bfloat16)
    grad_values = jnp.einsum(
        "nhqk,nqhd->nkhd", rounded_probs, grad_mixed, preferred_element_type=jnp.float32
    )
    grad_probs = jnp.einsum(
        "nqhd,nkhd->nhqk", grad_mixed, values, preferred_element_type=jnp.float32
    )
    grad_scores = probs * (grad_probs - jnp.sum(grad_probs * probs, axis=-1, keepdims=True))
    grad_scores = grad_scores.astype(jnp.bfloat16)
    grad_queries = jnp.einsum(
        "nhqk,nkhd->nqhd", grad_scores, keys, preferred_element_type=jnp.float32
    ) * HEAD_DIM ** (-0.5)
    grad_keys = jnp.einsum(
        "nhqk,nqhd->nkhd", grad_scores, queries, preferred_element_type=jnp.float32
    ) * HEAD_DIM ** (-0.5)
    grad_packed = jnp.stack([grad_queries, grad_keys, grad_values], axis=2)
    grad_packed = grad_packed.reshape(batch_items * seq_rows, 3 * model_width).astype(jnp.bfloat16)
    grad_qkv_weight = row_dot(first, grad_packed)
    grad_first = back_dot(grad_packed, qkv_weight)
    gain_one = jnp.sum(grad_first * normed_one, axis=0)
    shift_one = jnp.sum(grad_first, axis=0)
    grad_inputs = grad_middle + normalize_back(grad_first * gains[0], normed_one, factor_one)
    grads = (
        jnp.stack([gain_one, gain_two]),
        jnp.stack([shift_one, shift_two]),
        grad_qkv_weight,
        grad_out_weight,
        grad_out_bias,
        grad_up_weight,
        grad_up_bias,
        grad_down_weight,
        grad_down_bias,
    )
    return (grad_inputs.reshape(batch_items, seq_rows, model_width), grads)


def swap(values, axis, mask):
    size = lax.axis_size(axis)
    return lax.ppermute(values, axis, [(source, source ^ mask) for source in range(size)])


def masks(axis, skipped=0):
    size = lax.axis_size(axis)
    return [1 << bit for bit in range(skipped, size.bit_length() - 1)]


def gather_rows(shard):
    rows = shard.shape[0]
    me, place = lax.axis_index("narrow"), lax.axis_index("wide")
    sharing = [mask for mask in masks("wide")[:2]]
    count = 1 << len(sharing)
    quarter = place & (count - 1)
    length = rows // count
    held = lax.dynamic_slice_in_dim(shard, quarter * length, length)[None]
    for mask in masks("narrow"):
        held = jnp.concatenate([held, swap(held, "narrow", mask)])
    pieces = {0: held[1:]}
    for mask in reversed(sharing):
        pieces.update({key ^ mask: swap(piece, "wide", mask) for key, piece in pieces.items()})
    full = jnp.zeros((lax.axis_size("narrow") * rows,) + shard.shape[1:], shard.dtype)
    full = lax.dynamic_update_slice_in_dim(full, shard, me * rows, 0)
    for key, piece in pieces.items():
        for offset in range(1, lax.axis_size("narrow")):
            start = (me ^ offset) * rows + (quarter ^ key) * length
            full = lax.dynamic_update_slice_in_dim(full, piece[offset - 1], start, 0)
    return full


def halve(values, axis, mask):
    bit = (lax.axis_index(axis) & mask) // mask
    sent = lax.dynamic_index_in_dim(values, 1 - bit, 0, keepdims=False)
    kept = lax.dynamic_index_in_dim(values, bit, 0, keepdims=False)
    return kept + swap(sent, axis, mask)


def double(values, axis, mask):
    bit = (lax.axis_index(axis) & mask) // mask
    got = swap(values, axis, mask)
    both = jnp.stack([values, values])
    return lax.dynamic_update_index_in_dim(both, got, 1 - bit, 0)


def reduce_rows(term):
    rows, columns = term.shape
    narrow_size, wide_size = lax.axis_size("narrow"), lax.axis_size("wide")
    order = [("wide", mask) for mask in masks("wide")[:1]]
    order += [("narrow", mask) for mask in reversed(masks("narrow"))]
    order += [("wide", mask) for mask in masks("wide")[1:]]
    length = rows // (narrow_size * wide_size)
    values = term.reshape(narrow_size, 2, wide_size // 2, length, columns)
    values = values.swapaxes(0, 1)
    for axis, mask in order:
        values = values.reshape((2, -1, length, columns))
        values = halve(values, axis, mask)
    for axis, mask in reversed(order):
        if axis == "wide":
            values = double(values, axis, mask).reshape(-1, length, columns)
    return values.reshape(rows // narrow_size, columns)


def sum_all(values):
    for axis in ("wide", "narrow"):
        for mask in masks(axis):
            values = values + swap(values, axis, mask)
    return values


def on_device(
    tokens,
    skip,
    flags,
    cotangent,
    norm_gains,
    norm_biases,
    qkv_weight,
    out_weight,
    out_bias,
    up_weight,
    up_bias,
    down_weight,
    down_bias,
    skip_weight,
    skip_bias,
):
    batch_items, seq_rows, model_width = tokens.shape
    lengths = PATCHES + 1 + CAPTION * flags
    valid = lax.broadcasted_iota(jnp.int32, (batch_items, seq_rows), 1) < lengths[:, None]
    small = (norm_gains, norm_biases, out_bias, up_bias, down_bias, skip_bias)
    packed_small = jnp.concatenate([piece.reshape(-1) for piece in small])
    held = packed_small[None]
    for mask in masks("narrow"):
        held = jnp.concatenate([held, swap(held, "narrow", mask)])
    me = lax.axis_index("narrow")
    every = [lax.dynamic_index_in_dim(held, me ^ place, 0, keepdims=False) for place in range(lax.axis_size("narrow"))]
    whole, start = [], 0
    for piece in small:
        stop = start + piece.size
        whole.append(jnp.concatenate([part[start:stop].reshape(piece.shape) for part in every], axis=-1))
        start = stop
    gains, shifts, out_biases, up_biases, down_biases, skip_shift = whole

    def layer_params(layer):
        return (
            gains[layer],
            shifts[layer],
            gather_rows(qkv_weight[layer]),
            gather_rows(out_weight[layer]),
            out_biases[layer],
            gather_rows(up_weight[layer]),
            up_biases[layer],
            gather_rows(down_weight[layer]),
            down_biases[layer],
        )

    first_params = layer_params(0)
    inputs = tokens.astype(jnp.float32)
    middle, first_kept = block_forward(inputs, first_params, valid)
    join_weight = gather_rows(skip_weight)
    second_params = layer_params(1)
    joined = jnp.concatenate([middle.astype(jnp.bfloat16), skip], axis=-1)
    joined = joined.reshape(batch_items * seq_rows, 2 * model_width)
    entry = jnp.dot(joined, join_weight, preferred_element_type=jnp.float32) + skip_shift
    entry = entry.reshape(batch_items, seq_rows, model_width)
    final, second_kept = block_forward(entry, second_params, valid)
    row_valid = valid[:, :, None]
    output = jnp.where(row_valid, final, 0.0).astype(jnp.bfloat16)
    grad_final = jnp.where(row_valid, cotangent.astype(jnp.float32), 0.0)
    grad_entry, second_terms = block_backward(grad_final, second_params, second_kept, valid)
    rounded_entry = grad_entry.reshape(batch_items * seq_rows, model_width).astype(jnp.bfloat16)
    grad_skip_weight = row_dot(joined, rounded_entry)
    grad_skip_bias = jnp.sum(rounded_entry.astype(jnp.float32), axis=0)
    grad_joined = back_dot(rounded_entry, join_weight).reshape(
        batch_items, seq_rows, 2 * model_width
    )
    grad_middle = grad_joined[:, :, :model_width]
    skip_grad = grad_joined[:, :, model_width:]
    tokens_grad, first_terms = block_backward(grad_middle, first_params, first_kept, valid)
    inverse = 1.0 / lax.axis_size("wide")

    def summed(term):
        return reduce_rows(term.astype(jnp.bfloat16)).astype(jnp.float32) * inverse

    second_sums = [summed(second_terms[place]) for place in (7, 5, 3, 2)]
    join_sum = summed(grad_skip_weight)
    first_sums = [summed(first_terms[place]) for place in (7, 5, 3, 2)]
    large = [jnp.stack([lower, upper]) for lower, upper in zip(first_sums, second_sums)]
    shares = lax.axis_size("narrow")
    minor = [jnp.stack([first_terms[place], second_terms[place]]) for place in (0, 1, 4, 6, 8)]
    minor.append(grad_skip_bias)
    split = [jnp.moveaxis(piece.reshape(piece.shape[:-1] + (shares, -1)), -2, 0) for piece in minor]
    packed_minor = jnp.concatenate([piece.reshape(shares, -1) for piece in split], axis=1)
    owned = lax.dynamic_index_in_dim(sum_all(packed_minor), me, 0, keepdims=False) * inverse
    results, start = [], 0
    for piece in split:
        stop = start + piece.size // shares
        results.append(owned[start:stop].reshape(piece.shape[1:]))
        start = stop
    return (
        output,
        tokens_grad,
        skip_grad,
        results[0],
        results[1],
        large[3],
        large[2],
        results[2],
        large[1],
        results[3],
        large[0],
        results[4],
        join_sum,
        results[5],
    )


def solution(mesh):
    placed = (
        P(("wide", "narrow"), None, None),
        P(("wide", "narrow"), None, None),
        P(("wide", "narrow")),
        P(("wide", "narrow"), None, None),
        P(None, None, "narrow"),
        P(None, None, "narrow"),
        P(None, "narrow", None),
        P(None, "narrow", None),
        P(None, "narrow"),
        P(None, "narrow", None),
        P(None, "narrow"),
        P(None, "narrow", None),
        P(None, "narrow"),
        P("narrow", None),
        P("narrow"),
    )
    return jax.shard_map(
        on_device,
        mesh=mesh,
        in_specs=placed,
        out_specs=(
            P(("wide", "narrow"), None, None),
            P(("wide", "narrow"), None, None),
            P(("wide", "narrow"), None, None),
            P(None, None, "narrow"),
            P(None, None, "narrow"),
            P(None, "narrow", None),
            P(None, "narrow", None),
            P(None, "narrow"),
            P(None, "narrow", None),
            P(None, "narrow"),
            P(None, "narrow", None),
            P(None, "narrow"),
            P("narrow", None),
            P("narrow"),
        ),
        check_vma=False,
    )
```

time: 1350 us -> 1090 us (0.81)
  waiting for transfers between devices: 742 us -> 348 us
  starting transfers between devices: 1.52 us -> 157 us
  local copies, waits for them, and re-layouts: 145 us -> 250 us
  blocking collectives: 104 us -> 0 us
  matrix products: 265 us -> 237 us
    ppermute x0 -> x123, waiting for transfers between devices: none -> 348 us  [swap(): lax.ppermute(values, axis, [(source, source ^ mask) for source in range(s...]
    reduce_scatter x9 -> x0, waiting for transfers between devices: 284 us -> none  [the longest x1 62.9 us: on_device(): lax.psum_scatter(second_terms[5].astype(jnp.bfloat16), 'narrow', scatter_...]
    psum x1 -> x0, waiting for transfers between devices: 223 us -> none  [on_device(): lax.psum(second_shards[2].astype(jnp.bfloat16), 'wide').astype(jnp.float32)]
    all_gather x9 -> x0, waiting for transfers between devices: 207 us -> none  [the longest x1 46.1 us: on_device(): lax.all_gather(qkv_weight[1], 'narrow', axis=0, tiled=True)]
    ppermute x0 -> x123, starting transfers between devices: none -> 157 us  [swap(): lax.ppermute(values, axis, [(source, source ^ mask) for source in range(s...]
    psum x1 -> x0, blocking collectives: 60 us -> none  [on_device(): lax.psum(second_shards[0].astype(jnp.bfloat16), 'wide').astype(jnp.float32)]
    dynamic_update_slice x0 -> x80, local copies, waits for them, and re-layouts: none -> 51.5 us  [the longest x35 38.6 us: gather_rows(): full = lax.dynamic_update_slice_in_dim(full, piece[offset - 1], start, 0)]
    all_gather x11 -> x0, blocking collectives: 39 us -> none  [the longest x1 4.29 us: on_device(): lax.all_gather(norm_gains[0], 'narrow', axis=1, tiled=True)]
  transfers between devices with their start and end apart: 23 -> 123, of which waited for: 14 -> 65; matrix products, arithmetic and copies ran while one was open for 27% -> 30% of each run, Pallas kernels for 0% -> 0%
where the time goes in v1:
time: 1090 us; the launch traced here: 1080 us
  waiting for transfers between devices  348 us (32%)
  local copies, waits for them, and re-layouts  250 us (23%)
  matrix products  237 us (22%)
  starting transfers between devices  157 us (14%)
  other arithmetic  84.4 us (8%)
    ppermute x123, waiting for transfers between devices, swap(): lax.ppermute(values, axis, [(source, source ^ mask) for source in range(s...  348 us
    ppermute x123, starting transfers between devices, swap(): lax.ppermute(values, axis, [(source, source ^ mask) for source in range(s...  157 us
    dot_general x9, matrix products, back_dot(): lax.dot_general(left, weight, (((1,), (1,)), ((), ())), preferred_element...  75.6 us
    unnamed x352, local copies, waits for them, and re-layouts  44.1 us
    dot_general x9, matrix products, row_dot(): lax.dot_general(left, right, (((0,), (0,)), ((), ())), preferred_element_...  39.3 us
    dynamic_update_slice x35, local copies, waits for them, and re-layouts, gather_rows(): full = lax.dynamic_update_slice_in_dim(full, piece[offset - 1], start, 0)  38.6 us
    dot_general x2, matrix products, block_forward(): jnp.dot(second, up_weight, preferred_element_type=jnp.float32) + up_bias  30.3 us
  transfers between devices with their start and end apart: 123, of which 65 were waited for; matrix products, arithmetic and copies ran while one was open for 30% of the time, Pallas kernels for 0%

profile of v1, /device:TPU:1, one launch (start us, length us, event | category | flops | bytes accessed | tf_op | source)
XLA Modules:
  0.0 1080.2 jit_solution(8671888395152347542)
XLA Ops:
  116.6 6.8 collective-permute-done.13
  128.2 7.8 collective-permute-done.33
  143.3 9.4 collective-permute-done.10
  182.2 8.4 collective-permute-done.34
  203.3 10.3 reshape.1021
  250.8 24.7 %multiply_convert_fusion.3 = (bf16[672,3072]{1,0:T(8,128)(2,1)S(1)}, f32[672,3072]{1,0:T(8,128)}, f32[672,3072]{1,0:T(8,128)}) fusion(f32[3072]{0:T(1024)S(1)} %bitcast.820, bf16[768,3072]{1,0:T(8,128)(2,1)} %bitcast_dynamic-update-slice_fusion.30, f32[768]{0:T(1024)S(1)} %copy-done.124, f32[768]{0:T(1024)S(1)} %copy-done.101, ...), kind=kOutput, calls=%fused_computation.35 | convolution fusion | flops 3310239744 | bytes 27453696 | tf_op jit(solution)/shard_map/dot_general | solution.py:71
  294.4 6.9 reshape.1022
  349.4 25.8 %convert_reduce_fusion = (f32[3072]{0:T(1024)}, bf16[672,3072]{1,0:T(8,128)(2,1)S(1)}, f32[672,3072]{1,0:T(8,128)}) fusion(f32[672,3072]{1,0:T(8,128)S(1)} %fusion.81, f32[3072]{0:T(1024)S(1)} %bitcast.816, bf16[672,768]{1,0:T(8,128)(2,1)S(1)} %copy-done.68, bf16[3072,768]{1,0:T(8,128)(2,1)} %bitcast_dynamic-update-slice_fusion.17), kind=kOutput, calls=%fused_computation.18 | convolution fusion | flops 3325719552 | bytes 26419200 | tf_op jit(solution)/shard_map/dot_general | solution.py:22
  375.3 6.8 multiply_reduce_fusion.2
  382.1 6.2 convolution_convert_fusion.4
  402.6 8.1 fusion.25
  410.7 10.0 multiply_reduce_fusion.1
  420.8 7.1 multiply_convert_fusion.1
  440.2 8.2 multiply_reduce_fusion.3
  470.6 10.4 convert_reduce_fusion.1
  481.1 7.0 multiply_reduce_fusion.4
  488.1 6.4 convolution_convert_fusion.5
  506.3 9.1 convolution_bitcast_fusion
  515.4 10.1 multiply_reduce_fusion
  525.5 7.3 multiply_convert_fusion
  538.7 7.9 multiply_convert_fusion.2
  587.6 8.6 convert_element_type.422
  596.3 7.9 fusion.82
  651.1 6.6 collective-permute-done.70
  658.0 6.8 collective-permute-done.61
  695.2 12.1 %collective-permute-start.42 = (bf16[16,24,2304]{2,1,0:T(8,128)(2,1)S(1)}, bf16[16,24,2304]{2,1,0:T(8,128)(2,1)S(1)}, u32[]{:S(2)}, u32[]{:S(2)}) collective-permute-start(bf16[16,24,2304]{2,1,0:T(8,128)(2,1)S(1)} %copy-done.58), channel_id=1, source_target_pairs={{0,2},{2,0},{4,6},{6,4},{8,10},{10,8},{12,14},{14,12},{16,18},{18,... | collective-permute-start | bytes 5308424 | tf_op jit(solution)/shard_map/ppermute | solution.py:171
  731.3 12.8 %collective-permute-done.115 = bf16[8,48,768]{2,1,0:T(8,128)(2,1)S(1)} collective-permute-done((bf16[8,48,768]{2,1,0:T(8,128)(2,1)S(1)}, bf16[8,48,768]{2,1,0:T(8,128)(2,1)S(1)}, u32[]{:S(2)}, u32[]{:S(2)}) %collective-permute-start.115) | collective-permute-done | bytes 589856 | tf_op jit(solution)/shard_map/ppermute | solution.py:171
  747.6 6.3 collective-permute-done.116
  776.5 7.3 collective-permute-done.52
  784.3 18.5 %collective-permute-done.43 = bf16[8,24,2304]{2,1,0:T(8,128)(2,1)S(1)} collective-permute-done((bf16[8,24,2304]{2,1,0:T(8,128)(2,1)S(1)}, bf16[8,24,2304]{2,1,0:T(8,128)(2,1)S(1)}, u32[]{:S(2)}, u32[]{:S(2)}) %collective-permute-start.43) | collective-permute-done | bytes 884768 | tf_op jit(solution)/shard_map/ppermute | solution.py:171
  810.7 7.5 collective-permute-done.44
  828.3 14.7 %collective-permute-start.122 = (bf16[8,48,768]{2,1,0:T(8,128)(2,1)S(1)}, bf16[8,48,768]{2,1,0:T(8,128)(2,1)S(1)}, u32[]{:S(2)}, u32[]{:S(2)}) collective-permute-start(bf16[8,48,768]{2,1,0:T(8,128)(2,1)S(1)} %bitcast.731), channel_id=1, source_target_pairs={{0,2},{2,0},{4,6},{6,4},{8,10},{10,8},{12,14},{14,12},{16,18},{18,... | collective-permute-start | bytes 1769480 | tf_op jit(solution)/shard_map/ppermute | solution.py:171
  852.5 7.6 collective-permute-done.46
  860.1 7.3 collective-permute-done.56
  867.5 7.7 collective-permute-done.47
  879.2 24.8 %collective-permute-done.79 = bf16[8,24,3072]{2,1,0:T(8,128)(2,1)S(1)} collective-permute-done((bf16[8,24,3072]{2,1,0:T(8,128)(2,1)S(1)}, bf16[8,24,3072]{2,1,0:T(8,128)(2,1)S(1)}, u32[]{:S(2)}, u32[]{:S(2)}) %collective-permute-start.79) | collective-permute-done | bytes 1179680 | tf_op jit(solution)/shard_map/ppermute | solution.py:171
  912.8 12.8 %collective-permute-done.80 = bf16[4,24,3072]{2,1,0:T(8,128)(2,1)S(1)} collective-permute-done((bf16[4,24,3072]{2,1,0:T(8,128)(2,1)S(1)}, bf16[4,24,3072]{2,1,0:T(8,128)(2,1)S(1)}, u32[]{:S(2)}, u32[]{:S(2)}) %collective-permute-start.80) | collective-permute-done | bytes 589856 | tf_op jit(solution)/shard_map/ppermute | solution.py:171
  925.7 9.4 collective-permute-done.58
  935.3 9.3 collective-permute-done.49
  944.6 6.7 collective-permute-start.59
  954.7 15.5 %collective-permute-done.91 = bf16[1,24,3072]{2,1,0:T(8,128)(2,1)S(1)} collective-permute-done((bf16[1,24,3072]{2,1,0:T(8,128)(2,1)S(1)}, bf16[1,24,3072]{2,1,0:T(8,128)(2,1)S(1)}, u32[]{:S(2)}, u32[]{:S(2)}) %collective-permute-start.91) | collective-permute-done | bytes 147488 | tf_op jit(solution)/shard_map/ppermute | solution.py:171
  973.4 9.5 collective-permute-done.82
  983.0 9.4 collective-permute-done.110
  992.4 8.7 collective-permute-start.111
  1038.9 6.4 collective-permute-start.95
  1045.4 6.1 collective-permute-done.103
  1051.6 6.4 collective-permute-start.104
  1058.0 6.2 collective-permute-done.85
  (984 shorter events, 608.3 us)
Async XLA Ops:
  6.8 64.0 %collective-permute-start = (bf16[1,8064]{1,0:T(2,128)(2,1)}, bf16[1,8064]{1,0:T(2,128)(2,1)}, u32[]{:S(2)}, u32[]{:S(2)}) collective-permute-start(bf16[1,8064]{1,0:T(2,128)(2,1)} %broadcast_in_dim.233), channel_id=1, source_target_pairs={{0,1},{1,0},{2,3},{3,2},{4,5},{5,4},{6,7},{7,6},{8,9},{9,8},{10,11... | collective-permute-start | bytes 48392 | tf_op jit(solution)/shard_map/ppermute | solution.py:171
  10.6 86.3 %collective-permute-start.17 = (bf16[1,192,768]{2,1,0:T(8,128)(2,1)}, bf16[1,192,768]{2,1,0:T(8,128)(2,1)}, u32[]{:S(2)}, u32[]{:S(2)}) collective-permute-start(bf16[1,192,768]{2,1,0:T(8,128)(2,1)} %dynamic-slice_bitcast_fusion.29), channel_id=1, source_target_pairs={{0,1},{1,0},{2,3},{3,2},{4,5},{5,4},{6,7},{7,6},{8,9},{9,8},{10,11... | collective-permute-start | bytes 884744 | tf_op jit(solution)/shard_map/ppermute | solution.py:171
  12.6 64.7 %collective-permute-start.5 = (bf16[1,96,768]{2,1,0:T(8,128)(2,1)}, bf16[1,96,768]{2,1,0:T(8,128)(2,1)}, u32[]{:S(2)}, u32[]{:S(2)}) collective-permute-start(bf16[1,96,768]{2,1,0:T(8,128)(2,1)} %constant_dynamic-slice_fusion.21), channel_id=1, source_target_pairs={{0,1},{1,0},{2,3},{3,2},{4,5},{5,4},{6,7},{7,6},{8,9},{9,8},{10,11... | collective-permute-start | bytes 442376 | tf_op jit(solution)/shard_map/ppermute | solution.py:171
  14.7 65.4 %collective-permute-start.25 = (bf16[1,96,768]{2,1,0:T(8,128)(2,1)}, bf16[1,96,768]{2,1,0:T(8,128)(2,1)S(1)}, u32[]{:S(2)}, u32[]{:S(2)}) collective-permute-start(bf16[1,96,768]{2,1,0:T(8,128)(2,1)} %constant_dynamic-slice_fusion.17), channel_id=1, source_target_pairs={{0,1},{1,0},{2,3},{3,2},{4,5},{5,4},{6,7},{7,6},{8,9},{9,8},{10,11... | collective-permute-start | bytes 442376 | tf_op jit(solution)/shard_map/ppermute | solution.py:171
  19.1 80.9 %collective-permute-start.1 = (bf16[1,96,2304]{2,1,0:T(8,128)(2,1)}, bf16[1,96,2304]{2,1,0:T(8,128)(2,1)}, u32[]{:S(2)}, u32[]{:S(2)}) collective-permute-start(bf16[1,96,2304]{2,1,0:T(8,128)(2,1)} %constant_dynamic-slice_fusion.22), channel_id=1, source_target_pairs={{0,1},{1,0},{2,3},{3,2},{4,5},{5,4},{6,7},{7,6},{8,9},{9,8},{10,11... | collective-permute-start | bytes 1327112 | tf_op jit(solution)/shard_map/ppermute | solution.py:171
  70.9 33.2 %collective-permute-start.21 = (bf16[1,96,2304]{2,1,0:T(8,128)(2,1)}, bf16[1,96,2304]{2,1,0:T(8,128)(2,1)S(1)}, u32[]{:S(2)}, u32[]{:S(2)}) collective-permute-start(bf16[1,96,2304]{2,1,0:T(8,128)(2,1)} %constant_dynamic-slice_fusion.18), channel_id=1, source_target_pairs={{0,1},{1,0},{2,3},{3,2},{4,5},{5,4},{6,7},{7,6},{8,9},{9,8},{10,11... | collective-permute-start | bytes 1327112 | tf_op jit(solution)/shard_map/ppermute | solution.py:171
  77.3 28.0 %collective-permute-start.9 = (bf16[1,96,3072]{2,1,0:T(8,128)(2,1)}, bf16[1,96,3072]{2,1,0:T(8,128)(2,1)S(1)}, u32[]{:S(2)}, u32[]{:S(2)}) collective-permute-start(bf16[1,96,3072]{2,1,0:T(8,128)(2,1)} %constant_dynamic-slice_fusion.20), channel_id=1, source_target_pairs={{0,1},{1,0},{2,3},{3,2},{4,5},{5,4},{6,7},{7,6},{8,9},{9,8},{10,11... | collective-permute-start | bytes 1769480 | tf_op jit(solution)/shard_map/ppermute | solution.py:171
  96.9 26.5 %collective-permute-start.13 = (bf16[1,384,768]{2,1,0:T(8,128)(2,1)S(1)}, bf16[1,384,768]{2,1,0:T(8,128)(2,1)S(1)}, u32[]{:S(2)}, u32[]{:S(2)}) collective-permute-start(bf16[1,384,768]{2,1,0:T(8,128)(2,1)S(1)} %copy-done.74), channel_id=1, source_target_pairs={{0,1},{1,0},{2,3},{3,2},{4,5},{5,4},{6,7},{7,6},{8,9},{9,8},{10,11... | collective-permute-start | bytes 1769480 | tf_op jit(solution)/shard_map/ppermute | solution.py:171
  103.4 32.6 %collective-permute-start.33 = (bf16[1,384,768]{2,1,0:T(8,128)(2,1)S(1)}, bf16[1,384,768]{2,1,0:T(8,128)(2,1)S(1)}, u32[]{:S(2)}, u32[]{:S(2)}) collective-permute-start(bf16[1,384,768]{2,1,0:T(8,128)(2,1)S(1)} %copy-done.72), channel_id=1, source_target_pairs={{0,1},{1,0},{2,3},{3,2},{4,5},{5,4},{6,7},{7,6},{8,9},{9,8},{10,11... | collective-permute-start | bytes 1769480 | tf_op jit(solution)/shard_map/ppermute | solution.py:171
  110.7 27.4 %collective-permute-start.3 = (bf16[1,96,2304]{2,1,0:T(8,128)(2,1)}, bf16[1,96,2304]{2,1,0:T(8,128)(2,1)S(1)}, u32[]{:S(2)}, u32[]{:S(2)}) collective-permute-start(bf16[1,96,2304]{2,1,0:T(8,128)(2,1)} %collective-permute-done.1), channel_id=1, source_target_pairs={{0,2},{2,0},{4,6},{6,4},{8,10},{10,8},{12,14},{14,12},{16,18},{18,... | collective-permute-start | bytes 1327112 | tf_op jit(solution)/shard_map/ppermute | solution.py:171
  139.5 29.0 %collective-permute-start.31 = (bf16[1,96,3072]{2,1,0:T(8,128)(2,1)S(1)}, bf16[1,96,3072]{2,1,0:T(8,128)(2,1)S(1)}, u32[]{:S(2)}, u32[]{:S(2)}) collective-permute-start(bf16[1,96,3072]{2,1,0:T(8,128)(2,1)S(1)} %collective-permute-done.29), channel_id=1, source_target_pairs={{0,2},{2,0},{4,6},{6,4},{8,10},{10,8},{12,14},{14,12},{16,18},{18,... | collective-permute-start | bytes 1769480 | tf_op jit(solution)/shard_map/ppermute | solution.py:171
  142.1 51.7 %collective-permute-start.15 = (bf16[1,384,768]{2,1,0:T(8,128)(2,1)S(1)}, bf16[1,384,768]{2,1,0:T(8,128)(2,1)S(1)}, u32[]{:S(2)}, u32[]{:S(2)}) collective-permute-start(bf16[1,384,768]{2,1,0:T(8,128)(2,1)S(1)} %collective-permute-done.13), channel_id=1, source_target_pairs={{0,2},{2,0},{4,6},{6,4},{8,10},{10,8},{12,14},{14,12},{16,18},{18,... | collective-permute-start | bytes 1769480 | tf_op jit(solution)/shard_map/ppermute | solution.py:171
  152.7 25.3 %collective-permute-start.14 = (bf16[1,384,768]{2,1,0:T(8,128)(2,1)S(1)}, bf16[1,384,768]{2,1,0:T(8,128)(2,1)}, u32[]{:S(2)}, u32[]{:S(2)}) collective-permute-start(bf16[1,384,768]{2,1,0:T(8,128)(2,1)S(1)} %collective-permute-done.13), channel_id=1, source_target_pairs={{0,4},{2,6},{4,0},{6,2},{8,12},{10,14},{12,8},{14,10},{16,20},{18,... | collective-permute-start | bytes 1769480 | tf_op jit(solution)/shard_map/ppermute | solution.py:171
  155.8 38.9 %collective-permute-start.35 = (bf16[1,384,768]{2,1,0:T(8,128)(2,1)S(1)}, bf16[1,384,768]{2,1,0:T(8,128)(2,1)S(1)}, u32[]{:S(2)}, u32[]{:S(2)}) collective-permute-start(bf16[1,384,768]{2,1,0:T(8,128)(2,1)S(1)} %collective-permute-done.33), channel_id=1, source_target_pairs={{0,2},{2,0},{4,6},{6,4},{8,10},{10,8},{12,14},{14,12},{16,18},{18,... | collective-permute-start | bytes 1769480 | tf_op jit(solution)/shard_map/ppermute | solution.py:171
  165.3 25.3 %collective-permute-start.34 = (bf16[1,384,768]{2,1,0:T(8,128)(2,1)S(1)}, bf16[1,384,768]{2,1,0:T(8,128)(2,1)}, u32[]{:S(2)}, u32[]{:S(2)}) collective-permute-start(bf16[1,384,768]{2,1,0:T(8,128)(2,1)S(1)} %collective-permute-done.33), channel_id=1, source_target_pairs={{0,4},{2,6},{4,0},{6,2},{8,12},{10,14},{12,8},{14,10},{16,20},{18,... | collective-permute-start | bytes 1769480 | tf_op jit(solution)/shard_map/ppermute | solution.py:171
  168.5 27.6 %collective-permute-start.4 = (bf16[1,96,2304]{2,1,0:T(8,128)(2,1)S(1)}, bf16[1,96,2304]{2,1,0:T(8,128)(2,1)S(1)}, u32[]{:S(2)}, u32[]{:S(2)}) collective-permute-start(bf16[1,96,2304]{2,1,0:T(8,128)(2,1)S(1)} %collective-permute-done.2), channel_id=1, source_target_pairs={{0,2},{2,0},{4,6},{6,4},{8,10},{10,8},{12,14},{14,12},{16,18},{18,... | collective-permute-start | bytes 1327112 | tf_op jit(solution)/shard_map/ppermute | solution.py:171
  190.6 58.3 %collective-permute-start.12 = (bf16[1,96,3072]{2,1,0:T(8,128)(2,1)}, bf16[1,96,3072]{2,1,0:T(8,128)(2,1)}, u32[]{:S(2)}, u32[]{:S(2)}) collective-permute-start(bf16[1,96,3072]{2,1,0:T(8,128)(2,1)} %collective-permute-done.10), channel_id=1, source_target_pairs={{0,2},{2,0},{4,6},{6,4},{8,10},{10,8},{12,14},{14,12},{16,18},{18,... | collective-permute-start | bytes 1769480 | tf_op jit(solution)/shard_map/ppermute | solution.py:171
  193.9 144.8 %collective-permute-start.32 = (bf16[1,96,3072]{2,1,0:T(8,128)(2,1)}, bf16[1,96,3072]{2,1,0:T(8,128)(2,1)}, u32[]{:S(2)}, u32[]{:S(2)}) collective-permute-start(bf16[1,96,3072]{2,1,0:T(8,128)(2,1)} %collective-permute-done.30), channel_id=1, source_target_pairs={{0,2},{2,0},{4,6},{6,4},{8,10},{10,8},{12,14},{14,12},{16,18},{18,... | collective-permute-start | bytes 1769480 | tf_op jit(solution)/shard_map/ppermute | solution.py:171
  194.8 80.8 %collective-permute-start.16 = (bf16[1,384,768]{2,1,0:T(8,128)(2,1)}, bf16[1,384,768]{2,1,0:T(8,128)(2,1)}, u32[]{:S(2)}, u32[]{:S(2)}) collective-permute-start(bf16[1,384,768]{2,1,0:T(8,128)(2,1)} %collective-permute-done.14), channel_id=1, source_target_pairs={{0,2},{2,0},{4,6},{6,4},{8,10},{10,8},{12,14},{14,12},{16,18},{18,... | collective-permute-start | bytes 1769480 | tf_op jit(solution)/shard_map/ppermute | solution.py:171
  196.1 150.4 %collective-permute-start.36 = (bf16[1,384,768]{2,1,0:T(8,128)(2,1)}, bf16[1,384,768]{2,1,0:T(8,128)(2,1)}, u32[]{:S(2)}, u32[]{:S(2)}) collective-permute-start(bf16[1,384,768]{2,1,0:T(8,128)(2,1)} %collective-permute-done.34), channel_id=1, source_target_pairs={{0,2},{2,0},{4,6},{6,4},{8,10},{10,8},{12,14},{14,12},{16,18},{18,... | collective-permute-start | bytes 1769480 | tf_op jit(solution)/shard_map/ppermute | solution.py:171
  566.2 82.2 %collective-permute-start.69 = (bf16[16,24,768]{2,1,0:T(8,128)(2,1)}, bf16[16,24,768]{2,1,0:T(8,128)(2,1)}, u32[]{:S(2)}, u32[]{:S(2)}) collective-permute-start(bf16[16,24,768]{2,1,0:T(8,128)(2,1)} %dynamic-slice_bitcast_fusion.18), channel_id=1, source_target_pairs={{0,2},{2,0},{4,6},{6,4},{8,10},{10,8},{12,14},{14,12},{16,18},{18,... | collective-permute-start | bytes 1769480 | tf_op jit(solution)/shard_map/ppermute | solution.py:171
  570.0 197.8 %collective-permute-start.105 = (bf16[16,96,768]{2,1,0:T(8,128)(2,1)}, bf16[16,96,768]{2,1,0:T(8,128)(2,1)}, u32[]{:S(2)}, u32[]{:S(2)}) collective-permute-start(bf16[16,96,768]{2,1,0:T(8,128)(2,1)} %dynamic-slice_bitcast_fusion), channel_id=1, source_target_pairs={{0,2},{2,0},{4,6},{6,4},{8,10},{10,8},{12,14},{14,12},{16,18},{18,... | collective-permute-start | bytes 7077896 | tf_op jit(solution)/shard_map/ppermute | solution.py:171
  570.5 200.7 %collective-permute-start.87 = (bf16[16,24,3072]{2,1,0:T(8,128)(2,1)}, bf16[16,24,3072]{2,1,0:T(8,128)(2,1)}, u32[]{:S(2)}, u32[]{:S(2)}) collective-permute-start(bf16[16,24,3072]{2,1,0:T(8,128)(2,1)} %dynamic-slice_bitcast_fusion.2), channel_id=1, source_target_pairs={{0,2},{2,0},{4,6},{6,4},{8,10},{10,8},{12,14},{14,12},{16,18},{18,... | collective-permute-start | bytes 7077896 | tf_op jit(solution)/shard_map/ppermute | solution.py:171
  637.1 70.2 %collective-permute-start.114 = (bf16[16,48,768]{2,1,0:T(8,128)(2,1)}, bf16[16,48,768]{2,1,0:T(8,128)(2,1)}, u32[]{:S(2)}, u32[]{:S(2)}) collective-permute-start(bf16[16,48,768]{2,1,0:T(8,128)(2,1)} %dynamic-slice_bitcast_fusion.6), channel_id=1, source_target_pairs={{0,2},{2,0},{4,6},{6,4},{8,10},{10,8},{12,14},{14,12},{16,18},{18,... | collective-permute-start | bytes 3538952 | tf_op jit(solution)/shard_map/ppermute | solution.py:171
  648.4 97.0 %collective-permute-start.51 = (bf16[16,24,2304]{2,1,0:T(8,128)(2,1)}, bf16[16,24,2304]{2,1,0:T(8,128)(2,1)S(1)}, u32[]{:S(2)}, u32[]{:S(2)}) collective-permute-start(bf16[16,24,2304]{2,1,0:T(8,128)(2,1)} %dynamic-slice_bitcast_fusion.4), channel_id=1, source_target_pairs={{0,2},{2,0},{4,6},{6,4},{8,10},{10,8},{12,14},{14,12},{16,18},{18,... | collective-permute-start | bytes 5308424 | tf_op jit(solution)/shard_map/ppermute | solution.py:171
  695.2 50.5 %collective-permute-start.42 = (bf16[16,24,2304]{2,1,0:T(8,128)(2,1)S(1)}, bf16[16,24,2304]{2,1,0:T(8,128)(2,1)S(1)}, u32[]{:S(2)}, u32[]{:S(2)}) collective-permute-start(bf16[16,24,2304]{2,1,0:T(8,128)(2,1)S(1)} %copy-done.58), channel_id=1, source_target_pairs={{0,2},{2,0},{4,6},{6,4},{8,10},{10,8},{12,14},{14,12},{16,18},{18,... | collective-permute-start | bytes 5308424 | tf_op jit(solution)/shard_map/ppermute | solution.py:171
  744.1 30.4 %collective-permute-start.96 = (bf16[16,96,768]{2,1,0:T(8,128)(2,1)S(1)}, bf16[16,96,768]{2,1,0:T(8,128)(2,1)S(1)}, u32[]{:S(2)}, u32[]{:S(2)}) collective-permute-start(bf16[16,96,768]{2,1,0:T(8,128)(2,1)S(1)} %copy-done.51), channel_id=1, source_target_pairs={{0,2},{2,0},{4,6},{6,4},{8,10},{10,8},{12,14},{14,12},{16,18},{18,... | collective-permute-start | bytes 7077896 | tf_op jit(solution)/shard_map/ppermute | solution.py:171
  745.4 28.1 %collective-permute-start.78 = (bf16[16,24,3072]{2,1,0:T(8,128)(2,1)S(1)}, bf16[16,24,3072]{2,1,0:T(8,128)(2,1)S(1)}, u32[]{:S(2)}, u32[]{:S(2)}) collective-permute-start(bf16[16,24,3072]{2,1,0:T(8,128)(2,1)S(1)} %copy-done.50), channel_id=1, source_target_pairs={{0,2},{2,0},{4,6},{6,4},{8,10},{10,8},{12,14},{14,12},{16,18},{18,... | collective-permute-start | bytes 7077896 | tf_op jit(solution)/shard_map/ppermute | solution.py:171
  767.8 35.1 %collective-permute-start.43 = (bf16[8,24,2304]{2,1,0:T(8,128)(2,1)S(1)}, bf16[8,24,2304]{2,1,0:T(8,128)(2,1)S(1)}, u32[]{:S(2)}, u32[]{:S(2)}) collective-permute-start(bf16[8,24,2304]{2,1,0:T(8,128)(2,1)S(1)} %dynamic-slice_bitcast_fusion.12), channel_id=1, source_target_pairs={{0,1},{1,0},{2,3},{3,2},{4,5},{5,4},{6,7},{7,6},{8,9},{9,8},{10,11... | collective-permute-start | bytes 2654216 | tf_op jit(solution)/shard_map/ppermute | solution.py:171
  773.6 101.9 %collective-permute-start.106 = (bf16[8,96,768]{2,1,0:T(8,128)(2,1)S(1)}, bf16[8,96,768]{2,1,0:T(8,128)(2,1)S(1)}, u32[]{:S(2)}, u32[]{:S(2)}) collective-permute-start(bf16[8,96,768]{2,1,0:T(8,128)(2,1)S(1)} %dynamic-slice_bitcast_fusion.7), channel_id=1, source_target_pairs={{0,1},{1,0},{2,3},{3,2},{4,5},{5,4},{6,7},{7,6},{8,9},{9,8},{10,11... | collective-permute-start | bytes 3538952 | tf_op jit(solution)/shard_map/ppermute | solution.py:171
  774.5 102.6 %collective-permute-start.88 = (bf16[8,24,3072]{2,1,0:T(8,128)(2,1)S(1)}, bf16[8,24,3072]{2,1,0:T(8,128)(2,1)S(1)}, u32[]{:S(2)}, u32[]{:S(2)}) collective-permute-start(bf16[8,24,3072]{2,1,0:T(8,128)(2,1)S(1)} %dynamic-slice_bitcast_fusion.9), channel_id=1, source_target_pairs={{0,1},{1,0},{2,3},{3,2},{4,5},{5,4},{6,7},{7,6},{8,9},{9,8},{10,11... | collective-permute-start | bytes 3538952 | tf_op jit(solution)/shard_map/ppermute | solution.py:171
  776.2 102.5 %collective-permute-start.97 = (bf16[8,96,768]{2,1,0:T(8,128)(2,1)S(1)}, bf16[8,96,768]{2,1,0:T(8,128)(2,1)S(1)}, u32[]{:S(2)}, u32[]{:S(2)}) collective-permute-start(bf16[8,96,768]{2,1,0:T(8,128)(2,1)S(1)} %dynamic-slice_bitcast_fusion.8), channel_id=1, source_target_pairs={{0,1},{1,0},{2,3},{3,2},{4,5},{5,4},{6,7},{7,6},{8,9},{9,8},{10,11... | collective-permute-start | bytes 3538952 | tf_op jit(solution)/shard_map/ppermute | solution.py:171
  803.3 100.7 %collective-permute-start.79 = (bf16[8,24,3072]{2,1,0:T(8,128)(2,1)S(1)}, bf16[8,24,3072]{2,1,0:T(8,128)(2,1)S(1)}, u32[]{:S(2)}, u32[]{:S(2)}) collective-permute-start(bf16[8,24,3072]{2,1,0:T(8,128)(2,1)S(1)} %dynamic-slice_bitcast_fusion.10), channel_id=1, source_target_pairs={{0,1},{1,0},{2,3},{3,2},{4,5},{5,4},{6,7},{7,6},{8,9},{9,8},{10,11... | collective-permute-start | bytes 3538952 | tf_op jit(solution)/shard_map/ppermute | solution.py:171
  875.2 29.3 %collective-permute-start.57 = (bf16[2,24,2304]{2,1,0:T(8,128)(2,1)S(1)}, bf16[2,24,2304]{2,1,0:T(8,128)(2,1)S(1)}, u32[]{:S(2)}, u32[]{:S(2)}) collective-permute-start(bf16[2,24,2304]{2,1,0:T(8,128)(2,1)S(1)} %bitcast.788), channel_id=1, source_target_pairs={{0,8},{2,10},{4,12},{6,14},{8,0},{10,2},{12,4},{14,6},{16,24},{18,... | collective-permute-start | bytes 663560 | tf_op jit(solution)/shard_map/ppermute | solution.py:171
  875.5 30.2 %collective-permute-start.48 = (bf16[2,24,2304]{2,1,0:T(8,128)(2,1)S(1)}, bf16[2,24,2304]{2,1,0:T(8,128)(2,1)S(1)}, u32[]{:S(2)}, u32[]{:S(2)}) collective-permute-start(bf16[2,24,2304]{2,1,0:T(8,128)(2,1)S(1)} %bitcast.791), channel_id=1, source_target_pairs={{0,8},{2,10},{4,12},{6,14},{8,0},{10,2},{12,4},{14,6},{16,24},{18,... | collective-permute-start | bytes 663560 | tf_op jit(solution)/shard_map/ppermute | solution.py:171
  877.2 29.1 %collective-permute-start.107 = (bf16[4,96,768]{2,1,0:T(8,128)(2,1)S(1)}, bf16[4,96,768]{2,1,0:T(8,128)(2,1)S(1)}, u32[]{:S(2)}, u32[]{:S(2)}) collective-permute-start(bf16[4,96,768]{2,1,0:T(8,128)(2,1)S(1)} %dynamic-slice_bitcast_fusion.14), channel_id=1, source_target_pairs={{0,4},{2,6},{4,0},{6,2},{8,12},{10,14},{12,8},{14,10},{16,20},{18,... | collective-permute-start | bytes 1769480 | tf_op jit(solution)/shard_map/ppermute | solution.py:171
  878.7 28.9 %collective-permute-start.89 = (bf16[4,24,3072]{2,1,0:T(8,128)(2,1)S(1)}, bf16[4,24,3072]{2,1,0:T(8,128)(2,1)S(1)}, u32[]{:S(2)}, u32[]{:S(2)}) collective-permute-start(bf16[4,24,3072]{2,1,0:T(8,128)(2,1)S(1)} %dynamic-slice_bitcast_fusion.16), channel_id=1, source_target_pairs={{0,4},{2,6},{4,0},{6,2},{8,12},{10,14},{12,8},{14,10},{16,20},{18,... | collective-permute-start | bytes 1769480 | tf_op jit(solution)/shard_map/ppermute | solution.py:171
  905.7 29.4 %collective-permute-start.58 = (bf16[4,24,2304]{2,1,0:T(8,128)(2,1)S(1)}, bf16[4,24,2304]{2,1,0:T(8,128)(2,1)S(1)}, u32[]{:S(2)}, u32[]{:S(2)}) collective-permute-start(bf16[4,24,2304]{2,1,0:T(8,128)(2,1)S(1)} %bitcast.761), channel_id=1, source_target_pairs={{0,4},{2,6},{4,0},{6,2},{8,12},{10,14},{12,8},{14,10},{16,20},{18,... | collective-permute-start | bytes 1327112 | tf_op jit(solution)/shard_map/ppermute | solution.py:171
  906.3 38.3 %collective-permute-start.49 = (bf16[4,24,2304]{2,1,0:T(8,128)(2,1)S(1)}, bf16[4,24,2304]{2,1,0:T(8,128)(2,1)S(1)}, u32[]{:S(2)}, u32[]{:S(2)}) collective-permute-start(bf16[4,24,2304]{2,1,0:T(8,128)(2,1)S(1)} %bitcast.760), channel_id=1, source_target_pairs={{0,4},{2,6},{4,0},{6,2},{8,12},{10,14},{12,8},{14,10},{16,20},{18,... | collective-permute-start | bytes 1327112 | tf_op jit(solution)/shard_map/ppermute | solution.py:171
  907.6 43.9 %collective-permute-start.108 = (bf16[2,96,768]{2,1,0:T(8,128)(2,1)S(1)}, bf16[2,96,768]{2,1,0:T(8,128)(2,1)S(1)}, u32[]{:S(2)}, u32[]{:S(2)}) collective-permute-start(bf16[2,96,768]{2,1,0:T(8,128)(2,1)S(1)} %dynamic-slice_bitcast_fusion.23), channel_id=1, source_target_pairs={{0,8},{2,10},{4,12},{6,14},{8,0},{10,2},{12,4},{14,6},{16,24},{18,... | collective-permute-start | bytes 884744 | tf_op jit(solution)/shard_map/ppermute | solution.py:171
  912.7 39.0 %collective-permute-start.90 = (bf16[2,24,3072]{2,1,0:T(8,128)(2,1)S(1)}, bf16[2,24,3072]{2,1,0:T(8,128)(2,1)S(1)}, u32[]{:S(2)}, u32[]{:S(2)}) collective-permute-start(bf16[2,24,3072]{2,1,0:T(8,128)(2,1)S(1)} %dynamic-slice_bitcast_fusion.25), channel_id=1, source_target_pairs={{0,8},{2,10},{4,12},{6,14},{8,0},{10,2},{12,4},{14,6},{16,24},{18,... | collective-permute-start | bytes 884744 | tf_op jit(solution)/shard_map/ppermute | solution.py:171
  925.6 26.5 %collective-permute-start.99 = (bf16[2,96,768]{2,1,0:T(8,128)(2,1)S(1)}, bf16[2,96,768]{2,1,0:T(8,128)(2,1)S(1)}, u32[]{:S(2)}, u32[]{:S(2)}) collective-permute-start(bf16[2,96,768]{2,1,0:T(8,128)(2,1)S(1)} %dynamic-slice_bitcast_fusion.24), channel_id=1, source_target_pairs={{0,8},{2,10},{4,12},{6,14},{8,0},{10,2},{12,4},{14,6},{16,24},{18,... | collective-permute-start | bytes 884744 | tf_op jit(solution)/shard_map/ppermute | solution.py:171
  944.6 83.4 %collective-permute-start.59 = (bf16[8,24,2304]{2,1,0:T(8,128)(2,1)S(1)}, bf16[8,24,2304]{2,1,0:T(8,128)(2,1)S(1)}, u32[]{:S(2)}, u32[]{:S(2)}) collective-permute-start(bf16[8,24,2304]{2,1,0:T(8,128)(2,1)S(1)} %bitcast.725), channel_id=1, source_target_pairs={{0,2},{2,0},{4,6},{6,4},{8,10},{10,8},{12,14},{14,12},{16,18},{18,... | collective-permute-start | bytes 2654216 | tf_op jit(solution)/shard_map/ppermute | solution.py:171
  951.5 77.4 %collective-permute-start.50 = (bf16[8,24,2304]{2,1,0:T(8,128)(2,1)S(1)}, bf16[8,24,2304]{2,1,0:T(8,128)(2,1)S(1)}, u32[]{:S(2)}, u32[]{:S(2)}) collective-permute-start(bf16[8,24,2304]{2,1,0:T(8,128)(2,1)S(1)} %bitcast.723), channel_id=1, source_target_pairs={{0,2},{2,0},{4,6},{6,4},{8,10},{10,8},{12,14},{14,12},{16,18},{18,... | collective-permute-start | bytes 2654216 | tf_op jit(solution)/shard_map/ppermute | solution.py:171
  1026.5 25.0 %collective-permute-start.103 = (bf16[4,96,768]{2,1,0:T(8,128)(2,1)S(1)}, bf16[4,96,768]{2,1,0:T(8,128)(2,1)S(1)}, u32[]{:S(2)}, u32[]{:S(2)}) collective-permute-start(bf16[4,96,768]{2,1,0:T(8,128)(2,1)S(1)} %bitcast.732), channel_id=1, source_target_pairs={{0,4},{2,6},{4,0},{6,2},{8,12},{10,14},{12,8},{14,10},{16,20},{18,... | collective-permute-start | bytes 1769480 | tf_op jit(solution)/shard_map/ppermute | solution.py:171
  1028.0 36.2 %collective-permute-start.85 = (bf16[4,24,3072]{2,1,0:T(8,128)(2,1)S(1)}, bf16[4,24,3072]{2,1,0:T(8,128)(2,1)S(1)}, u32[]{:S(2)}, u32[]{:S(2)}) collective-permute-start(bf16[4,24,3072]{2,1,0:T(8,128)(2,1)S(1)} %bitcast.729), channel_id=1, source_target_pairs={{0,4},{2,6},{4,0},{6,2},{8,12},{10,14},{12,8},{14,10},{16,20},{18,... | collective-permute-start | bytes 1769480 | tf_op jit(solution)/shard_map/ppermute | solution.py:171
  1032.7 35.8 %collective-permute-start.113 = (bf16[8,96,768]{2,1,0:T(8,128)(2,1)S(1)}, bf16[8,96,768]{2,1,0:T(8,128)(2,1)S(1)}, u32[]{:S(2)}, u32[]{:S(2)}) collective-permute-start(bf16[8,96,768]{2,1,0:T(8,128)(2,1)S(1)} %bitcast.692), channel_id=1, source_target_pairs={{0,2},{2,0},{4,6},{6,4},{8,10},{10,8},{12,14},{14,12},{16,18},{18,... | collective-permute-start | bytes 3538952 | tf_op jit(solution)/shard_map/ppermute | solution.py:171
  1038.9 30.1 %collective-permute-start.95 = (bf16[8,24,3072]{2,1,0:T(8,128)(2,1)S(1)}, bf16[8,24,3072]{2,1,0:T(8,128)(2,1)S(1)}, u32[]{:S(2)}, u32[]{:S(2)}) collective-permute-start(bf16[8,24,3072]{2,1,0:T(8,128)(2,1)S(1)} %bitcast.690), channel_id=1, source_target_pairs={{0,2},{2,0},{4,6},{6,4},{8,10},{10,8},{12,14},{14,12},{16,18},{18,... | collective-permute-start | bytes 3538952 | tf_op jit(solution)/shard_map/ppermute | solution.py:171
  (239 other events, 2948.0 us)

commit v2 on v1

v2 whole, which is shorter than its diff:
```python
import jax
import jax.numpy as jnp
from jax import lax
from jax.experimental import pallas as pl
from jax.experimental.pallas import tpu as pltpu
from jax.sharding import PartitionSpec as P

HEAD_DIM = 64
PATCHES = 256
CAPTION = 77
PAIR = 2 * HEAD_DIM


epsilon = 1e-05
masked_score = -1e30
low = jnp.bfloat16
full = jnp.float32
ANY = pl.BlockSpec(memory_space=pl.ANY)
SCALARS = pl.BlockSpec(memory_space=pltpu.SMEM)


def dot(left, right, contract=(1, 0)):
    dims = (((contract[0],), (contract[1],)), ((), ()))
    return lax.dot_general(left, right, dims, preferred_element_type=full)


def normalize(values):
    centred = values - jnp.mean(values, axis=-1, keepdims=True)
    factor = lax.rsqrt(jnp.mean(centred * centred, axis=-1, keepdims=True) + epsilon)
    return centred * factor, factor


def normalize_back(upstream, normed, factor):
    return factor * (
        upstream
        - jnp.mean(upstream, axis=-1, keepdims=True)
        - normed * jnp.mean(upstream * normed, axis=-1, keepdims=True)
    )


def column_sum(values):
    return jnp.sum(values.astype(full), axis=0, keepdims=True)


def whole(shape):
    return pl.BlockSpec(shape, lambda *grid: (0,) * len(shape))


def call(body, grid, ins, outs, name, scratch=(), aliases=None, limit=56):
    return pl.pallas_call(
        body,
        grid=grid,
        in_specs=[spec for _, spec in ins],
        out_specs=[spec for _, _, spec in outs],
        out_shape=[jax.ShapeDtypeStruct(shape, kind) for shape, kind, _ in outs],
        scratch_shapes=list(scratch),
        name=name,
        input_output_aliases=aliases or {},
        cost_estimate=pl.CostEstimate(flops=10**6, bytes_accessed=10**6, transcendentals=0),
        compiler_params=pltpu.CompilerParams(vmem_limit_bytes=limit * 2**20),
    )(*[array for array, _ in ins])


class Weight:
    def __init__(self, array, layer, width, spots):
        self.array, self.layer, self.width, self.spots = array, layer, width, spots
        shard = array if layer is None else array[layer]
        self.rows, self.columns = shard.shape
        self.shares = lax.axis_size("narrow")
        self.blocks = self.columns // width
        self.total = self.rows * self.shares
        self.sharing = masks("wide")[:2]
        while self.rows % (16 << len(self.sharing)):
            self.sharing.pop()
        self.count = 1 << len(self.sharing)
        self.length = self.rows // self.count
        place = lax.axis_index("wide") & (self.count - 1)
        self.piece = lax.dynamic_slice_in_dim(shard, place * self.length, self.length)

    def fetch(self, *earlier):
        held = after(self.piece, *earlier)[None]
        for mask in masks("narrow"):
            held = jnp.concatenate([held, swap(held, "narrow", mask)])
        self.pieces = {0: held[1:]}

    def share(self, which, *earlier):
        if which < len(self.sharing):
            mask = self.sharing[which]
            got = {key ^ mask: swap(after(piece, *earlier), "wide", mask) for key, piece in self.pieces.items()}
            self.pieces.update(got)

    def arrays(self):
        return [self.array] + list(self.pieces.values())

    def scratch(self):
        copies = 1 + len(self.pieces) * (self.shares - 1)
        return [pltpu.VMEM((self.blocks, self.total, self.width), low), pltpu.SemaphoreType.DMA((self.blocks, copies))]

    def copies(self, spots, refs, held, signals, block):
        own, pieces = refs[0], refs[1:]
        columns = pl.ds(block * self.width, self.width)
        me = spots[0]
        own = own if self.layer is None else own.at[self.layer]
        begin = pl.multiple_of(me * self.rows, 16)
        found = [(own.at[:, columns], begin, self.rows)]
        for key, piece in zip(self.pieces, pieces):
            for offset in range(1, self.shares):
                begin = (me ^ offset) * self.rows + ((spots[1] & (self.count - 1)) ^ key) * self.length
                found.append((piece.at[offset - 1, :, columns], pl.multiple_of(begin, 16), self.length))
        return [
            pltpu.make_async_copy(source, held.at[block, pl.ds(begin, length)], signals.at[block, place])
            for place, (source, begin, length) in enumerate(found)
        ]

    def start(self, *refs):
        for block in range(self.blocks):
            for copy in self.copies(*refs, block):
                copy.start()

    def wait(self, *refs, block=0):
        for copy in self.copies(*refs, block):
            copy.wait()


def weighted(body, weights, grid, ins, outs, name, scratch=()):
    spots = weights[0].spots
    operands = [(spots, SCALARS)] + [(array, ANY) for weight in weights for array in weight.arrays()]
    counts = [len(weight.arrays()) for weight in weights]
    extra = [piece for weight in weights for piece in weight.scratch()]

    def wrapped(*refs):
        spots_ref, rest = refs[0], list(refs[1:])
        sources = []
        for count in counts:
            sources.append(rest[:count])
            rest = rest[count:]
        spare = rest[len(rest) - len(extra) :]
        rest = rest[: len(rest) - len(extra)]
        handles = []
        for place, weight in enumerate(weights):
            held, signals = spare[2 * place : 2 * place + 2]
            refs_of = (spots_ref, sources[place], held, signals)
            handles.append((weight, refs_of, held))

        @pl.when(pl.program_id(0) == 0)
        def _():
            for weight, refs_of, _ in handles:
                weight.start(*refs_of)

        def ready(place, block=0):
            weight, refs_of, held = handles[place]
            weight.wait(*refs_of, block=block)

        body(ready, [held for _, _, held in handles], *rest)

    return call(wrapped, grid, operands + ins, outs, name, list(scratch) + extra)


def project_qkv(inputs, gain, shift, weight):
    rows, width = inputs.shape

    def body(ready, held, x_ref, gain_ref, shift_ref, a_ref, out_ref):
        step = pl.program_id(0)

        @pl.when(step == 0)
        def _():
            normed, _ = normalize(x_ref[...].astype(full))
            a_ref[...] = (normed * gain_ref[...] + shift_ref[...]).astype(low)

        ready(0, step)
        scale = jnp.where(step == 0, HEAD_DIM ** (-0.5), 1.0)
        out_ref[0] = (dot(a_ref[...], held[0][step]).astype(low).astype(full) * scale).astype(low)

    return weighted(
        body,
        [weight],
        (3,),
        [
            (inputs, whole((rows, width))),
            (gain, whole((1, width))),
            (shift, whole((1, width))),
        ],
        [
            ((rows, width), low, whole((rows, width))),
            ((3, rows, width), low, pl.BlockSpec((1, rows, width), lambda j: (j, 0, 0))),
        ],
        "project_qkv",
    )


def join_qkv(middle, skip, join_weight, join_shift, gain, shift, weight):
    rows, width = middle.shape

    def body(ready, held, m_ref, s_ref, jb_ref, gain_ref, shift_ref, e_ref, a_ref, out_ref):
        step = pl.program_id(0)

        @pl.when(step == 0)
        def _():
            ready(0)
            entry = dot(m_ref[...], held[0][0, :width]) + dot(s_ref[...], held[0][0, width:]) + jb_ref[...]
            e_ref[...] = entry
            normed, _ = normalize(entry)
            a_ref[...] = (normed * gain_ref[...] + shift_ref[...]).astype(low)

        ready(1, step)
        scale = jnp.where(step == 0, HEAD_DIM ** (-0.5), 1.0)
        out_ref[0] = (dot(a_ref[...], held[1][step]).astype(low).astype(full) * scale).astype(low)

    return weighted(
        body,
        [join_weight, weight],
        (3,),
        [
            (middle, whole((rows, width))),
            (skip, whole((rows, width))),
            (join_shift, whole((1, width))),
            (gain, whole((1, width))),
            (shift, whole((1, width))),
        ],
        [
            ((rows, width), full, whole((rows, width))),
            ((rows, width), low, whole((rows, width))),
            ((3, rows, width), low, pl.BlockSpec((1, rows, width), lambda j: (j, 0, 0))),
        ],
        "join_qkv",
    )


def head_masks(seq_rows):
    lane = lax.broadcasted_iota(jnp.int32, (seq_rows, PAIR), 1)
    return [lane < HEAD_DIM, lane >= HEAD_DIM]


def attend(packed, lengths, items, seq_rows):
    width = packed.shape[-1]
    pairs = width // PAIR

    def body(length_ref, q_ref, k_ref, v_ref, out_ref, total_ref):
        length = length_ref[pl.program_id(0)]
        queries, keys, values = q_ref[0, 0], k_ref[0, 0], v_ref[0, 0]
        counts = lax.broadcasted_iota(jnp.int32, (seq_rows, seq_rows), 0) < length
        mixed = jnp.zeros((PAIR, seq_rows), full)
        for head, lanes in enumerate(head_masks(seq_rows)):
            scores = dot(keys, jnp.where(lanes, queries, 0), (1, 1))
            scores = jnp.where(counts, scores, masked_score)
            largest = jnp.max(scores, axis=0, keepdims=True)
            weights = jnp.exp(scores - largest)
            total = jnp.sum(weights, axis=0, keepdims=True)
            part = dot(jnp.where(lanes, values, 0), weights.astype(low), (0, 0))
            mixed += part * (1.0 / total)
            total_ref[0, 0, head : head + 1] = largest + jnp.log(total)
        out_ref[0] = mixed.T.astype(low)

    def block(which):
        return pl.BlockSpec((1, 1, seq_rows, PAIR), lambda n, h: (which, n, 0, h))

    return call(
        body,
        (items, pairs),
        [
            (lengths, SCALARS),
            (packed, block(0)),
            (packed, block(1)),
            (packed, block(2)),
        ],
        [
            ((items, seq_rows, width), low, pl.BlockSpec((1, seq_rows, PAIR), lambda n, h: (n, 0, h))),
            ((items, pairs, 8, seq_rows), full, pl.BlockSpec((1, 1, 8, seq_rows), lambda n, h: (n, h, 0, 0))),
        ],
        "attend",
    )


def attend_back(packed, grad_mixed, totals, lengths, items, seq_rows):
    width = packed.shape[-1]
    pairs = width // PAIR

    def body(length_ref, q_ref, k_ref, v_ref, g_ref, total_ref, out_ref):
        length = length_ref[pl.program_id(0)]
        queries, keys, values, upstream = q_ref[0, 0], k_ref[0, 0], v_ref[0, 0], g_ref[0]
        counts = lax.broadcasted_iota(jnp.int32, (seq_rows, seq_rows), 0) < length
        grad_queries = jnp.zeros((PAIR, seq_rows), full)
        grad_keys = jnp.zeros((seq_rows, PAIR), full)
        grad_values = jnp.zeros((seq_rows, PAIR), full)
        for head, lanes in enumerate(head_masks(seq_rows)):
            own_queries = jnp.where(lanes, queries, 0)
            own_upstream = jnp.where(lanes, upstream, 0)
            scores = dot(keys, own_queries, (1, 1))
            shifted = jnp.where(counts, scores, masked_score) - total_ref[0, 0, head : head + 1]
            probs = jnp.exp(shifted)
            grad_probs = dot(values, own_upstream, (1, 1))
            centre = jnp.sum(grad_probs * probs, axis=0, keepdims=True)
            grad_scores = (probs * (grad_probs - centre)).astype(low)
            grad_values += dot(probs.astype(low), own_upstream)
            grad_keys += dot(grad_scores, own_queries)
            grad_queries += dot(jnp.where(lanes, keys, 0), grad_scores, (0, 0))
        out_ref[0, 0] = (grad_queries.T * HEAD_DIM ** (-0.5)).astype(low)
        out_ref[1, 0] = grad_keys.astype(low)
        out_ref[2, 0] = grad_values.astype(low)

    def block(which):
        return pl.BlockSpec((1, 1, seq_rows, PAIR), lambda n, h: (which, n, 0, h))

    return call(
        body,
        (items, pairs),
        [
            (lengths, SCALARS),
            (packed, block(0)),
            (packed, block(1)),
            (packed, block(2)),
            (grad_mixed, pl.BlockSpec((1, seq_rows, PAIR), lambda n, h: (n, 0, h))),
            (totals, pl.BlockSpec((1, 1, 8, seq_rows), lambda n, h: (n, h, 0, 0))),
        ],
        [
            ((3, items, seq_rows, width), low, pl.BlockSpec((3, 1, seq_rows, PAIR), lambda n, h: (0, n, 0, h))),
        ],
        "attend_back",
    )[0]


def gelu_parts(before):
    decay = jnp.exp(before * before * -0.5)
    inverse = pl.reciprocal(1.0 + (0.3275911 * 0.5**0.5) * jnp.abs(before), approx=False)
    series = 1.061405429 * 0.5
    for term in (-1.453152027, 1.421413741, -0.284496736, 0.254829592):
        series = series * inverse + term * 0.5
    below = series * inverse * decay
    share = jnp.where(before >= 0, 1.0 - below, below)
    return before * share, share + before * decay * 0.3989422804014327


def feed_forward(inputs, mixed, out_weight, out_bias, gain, shift, up_weight, up_bias, down_weight, down_bias, keep):
    rows, width = inputs.shape
    steps = up_weight.blocks
    hidden = steps * width

    def body(ready, held, x_ref, o_ref, ob_ref, gain_ref, shift_ref, ub_ref, db_ref, keep_ref, m_ref, a_ref, g_ref, s_ref, y_ref, total):
        step = pl.program_id(0)

        @pl.when(step == 0)
        def _():
            ready(0)
            middle = x_ref[...].astype(full) + dot(o_ref[...], held[0][0]) + ob_ref[...]
            m_ref[...] = middle
            normed, _ = normalize(middle)
            a_ref[...] = (normed * gain_ref[...] + shift_ref[...]).astype(low)
            total[...] = middle + db_ref[...]

        ready(1, step)
        before = dot(a_ref[...], held[1][step]) + ub_ref[...]
        value, slope = gelu_parts(before)
        g_ref[...] = value.astype(low)
        s_ref[...] = slope.astype(low)

        @pl.when(step == 0)
        def _():
            ready(2)

        total[...] += dot(g_ref[...], held[2][0, pl.ds(pl.multiple_of(step * width, width), width)])

        @pl.when(step == steps - 1)
        def _():
            y_ref[...] = jnp.where(keep_ref[...] > 0, total[...], 0.0).astype(low)

    return weighted(
        body,
        [out_weight, up_weight, down_weight],
        (steps,),
        [
            (inputs, whole((rows, width))),
            (mixed, whole((rows, width))),
            (out_bias, whole((1, width))),
            (gain, whole((1, width))),
            (shift, whole((1, width))),
            (up_bias, pl.BlockSpec((1, width), lambda j: (0, j))),
            (down_bias, whole((1, width))),
            (keep, whole((rows, 1))),
        ],
        [
            ((rows, width), full, whole((rows, width))),
            ((rows, width), low, whole((rows, width))),
            ((rows, hidden), low, pl.BlockSpec((rows, width), lambda j: (0, j))),
            ((rows, hidden), low, pl.BlockSpec((rows, width), lambda j: (0, j))),
            ((rows, width), low, whole((rows, width))),
        ],
        "feed_forward",
        scratch=[pltpu.VMEM((rows, width), full)],
    )


def feed_forward_back(upstream, slope, down_weight, up_weight, middle, gain, out_weight, keep):
    rows, width = upstream.shape
    steps = up_weight.blocks
    hidden = steps * width

    def body(ready, held, y_ref, keep_ref, s_ref, m_ref, gain_ref, du_ref, dm_ref, db_ref, do_ref, dz_ref, sums_ref, usum_ref, total):
        step = pl.program_id(0)

        @pl.when(step == 0)
        def _():
            rounded = jnp.where(keep_ref[...] > 0, y_ref[...].astype(full), 0.0).astype(low)
            dz_ref[...] = rounded
            sums_ref[0:1] = column_sum(rounded)
            total[...] = jnp.zeros_like(total)
            ready(0)

        down = held[0][0, pl.ds(pl.multiple_of(step * width, width), width)]
        grad = (dot(dz_ref[...], down, (1, 1)) * s_ref[...].astype(full)).astype(low)
        du_ref[...] = grad
        usum_ref[...] = column_sum(grad)
        ready(1, step)
        total[...] += dot(grad, held[1][step], (1, 1))

        @pl.when(step == steps - 1)
        def _():
            grad_second = total[...]
            normed, factor = normalize(m_ref[...])
            sums_ref[1:2] = column_sum(grad_second * normed)
            sums_ref[2:3] = column_sum(grad_second)
            incoming = jnp.where(keep_ref[...] > 0, y_ref[...].astype(full), 0.0)
            grad_middle = incoming + normalize_back(grad_second * gain_ref[...], normed, factor)
            dm_ref[...] = grad_middle
            branch = grad_middle.astype(low)
            db_ref[...] = branch
            sums_ref[3:4] = column_sum(branch)
            ready(2)
            do_ref[...] = dot(branch, held[2][0], (1, 1)).astype(low)

    return weighted(
        body,
        [down_weight, up_weight, out_weight],
        (steps,),
        [
            (upstream, whole((rows, width))),
            (keep, whole((rows, 1))),
            (slope, pl.BlockSpec((rows, width), lambda j: (0, j))),
            (middle, whole((rows, width))),
            (gain, whole((1, width))),
        ],
        [
            ((rows, hidden), low, pl.BlockSpec((rows, width), lambda j: (0, j))),
            ((rows, width), full, whole((rows, width))),
            ((rows, width), low, whole((rows, width))),
            ((rows, width), low, whole((rows, width))),
            ((rows, width), low, whole((rows, width))),
            ((8, width), full, whole((8, width))),
            ((1, hidden), full, pl.BlockSpec((1, width), lambda j: (0, j))),
        ],
        "feed_forward_back",
        scratch=[pltpu.VMEM((rows, width), full)],
    )


def project_back(grad_packed, weight, inputs, gain, grad_middle, join_weight=None):
    rows, width = inputs.shape
    joined = join_weight is not None

    def body(ready, held, g_ref, x_ref, gain_ref, dm_ref, *rest):
        if joined:
            de_ref, dx_ref, skip_ref, sums_ref, total = rest
        else:
            dx_ref, sums_ref, total = rest
        step = pl.program_id(0)

        @pl.when(step == 0)
        def _():
            total[...] = jnp.zeros_like(total)

        ready(0, step)
        total[...] += dot(g_ref[0], held[0][step], (1, 1))

        @pl.when(step == 2)
        def _():
            grad_first = total[...]
            normed, factor = normalize(x_ref[...].astype(full))
            sums_ref[0:1] = column_sum(grad_first * normed)
            sums_ref[1:2] = column_sum(grad_first)
            grad = dm_ref[...] + normalize_back(grad_first * gain_ref[...], normed, factor)
            if joined:
                entry = grad.astype(low)
                de_ref[...] = entry
                sums_ref[2:3] = column_sum(entry)
                ready(1)
                dx_ref[...] = dot(entry, held[1][0, :width], (1, 1))
                skip_ref[...] = dot(entry, held[1][0, width:], (1, 1))
            else:
                dx_ref[...] = grad

    ins = [
        (grad_packed, pl.BlockSpec((1, rows, width), lambda j: (j, 0, 0))),
        (inputs, whole((rows, width))),
        (gain, whole((1, width))),
        (grad_middle, whole((rows, width))),
    ]
    outs = [((rows, width), full, whole((rows, width))), ((8, width), full, whole((8, width)))]
    if joined:
        outs = [((rows, width), low, whole((rows, width))), outs[0], outs[0], outs[1]]
    return weighted(
        body,
        [weight] + ([join_weight] if joined else []),
        (3,),
        ins,
        outs,
        "project_back",
        scratch=[pltpu.VMEM((rows, width), full)],
    )


def picked(body, which, grid, ins, outs, name, aliases=None):
    return pl.pallas_call(
        body,
        grid_spec=pltpu.PrefetchScalarGridSpec(
            num_scalar_prefetch=1,
            grid=grid,
            in_specs=[spec for _, spec in ins],
            out_specs=[spec for _, _, spec in outs],
        ),
        out_shape=[jax.ShapeDtypeStruct(shape, kind) for shape, kind, _ in outs],
        name=name,
        input_output_aliases={place + 1: out for place, out in (aliases or {}).items()},
        cost_estimate=pl.CostEstimate(flops=10**6, bytes_accessed=10**6, transcendentals=0),
        compiler_params=pltpu.CompilerParams(vmem_limit_bytes=48 * 2**20),
    )(which, *[array for array, _ in ins])


def up_term(left, right, core):
    rows, width = left.shape
    shares = lax.axis_size("narrow")
    part = width // shares

    def body(core_ref, l_ref, r_ref, out_ref):
        out_ref[...] = dot(l_ref[...], r_ref[...], (0, 0)).astype(low).reshape(shares, 1, part, width)

    return picked(
        body,
        core,
        (2,),
        [
            (left, pl.BlockSpec((rows, width), lambda g, core: (0, 0))),
            (right, pl.BlockSpec((rows, width), lambda g, core: (0, core[0] * 2 + g))),
        ],
        [((shares, 2, part, width), low, pl.BlockSpec((shares, 1, part, width), lambda g, core: (0, g, 0, 0)))],
        "up_term",
    )[0].reshape(shares, 2 * part, width)


def qkv_out_term(first, packed, mixed, branch, core):
    rows, width = first.shape
    shares = lax.axis_size("narrow")
    part = width // shares

    def body(core_ref, l_ref, r_ref, o_ref, b_ref, out_ref):
        last = core_ref[0] * 2 + pl.program_id(0) == 3

        @pl.when(last)
        def _():
            out_ref[...] = dot(o_ref[...], b_ref[...], (0, 0)).astype(low).reshape(shares, 1, part, width)

        @pl.when(jnp.logical_not(last))
        def _():
            out_ref[...] = dot(l_ref[...], r_ref[0], (0, 0)).astype(low).reshape(shares, 1, part, width)

    flat = pl.BlockSpec((rows, width), lambda g, core: (0, 0))
    return picked(
        body,
        core,
        (2,),
        [
            (first, flat),
            (packed, pl.BlockSpec((1, rows, width), lambda g, core: (jnp.minimum(core[0] * 2 + g, 2), 0, 0))),
            (mixed, flat),
            (branch, flat),
        ],
        [((shares, 2, part, width), low, pl.BlockSpec((shares, 1, part, width), lambda g, core: (0, g, 0, 0)))],
        "qkv_out_term",
    )[0].reshape(shares, 2 * part, width)


def down_term(left, right, core):
    rows, width = right.shape
    shares = lax.axis_size("narrow")
    part = left.shape[1] // (2 * shares)
    direct = part == width
    if not direct:
        left = left.reshape(rows, shares, 2, part)
        left = lax.dynamic_index_in_dim(left, core[0], 2, keepdims=False).reshape(rows, shares * part)
    steps = shares * part // width

    def body(core_ref, l_ref, r_ref, out_ref):
        out_ref[...] = dot(l_ref[...], r_ref[...], (0, 0)).astype(low)

    return picked(
        body,
        core,
        (steps,),
        [
            (left, pl.BlockSpec((rows, width), lambda g, core: (0, g * 2 + core[0] if direct else g))),
            (right, pl.BlockSpec((rows, width), lambda g, core: (0, 0))),
        ],
        [((shares * part, width), low, pl.BlockSpec((width, width), lambda g, core: (g, 0)))],
        "down_term",
    )[0].reshape(shares, part, width)


def join_term(middle, skip, right, core):
    rows, width = right.shape
    shares = lax.axis_size("narrow")
    half = width // 2

    def body(core_ref, m_ref, s_ref, r_ref, out_ref):
        out_ref[:width] = dot(m_ref[...], r_ref[...], (0, 0)).astype(low)
        out_ref[width:] = dot(s_ref[...], r_ref[...], (0, 0)).astype(low)

    flat = pl.BlockSpec((rows, width), lambda g, core: (0, 0))
    return picked(
        body,
        core,
        (1,),
        [(middle, flat), (skip, flat), (right, pl.BlockSpec((rows, half), lambda g, core: (0, core[0])))],
        [((2 * width, half), low, pl.BlockSpec((2 * width, half), lambda g, core: (0, 0)))],
        "join_term",
    )[0].reshape(shares, 2 * width // shares, half)


def add_halve(kept, got, bit):
    _, rows, columns = kept.shape
    steps = 2 if rows % 32 == 0 and rows >= 256 else 1
    block = pl.BlockSpec((2, rows // steps, columns), lambda g, bit: (0, g, 0))
    out = ((rows, columns), low, pl.BlockSpec((rows // steps, columns), lambda g, bit: (g, 0)))

    def body(bit_ref, kept_ref, got_ref, sent_ref, left_ref):
        mine = bit_ref[0]
        for target, place in ((sent_ref, 1 - mine), (left_ref, mine)):
            target[...] = (kept_ref[place].astype(full) + got_ref[place].astype(full)).astype(low)

    return picked(body, bit, (steps,), [(kept, block), (got, block)], [out, out], "add_halve")


def pair_up(own, got, bit):
    rows, columns = own.shape

    def body(bit_ref, own_ref, got_ref, out_ref):
        mine = bit_ref[0]
        out_ref[mine] = own_ref[...]
        out_ref[1 - mine] = got_ref[...]

    flat = pl.BlockSpec((rows, columns), lambda g, bit: (0, 0))
    out = ((2, rows, columns), low, pl.BlockSpec((2, rows, columns), lambda g, bit: (0, 0, 0)))
    return picked(body, bit, (1,), [(own, flat), (got, flat)], [out], "pair_up")[0]


def finish(kind, own, got, core, scale, layer, targets):
    shares = lax.axis_size("narrow")
    columns = own.shape[-1]
    aliases = {place + 2: place for place in range(len(targets))}

    def chosen(core_ref, half, own_ref, got_ref):
        return jnp.where(core_ref[0] == half, own_ref[...], got_ref[...]).astype(full) * scale

    if kind == "join":
        rows = own.shape[0]

        def body(core_ref, own_ref, got_ref, out_ref):
            out_ref[:, :columns] = chosen(core_ref, 0, own_ref, got_ref)
            out_ref[:, columns:] = chosen(core_ref, 1, own_ref, got_ref)

        flat = pl.BlockSpec((rows, columns), lambda g, core: (0, 0))
        out = ((rows, 2 * columns), full, pl.BlockSpec((rows, 2 * columns), lambda g, core: (0, 0)))
        return picked(body, core, (1,), [(own, flat), (got, flat)], [out], "finish_join")
    if kind == "down":
        rows = own.shape[0]

        def body(core_ref, own_ref, got_ref, *rest):
            rest[-1][0] = chosen(core_ref, pl.program_id(0), own_ref, got_ref)

        flat = pl.BlockSpec((rows, columns), lambda g, core: (0, 0))
        ins = [(own, flat), (got, flat)] + [(target, ANY) for target in targets]
        out = ((2, 2 * rows, columns), full, pl.BlockSpec((1, rows, columns), lambda g, core: (layer, g, 0)))
        return picked(body, core, (2,), ins, [out], "finish_down", aliases)
    rows = own.shape[0] // 2
    block = pl.BlockSpec((rows, columns), lambda g, core: (g % 2, 0))
    ins = [(own, block), (got, block)] + [(target, ANY) for target in targets]
    if kind == "up":

        def body(core_ref, own_ref, got_ref, *rest):
            rest[-1][0] = chosen(core_ref, pl.program_id(0) // 2, own_ref, got_ref)

        out = ((2, rows, 4 * columns), full, pl.BlockSpec((1, rows, columns), lambda g, core: (layer, 0, g)))
        return picked(body, core, (4,), ins, [out], "finish_up", aliases)

    def body(core_ref, own_ref, got_ref, *rest):
        qkv_ref, out_ref = rest[-2:]
        values = chosen(core_ref, pl.program_id(0) // 2, own_ref, got_ref)

        @pl.when(pl.program_id(0) < 3)
        def _():
            qkv_ref[0] = values

        @pl.when(pl.program_id(0) == 3)
        def _():
            out_ref[0] = values

    outs = [
        ((2, rows, 3 * columns), full, pl.BlockSpec((1, rows, columns), lambda g, core: (layer, 0, jnp.minimum(g, 2)))),
        ((2, rows, columns), full, pl.BlockSpec((1, rows, columns), lambda g, core: (layer, 0, 0))),
    ]
    return picked(body, core, (4,), ins, outs, "finish_qkv_out", aliases)


def after(value, *earlier):
    return lax.optimization_barrier((value,) + earlier)[0] if earlier else value


def swap(values, axis, mask):
    size = lax.axis_size(axis)
    return lax.ppermute(values, axis, [(source, source ^ mask) for source in range(size)])


def masks(axis):
    return [1 << bit for bit in range(lax.axis_size(axis).bit_length() - 1)]


class Order:
    def __init__(self):
        self.last = ()

    def run(self, function, *arrays, **named):
        held = lax.optimization_barrier(tuple(arrays) + self.last)[: len(arrays)]
        out = function(*held, **named)
        self.last = (jax.tree.leaves(out)[0],)
        return out


class Reduce:
    def __init__(self, order, kind, term, *arrays):
        self.order, self.kind = order, kind
        place = lax.axis_index("wide")
        self.core = (place & 1).astype(jnp.int32).reshape(1)
        self.sent = order.run(term, *arrays, 1 - self.core)
        self.got = swap(self.sent, "wide", 1)
        self.kept = order.run(term, *arrays, self.core)
        self.columns = self.kept.shape[-1]
        stages = [("narrow", mask) for mask in reversed(masks("narrow"))]
        stages += [("wide", mask) for mask in masks("wide")[1:]]
        self.down = list(stages)
        self.up = [stage for stage in reversed(stages) if stage[0] == "wide"]
        self.joining = None

    def bit(self, axis, mask):
        return ((lax.axis_index(axis) & mask) // mask).astype(jnp.int32).reshape(1)

    def step(self):
        if self.down:
            axis, mask = self.down.pop(0)
            shape = (2, -1, self.columns)
            kept, got = self.kept.reshape(shape), self.got.reshape(shape)
            self.sent, self.kept = self.order.run(add_halve, kept, got, self.bit(axis, mask))
            self.got = swap(self.sent, axis, mask)
            return
        if self.joining is None:
            total = self.order.run(lambda one, two: (one.astype(full) + two.astype(full)).astype(low), self.kept, self.got)
        else:
            total = self.order.run(pair_up, self.kept, self.got, self.bit(*self.joining))
            total = total.reshape(-1, self.columns)
        self.kept = total
        if self.up:
            self.joining = self.up.pop(0)
            self.got = swap(total, *self.joining)
        else:
            self.got = swap(total, "wide", 1)

    def steps_left(self):
        return len(self.down) + 1 + len([1 for _ in self.up])

    def finish(self, layer, targets=()):
        scale = 1.0 / lax.axis_size("wide")

        def last(own, got, core, *targets):
            return finish(self.kind, own, got, core, scale, layer, targets)

        return self.order.run(last, self.kept, self.got, self.core, *targets)


def sum_all(values):
    for axis in ("wide", "narrow"):
        for mask in masks(axis):
            values = values + swap(values, axis, mask)
    return values


def on_device(
    tokens,
    skip,
    flags,
    cotangent,
    norm_gains,
    norm_biases,
    qkv_weight,
    out_weight,
    out_bias,
    up_weight,
    up_bias,
    down_weight,
    down_bias,
    skip_weight,
    skip_bias,
):
    items, seq_rows, width = tokens.shape
    rows = items * seq_rows
    lengths = PATCHES + 1 + CAPTION * flags
    valid = lax.broadcasted_iota(jnp.int32, (items, seq_rows), 1) < lengths[:, None]
    keep = valid.reshape(rows, 1).astype(full)
    every = jnp.ones((rows, 1), full)
    me = lax.axis_index("narrow")
    shares = lax.axis_size("narrow")
    spots = jnp.stack([me, lax.axis_index("wide")]).astype(jnp.int32)
    order = Order()

    weights = (qkv_weight, out_weight, up_weight, down_weight)
    qkv0, out0, up0, down0 = [Weight(weight, 0, width, spots) for weight in weights]
    qkv1, out1, up1, down1 = [Weight(weight, 1, width, spots) for weight in weights]
    join = Weight(skip_weight, None, width, spots)

    small = (norm_gains, norm_biases, out_bias, up_bias, down_bias, skip_bias)
    held = jnp.concatenate([piece.reshape(-1) for piece in small])[None]
    for mask in masks("narrow"):
        held = jnp.concatenate([held, swap(held, "narrow", mask)])
    parts = [lax.dynamic_index_in_dim(held, me ^ place, 0, keepdims=False) for place in range(shares)]
    wide_small, begin = [], 0
    for piece in small:
        end = begin + piece.size
        both = [part[begin:end].reshape(piece.shape) for part in parts]
        wide_small.append(jnp.concatenate(both, axis=-1).astype(full))
        begin = end
    gains, shifts, out_biases, up_biases, down_biases, join_shift = wide_small

    def line(values):
        return values.reshape(1, -1)

    tokens_flat, skip_flat, cotangent_flat = [array.reshape(rows, width) for array in (tokens, skip, cotangent)]

    qkv0.fetch()
    out0.fetch()
    up0.fetch()
    down0.fetch()
    qkv0.share(1)
    out0.share(1)
    qkv0.share(0)
    out0.share(0)
    up0.share(1)
    a0, packed0 = order.run(lambda *x: project_qkv(*x, qkv0), tokens_flat, line(gains[0, 0]), line(shifts[0, 0]))
    down0.share(1, a0)
    up0.share(0, a0)
    join.fetch(a0)
    qkv1.fetch(a0)
    packed0 = packed0.reshape(3, items, seq_rows, width)
    mixed0, totals0 = order.run(lambda *x: attend(*x, items, seq_rows), packed0, lengths)
    down0.share(0, mixed0)
    join.share(1, mixed0)
    qkv1.share(1, mixed0)
    out1.fetch(mixed0)
    up1.fetch(mixed0)
    mixed0 = mixed0.reshape(rows, width)
    m0, second0, hidden0, slope0, middle = order.run(
        lambda x, o, ob, g, s, ub, db: feed_forward(x, o, out0, ob, g, s, up0, ub, down0, db, every),
        tokens_flat, mixed0, line(out_biases[0]), line(gains[0, 1]), line(shifts[0, 1]), line(up_biases[0]),
        line(down_biases[0]),
    )
    join.share(0, middle)
    qkv1.share(0, middle)
    out1.share(1, middle)
    up1.share(1, middle)
    down1.fetch(middle)
    entry, a1, packed1 = order.run(
        lambda m, s, jb, g, sh: join_qkv(m, s, join, jb, g, sh, qkv1),
        middle, skip_flat, line(join_shift), line(gains[1, 0]), line(shifts[1, 0]),
    )
    out1.share(0, a1)
    up1.share(0, a1)
    down1.share(1, a1)
    packed1 = packed1.reshape(3, items, seq_rows, width)
    mixed1, totals1 = order.run(lambda *x: attend(*x, items, seq_rows), packed1, lengths)
    mixed1 = mixed1.reshape(rows, width)
    down1.share(0, mixed1)
    m1, second1, hidden1, slope1, output = order.run(
        lambda x, o, ob, g, s, ub, db: feed_forward(x, o, out1, ob, g, s, up1, ub, down1, db, keep),
        entry, mixed1, line(out_biases[1]), line(gains[1, 1]), line(shifts[1, 1]), line(up_biases[1]),
        line(down_biases[1]),
    )

    dz1 = jnp.where(keep > 0, cotangent_flat, 0)
    reduce_down1 = Reduce(order, "down", down_term, hidden1, dz1)
    reduce_down1.step()
    du, dm, db, do, dz, sums1, usum1 = order.run(
        lambda y, s, m, g: feed_forward_back(y, s, down1, up1, m, g, out1, keep),
        cotangent_flat, slope1, m1, line(gains[1, 1]),
    )
    reduce_up1 = Reduce(order, "up", up_term, second1, du)
    reduce_up1.step()
    reduce_down1.step()
    dpacked = order.run(
        lambda *x: attend_back(*x, items, seq_rows), packed1, do.reshape(items, seq_rows, width), totals1, lengths
    )
    flat_packed = dpacked.reshape(3, rows, width)
    reduce_qkv1 = Reduce(order, "qkv", qkv_out_term, a1, flat_packed, mixed1, db)
    reduce_qkv1.step()
    reduce_down1.step()
    reduce_up1.step()
    dentry, dmiddle, skip_grad, sums3 = order.run(
        lambda gp, x, g, dm: project_back(gp, qkv1, x, g, dm, join), flat_packed, entry, line(gains[1, 0]), dm
    )
    reduce_join = Reduce(order, "join", join_term, middle, skip_flat, dentry)
    reduce_down1.step()
    reduce_up1.step()
    reduce_join.step()
    reduce_qkv1.step()

    dz0 = dmiddle.astype(low)
    reduce_down0 = Reduce(order, "down", down_term, hidden0, dz0)
    reduce_down0.step()
    reduce_down1.step()
    reduce_up1.step()
    reduce_qkv1.step()
    reduce_join.step()
    du, dm, db, do, dz, sums0, usum0 = order.run(
        lambda y, s, m, g: feed_forward_back(y, s, down0, up0, m, g, out0, every),
        dmiddle, slope0, m0, line(gains[0, 1]),
    )
    reduce_up0 = Reduce(order, "up", up_term, second0, du)
    reduce_up0.step()
    reduce_down1.step()
    reduce_up1.step()
    reduce_qkv1.step()
    reduce_join.step()
    reduce_down0.step()
    dpacked = order.run(
        lambda *x: attend_back(*x, items, seq_rows), packed0, do.reshape(items, seq_rows, width), totals0, lengths
    )
    flat_packed = dpacked.reshape(3, rows, width)
    reduce_qkv0 = Reduce(order, "qkv", qkv_out_term, a0, flat_packed, mixed0, db)
    reduce_qkv0.step()
    reduce_down1.step()
    reduce_up1.step()
    reduce_qkv1.step()
    reduce_join.step()
    reduce_down0.step()
    reduce_up0.step()
    tokens_grad, sums2 = order.run(
        lambda gp, x, g, dm: project_back(gp, qkv0, x, g, dm), flat_packed, tokens_flat, line(gains[0, 0]), dm
    )

    def norm_terms(place):
        return jnp.stack([jnp.stack([sums2[place], sums0[1 + place]]), jnp.stack([sums3[place], sums1[1 + place]])])

    minor = [
        norm_terms(0),
        norm_terms(1),
        jnp.stack([sums0[3], sums1[3]]),
        jnp.concatenate([usum0, usum1]),
        jnp.stack([sums0[0], sums1[0]]),
        sums3[2],
    ]
    split = [jnp.moveaxis(piece.reshape(piece.shape[:-1] + (shares, -1)), -2, 0) for piece in minor]
    packed_minor = jnp.concatenate([piece.reshape(shares, -1) for piece in split], axis=1)
    owned = lax.dynamic_index_in_dim(sum_all(packed_minor), me, 0, keepdims=False) * (1.0 / lax.axis_size("wide"))

    running = [reduce_down1, reduce_up1, reduce_qkv1, reduce_join, reduce_down0, reduce_up0, reduce_qkv0]
    done = {}
    while running:
        for each in list(running):
            if each.up or each.down or (each.joining is None):
                each.step()
            elif not getattr(each, "closed", False):
                each.step()
                each.closed = True
            else:
                running.remove(each)
                layer = 0 if each in (reduce_down0, reduce_up0, reduce_qkv0) else 1
                done[each.kind] = each.finish(layer, done.get(each.kind, ()))

    minor_sums, begin = [], 0
    for piece in split:
        end = begin + piece.size // shares
        minor_sums.append(owned[begin:end].reshape(piece.shape[1:]))
        begin = end
    return (
        output.reshape(tokens.shape),
        tokens_grad.reshape(tokens.shape),
        skip_grad.reshape(tokens.shape),
        minor_sums[0],
        minor_sums[1],
        done["qkv"][0],
        done["qkv"][1],
        minor_sums[2],
        done["up"][0],
        minor_sums[3],
        done["down"][0],
        minor_sums[4],
        done["join"][0],
        minor_sums[5],
    )


def solution(mesh):
    placed = (
        P(("wide", "narrow"), None, None),
        P(("wide", "narrow"), None, None),
        P(("wide", "narrow")),
        P(("wide", "narrow"), None, None),
        P(None, None, "narrow"),
        P(None, None, "narrow"),
        P(None, "narrow", None),
        P(None, "narrow", None),
        P(None, "narrow"),
        P(None, "narrow", None),
        P(None, "narrow"),
        P(None, "narrow", None),
        P(None, "narrow"),
        P("narrow", None),
        P("narrow"),
    )
    return jax.shard_map(
        on_device,
        mesh=mesh,
        in_specs=placed,
        out_specs=(
            P(("wide", "narrow"), None, None),
            P(("wide", "narrow"), None, None),
            P(("wide", "narrow"), None, None),
            P(None, None, "narrow"),
            P(None, None, "narrow"),
            P(None, "narrow", None),
            P(None, "narrow", None),
            P(None, "narrow"),
            P(None, "narrow", None),
            P(None, "narrow"),
            P(None, "narrow", None),
            P(None, "narrow"),
            P("narrow", None),
            P("narrow"),
        ),
        check_vma=False,
    )
```

time: 1090 us -> 721 us (0.66)
  Pallas kernels: 0 us -> 297 us
  matrix products: 237 us -> 0 us
  local copies, waits for them, and re-layouts: 250 us -> 59.9 us
  waiting for transfers between devices: 348 us -> 222 us
  other arithmetic: 84.4 us -> 9.71 us
  starting transfers between devices: 157 us -> 121 us
    pallas_call x0 -> x82, Pallas kernels: none -> 297 us  [the longest x12 199 us: call(): pl.pallas_call(body, grid=grid, in_specs=[spec for _, spec in ins], out_s...]
    dot_general x39 -> x0, matrix products: 237 us -> none  [the longest x9 75.6 us: back_dot(): lax.dot_general(left, weight, (((1,), (1,)), ((), ())), preferred_element...]
    ppermute x123 -> x105, waiting for transfers between devices: 348 us -> 222 us  [swap(): lax.ppermute(values, axis, [(source, source ^ mask) for source in range(s...]
    dynamic_update_slice x80 -> x0, local copies, waits for them, and re-layouts: 51.5 us -> none  [the longest x35 38.6 us: gather_rows(): full = lax.dynamic_update_slice_in_dim(full, piece[offset - 1], start, 0)]
    reshape x35 -> x18, local copies, waits for them, and re-layouts: 47.9 us -> 5.47 us  [the longest x5 3.5 us: on_device(): held = jnp.concatenate([piece.reshape(-1) for piece in small])[None]]
    ppermute x123 -> x105, starting transfers between devices: 157 us -> 121 us  [swap(): lax.ppermute(values, axis, [(source, source ^ mask) for source in range(s...]
    unnamed x352 -> x144, local copies, waits for them, and re-layouts: 44.1 us -> 13.2 us
    convert_element_type x11 -> x14, other arithmetic: 28.1 us -> 3.8 us  [the longest x1 1.68 us: on_device(): dz0 = dmiddle.astype(low)]
  transfers between devices with their start and end apart: 123 -> 105, of which waited for: 65 -> 49; matrix products, arithmetic and copies ran while one was open for 30% -> 7% of each run, Pallas kernels for 0% -> 20%
where the time goes in v2:
time: 721 us; the launch traced here: 712 us
  Pallas kernels  297 us (41%)
  waiting for transfers between devices  222 us (31%)
  starting transfers between devices  121 us (17%)
  local copies, waits for them, and re-layouts  59.9 us (8%)
  other arithmetic  9.71 us (1%)
    ppermute x105, waiting for transfers between devices, swap(): lax.ppermute(values, axis, [(source, source ^ mask) for source in range(s...  222 us
    pallas_call x12, Pallas kernels, call(): pl.pallas_call(body, grid=grid, in_specs=[spec for _, spec in ins], out_s...  199 us
    ppermute x105, starting transfers between devices, swap(): lax.ppermute(values, axis, [(source, source ^ mask) for source in range(s...  121 us
    pallas_call x70, Pallas kernels, picked(): pl.pallas_call(body, grid_spec=pltpu.PrefetchScalarGridSpec(num_scalar_pr...  98.5 us
  transfers between devices with their start and end apart: 105, of which 49 were waited for; matrix products, arithmetic and copies ran while one was open for 7% of the time, Pallas kernels for 20%

profile of v2, /device:TPU:1, one launch (start us, length us, event | category | flops | bytes accessed | tf_op | source)
XLA Modules:
  0.0 712.4 jit_solution(3160122049728769778)
XLA Ops:
  12.6 4.1 fusion.1
  19.0 4.1 fusion.2
  37.3 11.5 %collective-permute-done.10.refs_7_ = bf16[1,96,3072]{2,1,0:T(8,128)(2,1)S(1)} collective-permute-done((bf16[1,96,3072]{2,1,0:T(8,128)(2,1)}, bf16[1,96,3072]{2,1,0:T(8,128)(2,1)S(1)}, u32[]{:S(2)}, u32[]{:S(2)}) %collective-permute-start.10) | collective-permute-done | bytes 589856 | tf_op jit(solution)/shard_map/ppermute | solution.py:717
  50.0 3.7 collective-permute-start.2
  55.4 8.0 %collective-permute-done.7.refs_3_.refs_13_ = bf16[1,96,768]{2,1,0:T(8,128)(2,1)S(1)} collective-permute-done((bf16[1,96,768]{2,1,0:T(8,128)(2,1)S(1)}, bf16[1,96,768]{2,1,0:T(8,128)(2,1)S(1)}, u32[]{:S(2)}, u32[]{:S(2)}) %collective-permute-start.7) | collective-permute-done | bytes 147488 | tf_op jit(solution)/shard_map/ppermute | solution.py:717
  63.4 4.3 collective-permute-start.8
  68.5 6.6 project_qkv.1
  76.4 13.6 %attend.2 = (bf16[2,336,768]{2,1,0:T(8,128)(2,1)}, f32[2,6,8,336]{3,2,1,0:T(8,128)}) custom-call(s32[2]{0:T(128)} %multiply_add_fusion.length_ref, bf16[3,2,336,768]{3,2,1,0:T(8,128)(2,1)} %bitcast.242, bf16[3,2,336,768]{3,2,1,0:T(8,128)(2,1)} %bitcast.243, bf16[3,2,336,768]{3,2,1,0:T(8,128)(2,1)} %bitcast.244), custom_call_target="tpu_custom_call" | custom-call | flops 1000000 | bytes 1000000 | tf_op jit(solution)/shard_map/attend/pallas_call | solution.py:50
  94.0 8.3 %collective-permute-done.23.refs_7_.refs_2_ = bf16[1,96,2304]{2,1,0:T(8,128)(2,1)} collective-permute-done((bf16[1,96,2304]{2,1,0:T(8,128)(2,1)}, bf16[1,96,2304]{2,1,0:T(8,128)(2,1)}, u32[]{:S(2)}, u32[]{:S(2)}) %collective-permute-start.23) | collective-permute-done | bytes 442400 | tf_op jit(solution)/shard_map/ppermute | solution.py:717
  104.6 4.0 collective-permute-done.19.refs_2_.refs_7_
  111.8 25.1 %feed_forward.2 = (f32[672,768]{1,0:T(8,128)}, bf16[672,768]{1,0:T(8,128)(2,1)}, bf16[672,3072]{1,0:T(8,128)(2,1)}, bf16[672,3072]{1,0:T(8,128)(2,1)}, bf16[672,768]{1,0:T(8,128)(2,1)}) custom-call(s32[2]{0:T(128)} %pad_add_fusion.refs_0_, bf16[2,384,768]{2,1,0:T(8,128)(2,1)} %refs_11_.7, bf16[1,96,768]{2,1,0:T(8,128)(2,1)} %copy-done.48, ...), custom_call_target="tpu_custom_call" | custom-call | flops 1000000 | bytes 1000000 | tf_op jit(solution)/shard_map/feed_forward/pallas_call | solution.py:50
  144.7 11.1 %join_qkv.1 = (f32[672,768]{1,0:T(8,128)}, bf16[672,768]{1,0:T(8,128)(2,1)}, bf16[3,672,768]{2,1,0:T(8,128)(2,1)}) custom-call(s32[2]{0:T(128)} %pad_add_fusion.refs_0_, bf16[768,768]{1,0:T(8,128)(2,1)} %refs_6_.10, bf16[1,192,768]{2,1,0:T(8,128)(2,1)} %copy-done.44, bf16[1,192,768]{2,1,0:T(8,128)(2,1)} %copy-done.45, bf16[1,192,768]{2,1,0:T(8,128)(2,1)} %copy-done.47, ...), custom_call_target="tpu_custom_call" | custom-call | flops 1000000 | bytes 1000000 | tf_op jit(solution)/shard_map/join_qkv/pallas_call | solution.py:50
  158.3 4.2 collective-permute-done.5.refs_2_.refs_12_
  164.9 13.6 %attend.3 = (bf16[2,336,768]{2,1,0:T(8,128)(2,1)}, f32[2,6,8,336]{3,2,1,0:T(8,128)}) custom-call(s32[2]{0:T(128)} %multiply_add_fusion.length_ref, bf16[3,2,336,768]{3,2,1,0:T(8,128)(2,1)} %bitcast.248, bf16[3,2,336,768]{3,2,1,0:T(8,128)(2,1)} %bitcast.249, bf16[3,2,336,768]{3,2,1,0:T(8,128)(2,1)} %bitcast.250), custom_call_target="tpu_custom_call" | custom-call | flops 1000000 | bytes 1000000 | tf_op jit(solution)/shard_map/attend/pallas_call | solution.py:50
  184.9 25.3 %feed_forward.3 = (f32[672,768]{1,0:T(8,128)}, bf16[672,768]{1,0:T(8,128)(2,1)}, bf16[672,3072]{1,0:T(8,128)(2,1)}, bf16[672,3072]{1,0:T(8,128)(2,1)}, bf16[672,768]{1,0:T(8,128)(2,1)}) custom-call(s32[2]{0:T(128)} %pad_add_fusion.refs_0_, bf16[2,384,768]{2,1,0:T(8,128)(2,1)} %refs_11_.7, bf16[1,96,768]{2,1,0:T(8,128)(2,1)} %copy-done.51, ...), custom_call_target="tpu_custom_call" | custom-call | flops 1000000 | bytes 1000000 | tf_op jit(solution)/shard_map/feed_forward/pallas_call | solution.py:50
  222.3 22.7 %feed_forward_back.2 = (bf16[672,3072]{1,0:T(8,128)(2,1)}, f32[672,768]{1,0:T(8,128)}, bf16[672,768]{1,0:T(8,128)(2,1)}, bf16[672,768]{1,0:T(8,128)(2,1)}, bf16[...) custom-call(s32[2]{0:T(128)} %pad_add_fusion.refs_0_, bf16[2,1536,768]{2,1,0:T(8,128)(2,1)} %refs_1_.14, ...), custom_call_target="tpu_custom_call" | custom-call | flops 1000000 | bytes 1000000 | tf_op jit(solution)/shard_map/feed_forward_back/pallas_call | solution.py:50
  245.1 4.1 up_term.4
  256.7 20.6 %collective-permute-done.38 = bf16[768,768]{1,0:T(8,128)(2,1)} collective-permute-done((bf16[768,768]{1,0:T(8,128)(2,1)}, bf16[768,768]{1,0:T(8,128)(2,1)}, u32[]{:S(2)}, u32[]{:S(2)}) %collective-permute-start.38) | collective-permute-done | bytes 1179680 | tf_op jit(solution)/shard_map/ppermute | solution.py:717
  280.3 17.3 %attend_back.2 = bf16[3,2,336,768]{3,2,1,0:T(8,128)(2,1)} custom-call(s32[2]{0:T(128)} %multiply_add_fusion.length_ref, bf16[3,2,336,768]{3,2,1,0:T(8,128)(2,1)} %bitcast.251, bf16[3,2,336,768]{3,2,1,0:T(8,128)(2,1)} %bitcast.252, bf16[3,2,336,768]{3,2,1,0:T(8,128)(2,1)} %bitcast.253, bf16[2,336,768]{2,1,0:T(8,128)(2,1)} %bitcast.265, ...), custom_call_target="tpu_custom_call" | custom-call | flops 1000000 | bytes 1000000 | tf_op jit(solution)/shard_map/attend_back/pallas_call | solution.py:50
  297.6 4.6 qkv_out_term.4
  304.5 3.7 qkv_out_term.5
  311.2 7.1 %collective-permute-done.41 = bf16[384,768]{1,0:T(8,128)(2,1)} collective-permute-done((bf16[384,768]{1,0:T(8,128)(2,1)}, bf16[384,768]{1,0:T(8,128)(2,1)}, u32[]{:S(2)}, u32[]{:S(2)}) %collective-permute-start.41) | collective-permute-done | bytes 589856 | tf_op jit(solution)/shard_map/ppermute | solution.py:717
  320.2 10.9 %collective-permute-done.40 = bf16[768,768]{1,0:T(8,128)(2,1)} collective-permute-done((bf16[768,768]{1,0:T(8,128)(2,1)}, bf16[768,768]{1,0:T(8,128)(2,1)}, u32[]{:S(2)}, u32[]{:S(2)}) %collective-permute-start.40) | collective-permute-done | bytes 1179680 | tf_op jit(solution)/shard_map/ppermute | solution.py:717
  334.0 13.4 %project_back.2 = (bf16[672,768]{1,0:T(8,128)(2,1)}, f32[672,768]{1,0:T(8,128)}, f32[672,768]{1,0:T(8,128)}, f32[8,768]{1,0:T(8,128)}) custom-call(s32[2]{0:T(128)} %pad_add_fusion.refs_0_, bf16[2,384,2304]{2,1,0:T(8,128)(2,1)} %refs_1_.15, bf16[1,96,2304]{2,1,0:T(8,128)(2,1)} %collective-permute-done.23.refs_7_.refs_2_, bf16[1,96,2304]{2,1,0:T(8,128)(2,1)} %copy-done.41, ...), custom_call_target="tpu_custom_call" | custom-call | flops 1000000 | bytes 1000000 | tf_op jit(solution)/shard_map/project_back/pallas_call | solution.py:50
  357.7 3.9 collective-permute-done.45
  362.6 4.5 collective-permute-done.44
  369.8 10.0 %collective-permute-done.47 = bf16[768,768]{1,0:T(8,128)(2,1)} collective-permute-done((bf16[768,768]{1,0:T(8,128)(2,1)}, bf16[768,768]{1,0:T(8,128)(2,1)}, u32[]{:S(2)}, u32[]{:S(2)}) %collective-permute-start.47) | collective-permute-done | bytes 1179680 | tf_op jit(solution)/shard_map/ppermute | solution.py:717
  401.7 22.9 %feed_forward_back.3 = (bf16[672,3072]{1,0:T(8,128)(2,1)}, f32[672,768]{1,0:T(8,128)}, bf16[672,768]{1,0:T(8,128)(2,1)}, bf16[672,768]{1,0:T(8,128)(2,1)}, bf16[...) custom-call(s32[2]{0:T(128)} %pad_add_fusion.refs_0_, bf16[2,1536,768]{2,1,0:T(8,128)(2,1)} %refs_1_.14, ...), custom_call_target="tpu_custom_call" | custom-call | flops 1000000 | bytes 1000000 | tf_op jit(solution)/shard_map/feed_forward_back/pallas_call | solution.py:50
  424.7 3.9 up_term.6
  445.8 11.5 %collective-permute-done.52 = bf16[768,768]{1,0:T(8,128)(2,1)S(1)} collective-permute-done((bf16[768,768]{1,0:T(8,128)(2,1)S(1)}, bf16[768,768]{1,0:T(8,128)(2,1)S(1)}, u32[]{:S(2)}, u32[]{:S(2)}) %collective-permute-start.52) | collective-permute-done | bytes 1179680 | tf_op jit(solution)/shard_map/ppermute | solution.py:717
  457.9 17.3 %attend_back.3 = bf16[3,2,336,768]{3,2,1,0:T(8,128)(2,1)} custom-call(s32[2]{0:T(128)} %multiply_add_fusion.length_ref, bf16[3,2,336,768]{3,2,1,0:T(8,128)(2,1)} %bitcast.245, bf16[3,2,336,768]{3,2,1,0:T(8,128)(2,1)} %bitcast.246, bf16[3,2,336,768]{3,2,1,0:T(8,128)(2,1)} %bitcast.247, bf16[2,336,768]{2,1,0:T(8,128)(2,1)} %bitcast.264, ...), custom_call_target="tpu_custom_call" | custom-call | flops 1000000 | bytes 1000000 | tf_op jit(solution)/shard_map/attend_back/pallas_call | solution.py:50
  475.2 3.7 qkv_out_term.6
  481.7 3.7 qkv_out_term.7
  491.2 9.5 %collective-permute-done.62.got_ref = bf16[96,768]{1,0:T(8,128)(2,1)S(1)} collective-permute-done((bf16[96,768]{1,0:T(8,128)(2,1)S(1)}, bf16[96,768]{1,0:T(8,128)(2,1)S(1)}, u32[]{:S(2)}, u32[]{:S(2)}) %collective-permute-start.62) | collective-permute-done | bytes 147488 | tf_op jit(solution)/shard_map/ppermute | solution.py:717
  508.1 10.0 %project_back.3 = (f32[672,768]{1,0:T(8,128)}, f32[8,768]{1,0:T(8,128)}) custom-call(s32[2]{0:T(128)} %pad_add_fusion.refs_0_, bf16[2,384,2304]{2,1,0:T(8,128)(2,1)} %refs_1_.15, bf16[1,96,2304]{2,1,0:T(8,128)(2,1)} %copy-done.38, bf16[1,96,2304]{2,1,0:T(8,128)(2,1)} %copy-done.39, bf16[1,96,2304]{2,1,0:T(8,128)(2,1)} %copy-done.40, ...), custom_call_target="tpu_custom_call" | custom-call | flops 1000000 | bytes 1000000 | tf_op jit(solution)/shard_map/project_back/pallas_call | solution.py:50
  521.2 7.1 collective-permute-done.75.got_ref
  538.5 4.7 collective-permute-start.72
  543.3 4.7 collective-permute-done.72
  551.3 3.8 collective-permute-start.89
  556.0 7.7 %collective-permute-done.81.got_ref = bf16[192,768]{1,0:T(8,128)(2,1)S(1)} collective-permute-done((bf16[192,768]{1,0:T(8,128)(2,1)S(1)}, bf16[192,768]{1,0:T(8,128)(2,1)S(1)}, u32[]{:S(2)}, u32[]{:S(2)}) %collective-permute-start.81) | collective-permute-done | bytes 294944 | tf_op jit(solution)/shard_map/ppermute | solution.py:717
  566.5 9.5 %collective-permute-done.80.got_ref = bf16[96,384]{1,0:T(8,128)(2,1)S(1)} collective-permute-done((bf16[96,384]{1,0:T(8,128)(2,1)S(1)}, bf16[96,384]{1,0:T(8,128)(2,1)S(1)}, u32[]{:S(2)}, u32[]{:S(2)}) %collective-permute-start.80) | collective-permute-done | bytes 73760 | tf_op jit(solution)/shard_map/ppermute | solution.py:717
  577.6 5.8 collective-permute-done.78
  594.2 6.5 collective-permute-done.87.got_ref
  621.8 10.3 %collective-permute-done.91.got_ref = bf16[96,768]{1,0:T(8,128)(2,1)S(1)} collective-permute-done((bf16[96,768]{1,0:T(8,128)(2,1)S(1)}, bf16[96,768]{1,0:T(8,128)(2,1)S(1)}, u32[]{:S(2)}, u32[]{:S(2)}) %collective-permute-start.91) | collective-permute-done | bytes 147488 | tf_op jit(solution)/shard_map/ppermute | solution.py:717
  641.6 6.7 collective-permute-done.96.got_ref
  676.0 8.8 %collective-permute-done.66 = f32[2,8064]{1,0:T(2,128)S(1)} collective-permute-done((f32[2,8064]{1,0:T(2,128)S(1)}, f32[2,8064]{1,0:T(2,128)S(1)}, u32[]{:S(2)}, u32[]{:S(2)}) %collective-permute-start.66) | collective-permute-done | bytes 64544 | tf_op jit(solution)/shard_map/ppermute | solution.py:717
  689.7 3.8 collective-permute-start.68
  699.6 5.4 collective-permute-start.104
  (487 shorter events, 272.6 us)
Async XLA Ops:
  6.2 28.7 %collective-permute-start.4 = (bf16[1,8064]{1,0:T(2,128)(2,1)S(1)}, bf16[1,8064]{1,0:T(2,128)(2,1)S(1)}, u32[]{:S(2)}, u32[]{:S(2)}) collective-permute-start(bf16[1,8064]{1,0:T(2,128)(2,1)S(1)} %broadcast_in_dim.38), channel_id=1, source_target_pairs={{0,1},{1,0},{2,3},{3,2},{4,5},{5,4},{6,7},{7,6},{8,9},{9,8},{10,11... | collective-permute-start | bytes 48392 | tf_op jit(solution)/shard_map/ppermute | solution.py:717
  12.6 22.8 %collective-permute-start = (bf16[1,96,2304]{2,1,0:T(8,128)(2,1)}, bf16[1,96,2304]{2,1,0:T(8,128)(2,1)S(1)}, u32[]{:S(2)}, u32[]{:S(2)}) collective-permute-start(bf16[1,96,2304]{2,1,0:T(8,128)(2,1)} %constant_dynamic-slice_fusion.4), channel_id=1, source_target_pairs={{0,1},{1,0},{2,3},{3,2},{4,5},{5,4},{6,7},{7,6},{8,9},{9,8},{10,11... | collective-permute-start | bytes 1327112 | tf_op jit(solution)/shard_map/ppermute | solution.py:717
  17.5 57.6 %collective-permute-start.14 = (bf16[1,384,768]{2,1,0:T(8,128)(2,1)}, bf16[1,384,768]{2,1,0:T(8,128)(2,1)S(1)}, u32[]{:S(2)}, u32[]{:S(2)}) collective-permute-start(bf16[1,384,768]{2,1,0:T(8,128)(2,1)} %constant_dynamic-slice_fusion.1), channel_id=1, source_target_pairs={{0,1},{1,0},{2,3},{3,2},{4,5},{5,4},{6,7},{7,6},{8,9},{9,8},{10,11... | collective-permute-start | bytes 1769480 | tf_op jit(solution)/shard_map/ppermute | solution.py:717
  23.9 24.8 %collective-permute-start.10 = (bf16[1,96,3072]{2,1,0:T(8,128)(2,1)}, bf16[1,96,3072]{2,1,0:T(8,128)(2,1)S(1)}, u32[]{:S(2)}, u32[]{:S(2)}) collective-permute-start(bf16[1,96,3072]{2,1,0:T(8,128)(2,1)} %constant_dynamic-slice_fusion.2), channel_id=1, source_target_pairs={{0,1},{1,0},{2,3},{3,2},{4,5},{5,4},{6,7},{7,6},{8,9},{9,8},{10,11... | collective-permute-start | bytes 1769480 | tf_op jit(solution)/shard_map/ppermute | solution.py:717
  25.0 29.5 %collective-permute-start.6 = (bf16[1,96,768]{2,1,0:T(8,128)(2,1)S(1)}, bf16[1,96,768]{2,1,0:T(8,128)(2,1)S(1)}, u32[]{:S(2)}, u32[]{:S(2)}) collective-permute-start(bf16[1,96,768]{2,1,0:T(8,128)(2,1)S(1)} %constant_dynamic-slice_fusion.3), channel_id=1, source_target_pairs={{0,1},{1,0},{2,3},{3,2},{4,5},{5,4},{6,7},{7,6},{8,9},{9,8},{10,11... | collective-permute-start | bytes 442376 | tf_op jit(solution)/shard_map/ppermute | solution.py:717
  35.3 18.3 %collective-permute-start.1 = (bf16[1,96,2304]{2,1,0:T(8,128)(2,1)S(1)}, bf16[1,96,2304]{2,1,0:T(8,128)(2,1)S(1)}, u32[]{:S(2)}, u32[]{:S(2)}) collective-permute-start(bf16[1,96,2304]{2,1,0:T(8,128)(2,1)S(1)} %collective-permute-done.refs_2_), channel_id=1, source_target_pairs={{0,4},{2,6},{4,0},{6,2},{8,12},{10,14},{12,8},{14,10},{16,20},{18,... | collective-permute-start | bytes 1327112 | tf_op jit(solution)/shard_map/ppermute | solution.py:717
  48.8 41.7 %collective-permute-start.11 = (bf16[1,96,3072]{2,1,0:T(8,128)(2,1)S(1)}, bf16[1,96,3072]{2,1,0:T(8,128)(2,1)S(1)}, u32[]{:S(2)}, u32[]{:S(2)}) collective-permute-start(bf16[1,96,3072]{2,1,0:T(8,128)(2,1)S(1)} %collective-permute-done.10.refs_7_), channel_id=1, source_target_pairs={{0,4},{2,6},{4,0},{6,2},{8,12},{10,14},{12,8},{14,10},{16,20},{18,... | collective-permute-start | bytes 1769480 | tf_op jit(solution)/shard_map/ppermute | solution.py:717
  50.0 17.7 %collective-permute-start.2 = (bf16[1,96,2304]{2,1,0:T(8,128)(2,1)S(1)}, bf16[1,96,2304]{2,1,0:T(8,128)(2,1)S(1)}, u32[]{:S(2)}, u32[]{:S(2)}) collective-permute-start(bf16[1,96,2304]{2,1,0:T(8,128)(2,1)S(1)} %collective-permute-done.refs_2_), channel_id=1, source_target_pairs={{0,2},{2,0},{4,6},{6,4},{8,10},{10,8},{12,14},{14,12},{16,18},{18,... | collective-permute-start | bytes 1327112 | tf_op jit(solution)/shard_map/ppermute | solution.py:717
  63.4 29.3 %collective-permute-start.8 = (bf16[1,96,768]{2,1,0:T(8,128)(2,1)S(1)}, bf16[1,96,768]{2,1,0:T(8,128)(2,1)}, u32[]{:S(2)}, u32[]{:S(2)}) collective-permute-start(bf16[1,96,768]{2,1,0:T(8,128)(2,1)S(1)} %collective-permute-done.6.refs_2_.refs_12_), channel_id=1, source_target_pairs={{0,2},{2,0},{4,6},{6,4},{8,10},{10,8},{12,14},{14,12},{16,18},{18,... | collective-permute-start | bytes 442376 | tf_op jit(solution)/shard_map/ppermute | solution.py:717
  67.7 25.1 %collective-permute-start.9 = (bf16[1,96,768]{2,1,0:T(8,128)(2,1)S(1)}, bf16[1,96,768]{2,1,0:T(8,128)(2,1)}, u32[]{:S(2)}, u32[]{:S(2)}) collective-permute-start(bf16[1,96,768]{2,1,0:T(8,128)(2,1)S(1)} %collective-permute-done.7.refs_3_.refs_13_), channel_id=1, source_target_pairs={{0,2},{2,0},{4,6},{6,4},{8,10},{10,8},{12,14},{14,12},{16,18},{18,... | collective-permute-start | bytes 442376 | tf_op jit(solution)/shard_map/ppermute | solution.py:717
  75.1 17.0 %collective-permute-start.15 = (bf16[1,384,768]{2,1,0:T(8,128)(2,1)S(1)}, bf16[1,384,768]{2,1,0:T(8,128)(2,1)S(1)}, u32[]{:S(2)}, u32[]{:S(2)}) collective-permute-start(bf16[1,384,768]{2,1,0:T(8,128)(2,1)S(1)} %collective-permute-done.14.refs_12_.refs_2_), channel_id=1, source_target_pairs={{0,4},{2,6},{4,0},{6,2},{8,12},{10,14},{12,8},{14,10},{16,20},{18,... | collective-permute-start | bytes 1769480 | tf_op jit(solution)/shard_map/ppermute | solution.py:717
  90.1 18.8 %collective-permute-start.16 = (bf16[1,384,768]{2,1,0:T(8,128)(2,1)S(1)}, bf16[1,384,768]{2,1,0:T(8,128)(2,1)S(1)}, u32[]{:S(2)}, u32[]{:S(2)}) collective-permute-start(bf16[1,384,768]{2,1,0:T(8,128)(2,1)S(1)} %collective-permute-done.14.refs_12_.refs_2_), channel_id=1, source_target_pairs={{0,2},{2,0},{4,6},{6,4},{8,10},{10,8},{12,14},{14,12},{16,18},{18,... | collective-permute-start | bytes 1769480 | tf_op jit(solution)/shard_map/ppermute | solution.py:717
  92.2 17.6 %collective-permute-start.13 = (bf16[1,96,3072]{2,1,0:T(8,128)(2,1)S(1)}, bf16[1,96,3072]{2,1,0:T(8,128)(2,1)}, u32[]{:S(2)}, u32[]{:S(2)}) collective-permute-start(bf16[1,96,3072]{2,1,0:T(8,128)(2,1)S(1)} %collective-permute-done.11.refs_8_), channel_id=1, source_target_pairs={{0,2},{2,0},{4,6},{6,4},{8,10},{10,8},{12,14},{14,12},{16,18},{18,... | collective-permute-start | bytes 1769480 | tf_op jit(solution)/shard_map/ppermute | solution.py:717
  92.7 18.2 %collective-permute-start.12 = (bf16[1,96,3072]{2,1,0:T(8,128)(2,1)S(1)}, bf16[1,96,3072]{2,1,0:T(8,128)(2,1)}, u32[]{:S(2)}, u32[]{:S(2)}) collective-permute-start(bf16[1,96,3072]{2,1,0:T(8,128)(2,1)S(1)} %collective-permute-done.10.refs_7_), channel_id=1, source_target_pairs={{0,2},{2,0},{4,6},{6,4},{8,10},{10,8},{12,14},{14,12},{16,18},{18,... | collective-permute-start | bytes 1769480 | tf_op jit(solution)/shard_map/ppermute | solution.py:717
  92.8 15.8 %collective-permute-start.19 = (bf16[1,192,768]{2,1,0:T(8,128)(2,1)}, bf16[1,192,768]{2,1,0:T(8,128)(2,1)S(1)}, u32[]{:S(2)}, u32[]{:S(2)}) collective-permute-start(bf16[1,192,768]{2,1,0:T(8,128)(2,1)} %bitcast.268), channel_id=1, source_target_pairs={{0,1},{1,0},{2,3},{3,2},{4,5},{5,4},{6,7},{7,6},{8,9},{9,8},{10,11... | collective-permute-start | bytes 884744 | tf_op jit(solution)/shard_map/ppermute | solution.py:717
  108.6 32.2 %collective-permute-start.29 = (bf16[1,96,3072]{2,1,0:T(8,128)(2,1)}, bf16[1,96,3072]{2,1,0:T(8,128)(2,1)}, u32[]{:S(2)}, u32[]{:S(2)}) collective-permute-start(bf16[1,96,3072]{2,1,0:T(8,128)(2,1)} %bitcast.267), channel_id=1, source_target_pairs={{0,1},{1,0},{2,3},{3,2},{4,5},{5,4},{6,7},{7,6},{8,9},{9,8},{10,11... | collective-permute-start | bytes 1769480 | tf_op jit(solution)/shard_map/ppermute | solution.py:717
  108.9 29.2 %collective-permute-start.24 = (bf16[1,96,2304]{2,1,0:T(8,128)(2,1)}, bf16[1,96,2304]{2,1,0:T(8,128)(2,1)S(1)}, u32[]{:S(2)}, u32[]{:S(2)}) collective-permute-start(bf16[1,96,2304]{2,1,0:T(8,128)(2,1)} %collective-permute-done.23.refs_7_.refs_2_), channel_id=1, source_target_pairs={{0,4},{2,6},{4,0},{6,2},{8,12},{10,14},{12,8},{14,10},{16,20},{18,... | collective-permute-start | bytes 1327112 | tf_op jit(solution)/shard_map/ppermute | solution.py:717
  109.8 30.5 %collective-permute-start.20 = (bf16[1,192,768]{2,1,0:T(8,128)(2,1)S(1)}, bf16[1,192,768]{2,1,0:T(8,128)(2,1)S(1)}, u32[]{:S(2)}, u32[]{:S(2)}) collective-permute-start(bf16[1,192,768]{2,1,0:T(8,128)(2,1)S(1)} %collective-permute-done.19.refs_2_.refs_7_), channel_id=1, source_target_pairs={{0,4},{2,6},{4,0},{6,2},{8,12},{10,14},{12,8},{14,10},{16,20},{18,... | collective-permute-start | bytes 884744 | tf_op jit(solution)/shard_map/ppermute | solution.py:717
  136.9 19.0 %collective-permute-start.33 = (bf16[1,384,768]{2,1,0:T(8,128)(2,1)S(1)}, bf16[1,384,768]{2,1,0:T(8,128)(2,1)S(1)}, u32[]{:S(2)}, u32[]{:S(2)}) collective-permute-start(bf16[1,384,768]{2,1,0:T(8,128)(2,1)S(1)} %bitcast.266), channel_id=1, source_target_pairs={{0,1},{1,0},{2,3},{3,2},{4,5},{5,4},{6,7},{7,6},{8,9},{9,8},{10,11... | collective-permute-start | bytes 1769480 | tf_op jit(solution)/shard_map/ppermute | solution.py:717
  142.8 35.9 %collective-permute-start.30 = (bf16[1,96,3072]{2,1,0:T(8,128)(2,1)}, bf16[1,96,3072]{2,1,0:T(8,128)(2,1)S(1)}, u32[]{:S(2)}, u32[]{:S(2)}) collective-permute-start(bf16[1,96,3072]{2,1,0:T(8,128)(2,1)} %collective-permute-done.29.refs_7_), channel_id=1, source_target_pairs={{0,4},{2,6},{4,0},{6,2},{8,12},{10,14},{12,8},{14,10},{16,20},{18,... | collective-permute-start | bytes 1769480 | tf_op jit(solution)/shard_map/ppermute | solution.py:717
  155.8 23.3 %collective-permute-start.34 = (bf16[1,384,768]{2,1,0:T(8,128)(2,1)S(1)}, bf16[1,384,768]{2,1,0:T(8,128)(2,1)}, u32[]{:S(2)}, u32[]{:S(2)}) collective-permute-start(bf16[1,384,768]{2,1,0:T(8,128)(2,1)S(1)} %collective-permute-done.33.refs_12_.refs_2_), channel_id=1, source_target_pairs={{0,4},{2,6},{4,0},{6,2},{8,12},{10,14},{12,8},{14,10},{16,20},{18,... | collective-permute-start | bytes 1769480 | tf_op jit(solution)/shard_map/ppermute | solution.py:717
  162.5 16.7 %collective-permute-start.18 = (bf16[1,96,768]{2,1,0:T(8,128)(2,1)S(1)}, bf16[1,96,768]{2,1,0:T(8,128)(2,1)S(1)}, u32[]{:S(2)}, u32[]{:S(2)}) collective-permute-start(bf16[1,96,768]{2,1,0:T(8,128)(2,1)S(1)} %collective-permute-done.5.refs_2_.refs_12_), channel_id=1, source_target_pairs={{0,4},{2,6},{4,0},{6,2},{8,12},{10,14},{12,8},{14,10},{16,20},{18,... | collective-permute-start | bytes 442376 | tf_op jit(solution)/shard_map/ppermute | solution.py:717
  163.0 21.3 %collective-permute-start.31 = (bf16[1,96,3072]{2,1,0:T(8,128)(2,1)}, bf16[1,96,3072]{2,1,0:T(8,128)(2,1)}, u32[]{:S(2)}, u32[]{:S(2)}) collective-permute-start(bf16[1,96,3072]{2,1,0:T(8,128)(2,1)} %collective-permute-done.29.refs_7_), channel_id=1, source_target_pairs={{0,2},{2,0},{4,6},{6,4},{8,10},{10,8},{12,14},{14,12},{16,18},{18,... | collective-permute-start | bytes 1769480 | tf_op jit(solution)/shard_map/ppermute | solution.py:717
  249.6 27.7 %collective-permute-start.38 = (bf16[768,768]{1,0:T(8,128)(2,1)}, bf16[768,768]{1,0:T(8,128)(2,1)}, u32[]{:S(2)}, u32[]{:S(2)}) collective-permute-start(bf16[768,768]{1,0:T(8,128)(2,1)} %get-tuple-element.497), channel_id=1, source_target_pairs={{0,1},{1,0},{2,3},{3,2},{4,5},{5,4},{6,7},{7,6},{8,9},{9,8},{10,11... | collective-permute-start | bytes 3538952 | tf_op jit(solution)/shard_map/ppermute | solution.py:717
  303.1 27.9 %collective-permute-start.40 = (bf16[768,768]{1,0:T(8,128)(2,1)}, bf16[768,768]{1,0:T(8,128)(2,1)}, u32[]{:S(2)}, u32[]{:S(2)}) collective-permute-start(bf16[768,768]{1,0:T(8,128)(2,1)} %get-tuple-element.516), channel_id=1, source_target_pairs={{0,1},{1,0},{2,3},{3,2},{4,5},{5,4},{6,7},{7,6},{8,9},{9,8},{10,11... | collective-permute-start | bytes 3538952 | tf_op jit(solution)/shard_map/ppermute | solution.py:717
  303.4 15.0 %collective-permute-start.41 = (bf16[384,768]{1,0:T(8,128)(2,1)}, bf16[384,768]{1,0:T(8,128)(2,1)}, u32[]{:S(2)}, u32[]{:S(2)}) collective-permute-start(bf16[384,768]{1,0:T(8,128)(2,1)} %get-tuple-element.520), channel_id=1, source_target_pairs={{0,4},{2,6},{4,0},{6,2},{8,12},{10,14},{12,8},{14,10},{16,20},{18,... | collective-permute-start | bytes 1769480 | tf_op jit(solution)/shard_map/ppermute | solution.py:717
  351.1 17.2 %collective-permute-start.43 = (bf16[2,768,384]{2,1,0:T(8,128)(2,1)}, bf16[2,768,384]{2,1,0:T(8,128)(2,1)}, u32[]{:S(2)}, u32[]{:S(2)}) collective-permute-start(bf16[2,768,384]{2,1,0:T(8,128)(2,1)} %bitcast.45), channel_id=1, source_target_pairs={{0,2},{2,0},{4,6},{6,4},{8,10},{10,8},{12,14},{14,12},{16,18},{18,... | collective-permute-start | bytes 3538952 | tf_op jit(solution)/shard_map/ppermute | solution.py:717
  351.9 27.9 %collective-permute-start.47 = (bf16[768,768]{1,0:T(8,128)(2,1)}, bf16[768,768]{1,0:T(8,128)(2,1)}, u32[]{:S(2)}, u32[]{:S(2)}) collective-permute-start(bf16[768,768]{1,0:T(8,128)(2,1)} %get-tuple-element.542), channel_id=1, source_target_pairs={{0,1},{1,0},{2,3},{3,2},{4,5},{5,4},{6,7},{7,6},{8,9},{9,8},{10,11... | collective-permute-start | bytes 3538952 | tf_op jit(solution)/shard_map/ppermute | solution.py:717
  352.1 15.0 %collective-permute-start.44 = (bf16[384,768]{1,0:T(8,128)(2,1)}, bf16[384,768]{1,0:T(8,128)(2,1)}, u32[]{:S(2)}, u32[]{:S(2)}) collective-permute-start(bf16[384,768]{1,0:T(8,128)(2,1)} %get-tuple-element.550), channel_id=1, source_target_pairs={{0,4},{2,6},{4,0},{6,2},{8,12},{10,14},{12,8},{14,10},{16,20},{18,... | collective-permute-start | bytes 1769480 | tf_op jit(solution)/shard_map/ppermute | solution.py:717
  385.7 14.9 %collective-permute-start.48 = (bf16[384,768]{1,0:T(8,128)(2,1)S(1)}, bf16[384,768]{1,0:T(8,128)(2,1)S(1)}, u32[]{:S(2)}, u32[]{:S(2)}) collective-permute-start(bf16[384,768]{1,0:T(8,128)(2,1)S(1)} %get-tuple-element.586), channel_id=1, source_target_pairs={{0,4},{2,6},{4,0},{6,2},{8,12},{10,14},{12,8},{14,10},{16,20},{18,... | collective-permute-start | bytes 1769480 | tf_op jit(solution)/shard_map/ppermute | solution.py:717
  429.8 27.5 %collective-permute-start.52 = (bf16[768,768]{1,0:T(8,128)(2,1)S(1)}, bf16[768,768]{1,0:T(8,128)(2,1)S(1)}, u32[]{:S(2)}, u32[]{:S(2)}) collective-permute-start(bf16[768,768]{1,0:T(8,128)(2,1)S(1)} %get-tuple-element.599), channel_id=1, source_target_pairs={{0,1},{1,0},{2,3},{3,2},{4,5},{5,4},{6,7},{7,6},{8,9},{9,8},{10,11... | collective-permute-start | bytes 3538952 | tf_op jit(solution)/shard_map/ppermute | solution.py:717
  479.8 27.8 %collective-permute-start.58 = (bf16[768,768]{1,0:T(8,128)(2,1)}, bf16[768,768]{1,0:T(8,128)(2,1)S(1)}, u32[]{:S(2)}, u32[]{:S(2)}) collective-permute-start(bf16[768,768]{1,0:T(8,128)(2,1)} %get-tuple-element.635), channel_id=1, source_target_pairs={{0,1},{1,0},{2,3},{3,2},{4,5},{5,4},{6,7},{7,6},{8,9},{9,8},{10,11... | collective-permute-start | bytes 3538952 | tf_op jit(solution)/shard_map/ppermute | solution.py:717
  481.4 25.3 %collective-permute-start.59 = (bf16[384,768]{1,0:T(8,128)(2,1)S(1)}, bf16[384,768]{1,0:T(8,128)(2,1)S(1)}, u32[]{:S(2)}, u32[]{:S(2)}) collective-permute-start(bf16[384,768]{1,0:T(8,128)(2,1)S(1)} %get-tuple-element.652), channel_id=1, source_target_pairs={{0,4},{2,6},{4,0},{6,2},{8,12},{10,14},{12,8},{14,10},{16,20},{18,... | collective-permute-start | bytes 1769480 | tf_op jit(solution)/shard_map/ppermute | solution.py:717
  488.4 29.7 %collective-permute-start.76 = (bf16[384,768]{1,0:T(8,128)(2,1)S(1)}, bf16[384,768]{1,0:T(8,128)(2,1)S(1)}, u32[]{:S(2)}, u32[]{:S(2)}) collective-permute-start(bf16[384,768]{1,0:T(8,128)(2,1)S(1)} %bitcast.171), channel_id=1, source_target_pairs={{0,4},{2,6},{4,0},{6,2},{8,12},{10,14},{12,8},{14,10},{16,20},{18,... | collective-permute-start | bytes 1769480 | tf_op jit(solution)/shard_map/ppermute | solution.py:717
  503.9 44.4 %collective-permute-start.70 = (bf16[768,768]{1,0:T(8,128)(2,1)S(1)}, bf16[768,768]{1,0:T(8,128)(2,1)S(1)}, u32[]{:S(2)}, u32[]{:S(2)}) collective-permute-start(bf16[768,768]{1,0:T(8,128)(2,1)S(1)} %get-tuple-element.676), channel_id=1, source_target_pairs={{0,1},{1,0},{2,3},{3,2},{4,5},{5,4},{6,7},{7,6},{8,9},{9,8},{10,11... | collective-permute-start | bytes 3538952 | tf_op jit(solution)/shard_map/ppermute | solution.py:717
  518.2 30.6 %collective-permute-start.83 = (bf16[768,768]{1,0:T(8,128)(2,1)S(1)}, bf16[768,768]{1,0:T(8,128)(2,1)S(1)}, u32[]{:S(2)}, u32[]{:S(2)}) collective-permute-start(bf16[768,768]{1,0:T(8,128)(2,1)S(1)} %bitcast.160), channel_id=1, source_target_pairs={{0,2},{2,0},{4,6},{6,4},{8,10},{10,8},{12,14},{14,12},{16,18},{18,... | collective-permute-start | bytes 3538952 | tf_op jit(solution)/shard_map/ppermute | solution.py:717
  520.9 27.2 %collective-permute-start.71 = (bf16[384,768]{1,0:T(8,128)(2,1)S(1)}, bf16[384,768]{1,0:T(8,128)(2,1)S(1)}, u32[]{:S(2)}, u32[]{:S(2)}) collective-permute-start(bf16[384,768]{1,0:T(8,128)(2,1)S(1)} %get-tuple-element.696), channel_id=1, source_target_pairs={{0,4},{2,6},{4,0},{6,2},{8,12},{10,14},{12,8},{14,10},{16,20},{18,... | collective-permute-start | bytes 1769480 | tf_op jit(solution)/shard_map/ppermute | solution.py:717
  528.3 22.9 %collective-permute-start.82 = (bf16[384,768]{1,0:T(8,128)(2,1)S(1)}, bf16[384,768]{1,0:T(8,128)(2,1)S(1)}, u32[]{:S(2)}, u32[]{:S(2)}) collective-permute-start(bf16[384,768]{1,0:T(8,128)(2,1)S(1)} %bitcast.173), channel_id=1, source_target_pairs={{0,4},{2,6},{4,0},{6,2},{8,12},{10,14},{12,8},{14,10},{16,20},{18,... | collective-permute-start | bytes 1769480 | tf_op jit(solution)/shard_map/ppermute | solution.py:717
  551.3 32.3 %collective-permute-start.89 = (bf16[768,768]{1,0:T(8,128)(2,1)S(1)}, bf16[768,768]{1,0:T(8,128)(2,1)S(1)}, u32[]{:S(2)}, u32[]{:S(2)}) collective-permute-start(bf16[768,768]{1,0:T(8,128)(2,1)S(1)} %bitcast.164), channel_id=1, source_target_pairs={{0,2},{2,0},{4,6},{6,4},{8,10},{10,8},{12,14},{14,12},{16,18},{18,... | collective-permute-start | bytes 3538952 | tf_op jit(solution)/shard_map/ppermute | solution.py:717
  556.0 27.4 %collective-permute-start.77 = (bf16[384,768]{1,0:T(8,128)(2,1)S(1)}, bf16[384,768]{1,0:T(8,128)(2,1)S(1)}, u32[]{:S(2)}, u32[]{:S(2)}) collective-permute-start(bf16[384,768]{1,0:T(8,128)(2,1)S(1)} %get-tuple-element.736), channel_id=1, source_target_pairs={{0,4},{2,6},{4,0},{6,2},{8,12},{10,14},{12,8},{14,10},{16,20},{18,... | collective-permute-start | bytes 1769480 | tf_op jit(solution)/shard_map/ppermute | solution.py:717
  563.7 22.6 %collective-permute-start.88 = (bf16[384,768]{1,0:T(8,128)(2,1)S(1)}, bf16[384,768]{1,0:T(8,128)(2,1)S(1)}, u32[]{:S(2)}, u32[]{:S(2)}) collective-permute-start(bf16[384,768]{1,0:T(8,128)(2,1)S(1)} %bitcast.177), channel_id=1, source_target_pairs={{0,4},{2,6},{4,0},{6,2},{8,12},{10,14},{12,8},{14,10},{16,20},{18,... | collective-permute-start | bytes 1769480 | tf_op jit(solution)/shard_map/ppermute | solution.py:717
  586.4 21.8 %collective-permute-start.94 = (bf16[768,768]{1,0:T(8,128)(2,1)S(1)}, bf16[768,768]{1,0:T(8,128)(2,1)S(1)}, u32[]{:S(2)}, u32[]{:S(2)}) collective-permute-start(bf16[768,768]{1,0:T(8,128)(2,1)S(1)} %bitcast.168), channel_id=1, source_target_pairs={{0,2},{2,0},{4,6},{6,4},{8,10},{10,8},{12,14},{14,12},{16,18},{18,... | collective-permute-start | bytes 3538952 | tf_op jit(solution)/shard_map/ppermute | solution.py:717
  614.4 21.5 %collective-permute-start.98 = (bf16[768,384]{1,0:T(8,128)(2,1)S(1)}, bf16[768,384]{1,0:T(8,128)(2,1)S(1)}, u32[]{:S(2)}, u32[]{:S(2)}) collective-permute-start(bf16[768,384]{1,0:T(8,128)(2,1)S(1)} %bitcast.188), channel_id=1, source_target_pairs={{0,2},{2,0},{4,6},{6,4},{8,10},{10,8},{12,14},{14,12},{16,18},{18,... | collective-permute-start | bytes 1769480 | tf_op jit(solution)/shard_map/ppermute | solution.py:717
  615.8 21.8 %collective-permute-start.97 = (bf16[384,768]{1,0:T(8,128)(2,1)S(1)}, bf16[384,768]{1,0:T(8,128)(2,1)S(1)}, u32[]{:S(2)}, u32[]{:S(2)}) collective-permute-start(bf16[384,768]{1,0:T(8,128)(2,1)S(1)} %bitcast.179), channel_id=1, source_target_pairs={{0,4},{2,6},{4,0},{6,2},{8,12},{10,14},{12,8},{14,10},{16,20},{18,... | collective-permute-start | bytes 1769480 | tf_op jit(solution)/shard_map/ppermute | solution.py:717
  637.6 27.2 %collective-permute-start.101 = (bf16[768,768]{1,0:T(8,128)(2,1)S(1)}, bf16[768,768]{1,0:T(8,128)(2,1)S(1)}, u32[]{:S(2)}, u32[]{:S(2)}) collective-permute-start(bf16[768,768]{1,0:T(8,128)(2,1)S(1)} %bitcast.158), channel_id=1, source_target_pairs={{0,2},{2,0},{4,6},{6,4},{8,10},{10,8},{12,14},{14,12},{16,18},{18,... | collective-permute-start | bytes 3538952 | tf_op jit(solution)/shard_map/ppermute | solution.py:717
  648.4 18.8 %collective-permute-start.100 = (bf16[384,768]{1,0:T(8,128)(2,1)S(1)}, bf16[384,768]{1,0:T(8,128)(2,1)S(1)}, u32[]{:S(2)}, u32[]{:S(2)}) collective-permute-start(bf16[384,768]{1,0:T(8,128)(2,1)S(1)} %bitcast.181), channel_id=1, source_target_pairs={{0,4},{2,6},{4,0},{6,2},{8,12},{10,14},{12,8},{14,10},{16,20},{18,... | collective-permute-start | bytes 1769480 | tf_op jit(solution)/shard_map/ppermute | solution.py:717
  667.3 29.5 %collective-permute-start.103 = (bf16[768,768]{1,0:T(8,128)(2,1)S(1)}, bf16[768,768]{1,0:T(8,128)(2,1)S(1)}, u32[]{:S(2)}, u32[]{:S(2)}) collective-permute-start(bf16[768,768]{1,0:T(8,128)(2,1)S(1)} %bitcast.162), channel_id=1, source_target_pairs={{0,2},{2,0},{4,6},{6,4},{8,10},{10,8},{12,14},{14,12},{16,18},{18,... | collective-permute-start | bytes 3538952 | tf_op jit(solution)/shard_map/ppermute | solution.py:717
  670.8 28.7 %collective-permute-start.102 = (bf16[384,768]{1,0:T(8,128)(2,1)S(1)}, bf16[384,768]{1,0:T(8,128)(2,1)S(1)}, u32[]{:S(2)}, u32[]{:S(2)}) collective-permute-start(bf16[384,768]{1,0:T(8,128)(2,1)S(1)} %bitcast.175), channel_id=1, source_target_pairs={{0,4},{2,6},{4,0},{6,2},{8,12},{10,14},{12,8},{14,10},{16,20},{18,... | collective-permute-start | bytes 1769480 | tf_op jit(solution)/shard_map/ppermute | solution.py:717
  (124 other events, 1364.1 us)

commit v3 on v2

--- a/solution.py
+++ b/solution.py
@@ -46,7 +46,11 @@
     return pl.BlockSpec(shape, lambda *grid: (0,) * len(shape))
 
 
-def call(body, grid, ins, outs, name, scratch=(), aliases=None, limit=56):
+def cost(micros):
+    return pl.CostEstimate(flops=int(micros * 10**9), bytes_accessed=10**5, transcendentals=0)
+
+
+def call(body, grid, ins, outs, name, micros, scratch=(), limit=56):
     return pl.pallas_call(
         body,
         grid=grid,
@@ -55,8 +59,7 @@
         out_shape=[jax.ShapeDtypeStruct(shape, kind) for shape, kind, _ in outs],
         scratch_shapes=list(scratch),
         name=name,
-        input_output_aliases=aliases or {},
-        cost_estimate=pl.CostEstimate(flops=10**6, bytes_accessed=10**6, transcendentals=0),
+        cost_estimate=cost(micros),
         compiler_params=pltpu.CompilerParams(vmem_limit_bytes=limit * 2**20),
     )(*[array for array, _ in ins])
 
@@ -64,8 +67,7 @@
 class Weight:
     def __init__(self, array, layer, width, spots):
         self.array, self.layer, self.width, self.spots = array, layer, width, spots
-        shard = array if layer is None else array[layer]
-        self.rows, self.columns = shard.shape
+        self.rows, self.columns = array.shape[-2:]
         self.shares = lax.axis_size("narrow")
         self.blocks = self.columns // width
         self.total = self.rows * self.shares
@@ -74,11 +76,14 @@
             self.sharing.pop()
         self.count = 1 << len(self.sharing)
         self.length = self.rows // self.count
-        place = lax.axis_index("wide") & (self.count - 1)
-        self.piece = lax.dynamic_slice_in_dim(shard, place * self.length, self.length)
 
     def fetch(self, *earlier):
-        held = after(self.piece, *earlier)[None]
+        array = after(self.array, *earlier)
+        place = (lax.axis_index("wide") & (self.count - 1)) * self.length
+        lead = () if self.layer is None else (self.layer,)
+        sizes = (1,) * len(lead) + (self.length, self.columns)
+        self.sent = lax.dynamic_slice(array, lead + (place, 0), sizes).reshape(1, self.length, self.columns)
+        held = self.sent
         for mask in masks("narrow"):
             held = jnp.concatenate([held, swap(held, "narrow", mask)])
         self.pieces = {0: held[1:]}
@@ -122,7 +127,7 @@
             copy.wait()
 
 
-def weighted(body, weights, grid, ins, outs, name, scratch=()):
+def weighted(body, weights, grid, ins, outs, name, micros, scratch=()):
     spots = weights[0].spots
     operands = [(spots, SCALARS)] + [(array, ANY) for weight in weights for array in weight.arrays()]
     counts = [len(weight.arrays()) for weight in weights]
@@ -153,7 +158,7 @@
 
         body(ready, [held for _, _, held in handles], *rest)
 
-    return call(wrapped, grid, operands + ins, outs, name, list(scratch) + extra)
+    return call(wrapped, grid, operands + ins, outs, name, micros, list(scratch) + extra)
 
 
 def project_qkv(inputs, gain, shift, weight):
@@ -185,6 +190,7 @@
             ((3, rows, width), low, pl.BlockSpec((1, rows, width), lambda j: (j, 0, 0))),
         ],
         "project_qkv",
+        7,
     )
 
 
@@ -223,6 +229,7 @@
             ((3, rows, width), low, pl.BlockSpec((1, rows, width), lambda j: (j, 0, 0))),
         ],
         "join_qkv",
+        11,
     )
 
 
@@ -268,6 +275,7 @@
             ((items, pairs, 8, seq_rows), full, pl.BlockSpec((1, 1, 8, seq_rows), lambda n, h: (n, h, 0, 0))),
         ],
         "attend",
+        13,
     )
 
 
@@ -316,6 +324,7 @@
             ((3, items, seq_rows, width), low, pl.BlockSpec((3, 1, seq_rows, PAIR), lambda n, h: (0, n, 0, h))),
         ],
         "attend_back",
+        17,
     )[0]
 
 
@@ -330,12 +339,13 @@
     return before * share, share + before * decay * 0.3989422804014327
 
 
-def feed_forward(inputs, mixed, out_weight, out_bias, gain, shift, up_weight, up_bias, down_weight, down_bias, keep):
+def feed_forward(inputs, mixed, out_weight, out_bias, gain, shift, up_weight, up_bias, down_weight, down_bias, keep=None):
     rows, width = inputs.shape
     steps = up_weight.blocks
     hidden = steps * width
 
-    def body(ready, held, x_ref, o_ref, ob_ref, gain_ref, shift_ref, ub_ref, db_ref, keep_ref, m_ref, a_ref, g_ref, s_ref, y_ref, total):
+    def body(ready, held, x_ref, o_ref, ob_ref, gain_ref, shift_ref, ub_ref, db_ref, *rest):
+        m_ref, a_ref, g_ref, s_ref, y_ref, total = rest[-6:]
         step = pl.program_id(0)
 
         @pl.when(step == 0)
@@ -361,7 +371,10 @@
 
         @pl.when(step == steps - 1)
         def _():
-            y_ref[...] = jnp.where(keep_ref[...] > 0, total[...], 0.0).astype(low)
+            value = total[...]
+            if keep is not None:
+                value = jnp.where(rest[0][...] > 0, value, 0.0)
+            y_ref[...] = value.astype(low)
 
     return weighted(
         body,
@@ -375,8 +388,8 @@
             (shift, whole((1, width))),
             (up_bias, pl.BlockSpec((1, width), lambda j: (0, j))),
             (down_bias, whole((1, width))),
-            (keep, whole((rows, 1))),
-        ],
+        ]
+        + ([] if keep is None else [(keep, whole((rows, 1)))]),
         [
             ((rows, width), full, whole((rows, width))),
             ((rows, width), low, whole((rows, width))),
@@ -385,23 +398,22 @@
             ((rows, width), low, whole((rows, width))),
         ],
         "feed_forward",
+        23,
         scratch=[pltpu.VMEM((rows, width), full)],
     )
 
 
-def feed_forward_back(upstream, slope, down_weight, up_weight, middle, gain, out_weight, keep):
+def feed_forward_back(upstream, rounded, slope, down_weight, up_weight, middle, gain, out_weight):
     rows, width = upstream.shape
     steps = up_weight.blocks
     hidden = steps * width
 
-    def body(ready, held, y_ref, keep_ref, s_ref, m_ref, gain_ref, du_ref, dm_ref, db_ref, do_ref, dz_ref, sums_ref, usum_ref, total):
+    def body(ready, held, y_ref, dz_ref, s_ref, m_ref, gain_ref, du_ref, dm_ref, db_ref, do_ref, sums_ref, usum_ref, total):
         step = pl.program_id(0)
 
         @pl.when(step == 0)
         def _():
-            rounded = jnp.where(keep_ref[...] > 0, y_ref[...].astype(full), 0.0).astype(low)
-            dz_ref[...] = rounded
-            sums_ref[0:1] = column_sum(rounded)
+            sums_ref[0:1] = column_sum(dz_ref[...])
             total[...] = jnp.zeros_like(total)
             ready(0)
 
@@ -418,8 +430,7 @@
             normed, factor = normalize(m_ref[...])
             sums_ref[1:2] = column_sum(grad_second * normed)
             sums_ref[2:3] = column_sum(grad_second)
-            incoming = jnp.where(keep_ref[...] > 0, y_ref[...].astype(full), 0.0)
-            grad_middle = incoming + normalize_back(grad_second * gain_ref[...], normed, factor)
+            grad_middle = y_ref[...].astype(full) + normalize_back(grad_second * gain_ref[...], normed, factor)
             dm_ref[...] = grad_middle
             branch = grad_middle.astype(low)
             db_ref[...] = branch
@@ -433,7 +444,7 @@
         (steps,),
         [
             (upstream, whole((rows, width))),
-            (keep, whole((rows, 1))),
+            (rounded, whole((rows, width))),
             (slope, pl.BlockSpec((rows, width), lambda j: (0, j))),
             (middle, whole((rows, width))),
             (gain, whole((1, width))),
@@ -443,11 +454,11 @@
             ((rows, width), full, whole((rows, width))),
             ((rows, width), low, whole((rows, width))),
             ((rows, width), low, whole((rows, width))),
-            ((rows, width), low, whole((rows, width))),
             ((8, width), full, whole((8, width))),
             ((1, hidden), full, pl.BlockSpec((1, width), lambda j: (0, j))),
         ],
         "feed_forward_back",
+        21,
         scratch=[pltpu.VMEM((rows, width), full)],
     )
 
@@ -458,7 +469,7 @@
 
     def body(ready, held, g_ref, x_ref, gain_ref, dm_ref, *rest):
         if joined:
-            de_ref, dx_ref, skip_ref, sums_ref, total = rest
+            de_ref, dx_ref, dz_ref, skip_ref, sums_ref, total = rest
         else:
             dx_ref, sums_ref, total = rest
         step = pl.program_id(0)
@@ -482,7 +493,9 @@
                 de_ref[...] = entry
                 sums_ref[2:3] = column_sum(entry)
                 ready(1)
-                dx_ref[...] = dot(entry, held[1][0, :width], (1, 1))
+                grad = dot(entry, held[1][0, :width], (1, 1))
+                dx_ref[...] = grad
+                dz_ref[...] = grad.astype(low)
                 skip_ref[...] = dot(entry, held[1][0, width:], (1, 1))
             else:
                 dx_ref[...] = grad
@@ -495,7 +508,8 @@
     ]
     outs = [((rows, width), full, whole((rows, width))), ((8, width), full, whole((8, width)))]
     if joined:
-        outs = [((rows, width), low, whole((rows, width))), outs[0], outs[0], outs[1]]
+        rounded = ((rows, width), low, whole((rows, width)))
+        outs = [rounded, outs[0], rounded, outs[0], outs[1]]
     return weighted(
         body,
         [weight] + ([join_weight] if joined else []),
@@ -503,11 +517,12 @@
         ins,
         outs,
         "project_back",
+        13 if joined else 9,
         scratch=[pltpu.VMEM((rows, width), full)],
     )
 
 
-def picked(body, which, grid, ins, outs, name, aliases=None):
+def picked(body, which, grid, ins, outs, name, micros, aliases=None):
     return pl.pallas_call(
         body,
         grid_spec=pltpu.PrefetchScalarGridSpec(
@@ -519,7 +534,7 @@
         out_shape=[jax.ShapeDtypeStruct(shape, kind) for shape, kind, _ in outs],
         name=name,
         input_output_aliases={place + 1: out for place, out in (aliases or {}).items()},
-        cost_estimate=pl.CostEstimate(flops=10**6, bytes_accessed=10**6, transcendentals=0),
+        cost_estimate=cost(micros),
         compiler_params=pltpu.CompilerParams(vmem_limit_bytes=48 * 2**20),
     )(which, *[array for array, _ in ins])
 
@@ -542,6 +557,7 @@
         ],
         [((shares, 2, part, width), low, pl.BlockSpec((shares, 1, part, width), lambda g, core: (0, g, 0, 0)))],
         "up_term",
+        3.5,
     )[0].reshape(shares, 2 * part, width)
 
 
@@ -550,18 +566,28 @@
     shares = lax.axis_size("narrow")
     part = width // shares
 
-    def body(core_ref, l_ref, r_ref, o_ref, b_ref, out_ref):
-        last = core_ref[0] * 2 + pl.program_id(0) == 3
+    def body(core_ref, l_ref, r_ref, o_ref, b_ref, one_ref, two_ref):
+        step = pl.program_id(0)
+        last = core_ref[0] * 2 + step == 3
 
         @pl.when(last)
         def _():
-            out_ref[...] = dot(o_ref[...], b_ref[...], (0, 0)).astype(low).reshape(shares, 1, part, width)
+            two_ref[...] = dot(o_ref[...], b_ref[...], (0, 0)).astype(low).reshape(shares, part, width)
 
         @pl.when(jnp.logical_not(last))
         def _():
-            out_ref[...] = dot(l_ref[...], r_ref[0], (0, 0)).astype(low).reshape(shares, 1, part, width)
+            value = dot(l_ref[...], r_ref[0], (0, 0)).astype(low).reshape(shares, part, width)
+
+            @pl.when(step == 0)
+            def _():
+                one_ref[...] = value
+
+            @pl.when(step == 1)
+            def _():
+                two_ref[...] = value
 
     flat = pl.BlockSpec((rows, width), lambda g, core: (0, 0))
+    out = ((shares, part, width), low, pl.BlockSpec((shares, part, width), lambda g, core: (0, 0, 0)))
     return picked(
         body,
         core,
@@ -572,9 +598,10 @@
             (mixed, flat),
             (branch, flat),
         ],
-        [((shares, 2, part, width), low, pl.BlockSpec((shares, 1, part, width), lambda g, core: (0, g, 0, 0)))],
+        [out, out],
         "qkv_out_term",
-    )[0].reshape(shares, 2 * part, width)
+        3.5,
+    )
 
 
 def down_term(left, right, core):
@@ -600,41 +627,67 @@
         ],
         [((shares * part, width), low, pl.BlockSpec((width, width), lambda g, core: (g, 0)))],
         "down_term",
+        3.5,
     )[0].reshape(shares, part, width)
 
 
 def join_term(middle, skip, right, core):
     rows, width = right.shape
     shares = lax.axis_size("narrow")
+    part = width // shares
     half = width // 2
+    if part != half:
+        left = jnp.concatenate([middle, skip], axis=1).reshape(rows, shares, 2, part)
+        left = lax.dynamic_index_in_dim(left, core[0], 2, keepdims=False).reshape(rows, shares * part)
+        middle, skip = left[:, :half], left[:, half:]
 
     def body(core_ref, m_ref, s_ref, r_ref, out_ref):
-        out_ref[:width] = dot(m_ref[...], r_ref[...], (0, 0)).astype(low)
-        out_ref[width:] = dot(s_ref[...], r_ref[...], (0, 0)).astype(low)
-
-    flat = pl.BlockSpec((rows, width), lambda g, core: (0, 0))
+        out_ref[:half] = dot(m_ref[...], r_ref[...], (0, 0)).astype(low)
+        out_ref[half:] = dot(s_ref[...], r_ref[...], (0, 0)).astype(low)
+
+    side = pl.BlockSpec((rows, half), lambda g, core: (0, core[0] if part == half else 0))
     return picked(
         body,
         core,
         (1,),
-        [(middle, flat), (skip, flat), (right, pl.BlockSpec((rows, half), lambda g, core: (0, core[0])))],
-        [((2 * width, half), low, pl.BlockSpec((2 * width, half), lambda g, core: (0, 0)))],
+        [(middle, side), (skip, side), (right, pl.BlockSpec((rows, width), lambda g, core: (0, 0)))],
+        [((width, width), low, pl.BlockSpec((width, width), lambda g, core: (0, 0)))],
         "join_term",
-    )[0].reshape(shares, 2 * width // shares, half)
-
-
-def add_halve(kept, got, bit):
-    _, rows, columns = kept.shape
-    steps = 2 if rows % 32 == 0 and rows >= 256 else 1
-    block = pl.BlockSpec((2, rows // steps, columns), lambda g, bit: (0, g, 0))
-    out = ((rows, columns), low, pl.BlockSpec((rows // steps, columns), lambda g, bit: (g, 0)))
-
-    def body(bit_ref, kept_ref, got_ref, sent_ref, left_ref):
+        2,
+    )[0].reshape(shares, part, width)
+
+
+def add_halve(bit, *pairs):
+    lead, columns = pairs[0].shape[0], pairs[0].shape[-1]
+    sizes = [pair.shape[2] for pair in pairs[::2]]
+    total = sum(sizes)
+    steps = 2 if len(sizes) == 1 and total % 32 == 0 and total >= 256 else 1
+
+    def body(bit_ref, *refs):
         mine = bit_ref[0]
-        for target, place in ((sent_ref, 1 - mine), (left_ref, mine)):
-            target[...] = (kept_ref[place].astype(full) + got_ref[place].astype(full)).astype(low)
-
-    return picked(body, bit, (steps,), [(kept, block), (got, block)], [out, out], "add_halve")
+        for target, place in ((refs[-2], 1 - mine), (refs[-1], mine)):
+            begin = 0
+            for kept_ref, got_ref in zip(refs[:-2:2], refs[1:-2:2]):
+                length = kept_ref.shape[2]
+                for each in range(lead):
+                    value = kept_ref[each, place].astype(full) + got_ref[each, place].astype(full)
+                    target[each, begin : begin + length] = value.astype(low)
+                begin += length
+
+    ins = [
+        (pair, pl.BlockSpec((lead, 2, pair.shape[2] // steps, columns), lambda g, bit: (0, 0, g, 0)))
+        for pair in pairs
+    ]
+    out = (
+        (lead, total, columns),
+        low,
+        pl.BlockSpec((lead, total // steps, columns), lambda g, bit: (0, g, 0)),
+    )
+    return picked(body, bit, (steps,), ins, [out, out], "add_halve", 2)
+
+
+def add(one, two):
+    return (one.astype(full) + two.astype(full)).astype(low)
 
 
 def pair_up(own, got, bit):
@@ -647,65 +700,74 @@
 
     flat = pl.BlockSpec((rows, columns), lambda g, bit: (0, 0))
     out = ((2, rows, columns), low, pl.BlockSpec((2, rows, columns), lambda g, bit: (0, 0, 0)))
-    return picked(body, bit, (1,), [(own, flat), (got, flat)], [out], "pair_up")[0]
-
-
-def finish(kind, own, got, core, scale, layer, targets):
-    shares = lax.axis_size("narrow")
-    columns = own.shape[-1]
+    return picked(body, bit, (1,), [(own, flat), (got, flat)], [out], "pair_up", 1)[0]
+
+
+def finish(kind, half, own, got, begin, length, core, layer, targets):
+    pieces, _, columns = own.shape
+    scale = 1.0 / lax.axis_size("wide")
     aliases = {place + 2: place for place in range(len(targets))}
-
-    def chosen(core_ref, half, own_ref, got_ref):
-        return jnp.where(core_ref[0] == half, own_ref[...], got_ref[...]).astype(full) * scale
-
-    if kind == "join":
-        rows = own.shape[0]
-
-        def body(core_ref, own_ref, got_ref, out_ref):
-            out_ref[:, :columns] = chosen(core_ref, 0, own_ref, got_ref)
-            out_ref[:, columns:] = chosen(core_ref, 1, own_ref, got_ref)
-
-        flat = pl.BlockSpec((rows, columns), lambda g, core: (0, 0))
-        out = ((rows, 2 * columns), full, pl.BlockSpec((rows, 2 * columns), lambda g, core: (0, 0)))
-        return picked(body, core, (1,), [(own, flat), (got, flat)], [out], "finish_join")
-    if kind == "down":
-        rows = own.shape[0]
+    source = pl.BlockSpec((pieces, length, columns), lambda g, core: (0, begin // length, 0))
+    ins = [(own, source), (got, source)] + [(target, ANY) for target in targets]
+    rows = pieces * length
+
+    def chosen(core_ref, which, own_ref, got_ref, place=None):
+        sides = [own_ref, got_ref]
+        if place is None:
+            values = [side[...].reshape(pieces * length, columns) for side in sides]
+        else:
+            near = pl.ds(place * (pieces // 2), pieces // 2)
+            values = [side[near].reshape(pieces * length // 2, columns) for side in sides]
+        return jnp.where(core_ref[0] == which, values[0], values[1]).astype(full) * scale
+
+    if kind in ("down", "join"):
 
         def body(core_ref, own_ref, got_ref, *rest):
             rest[-1][0] = chosen(core_ref, pl.program_id(0), own_ref, got_ref)
 
-        flat = pl.BlockSpec((rows, columns), lambda g, core: (0, 0))
-        ins = [(own, flat), (got, flat)] + [(target, ANY) for target in targets]
-        out = ((2, 2 * rows, columns), full, pl.BlockSpec((1, rows, columns), lambda g, core: (layer, g, 0)))
-        return picked(body, core, (2,), ins, [out], "finish_down", aliases)
-    rows = own.shape[0] // 2
-    block = pl.BlockSpec((rows, columns), lambda g, core: (g % 2, 0))
-    ins = [(own, block), (got, block)] + [(target, ANY) for target in targets]
+        place = layer if kind == "down" else 0
+        shape = (2 if kind == "down" else 1, 2 * rows, columns)
+        out = (shape, full, pl.BlockSpec((1, rows, columns), lambda g, core: (place, g, 0)))
+        return picked(body, core, (2,), ins, [out], "finish_rows", 3, aliases)
+    steps = 4 if half is None else 2
+    rows = rows // 2 if half is None else rows
+
+    def block(step):
+        return step if half is None else 2 * step + half
+
+    def values_of(core_ref, own_ref, got_ref):
+        step = pl.program_id(0)
+        if half is None:
+            return chosen(core_ref, step // 2, own_ref, got_ref, step % 2)
+        return chosen(core_ref, step, own_ref, got_ref)
+
+    def body(core_ref, own_ref, got_ref, *rest):
+        values = values_of(core_ref, own_ref, got_ref)
+        if kind == "up":
+            rest[-1][0] = values
+            return
+        last = block(pl.program_id(0)) == 3
+
+        @pl.when(jnp.logical_not(last))
+        def _():
+            rest[-2][0] = values
+
+        @pl.when(last)
+        def _():
+            rest[-1][0] = values
+
     if kind == "up":
-
-        def body(core_ref, own_ref, got_ref, *rest):
-            rest[-1][0] = chosen(core_ref, pl.program_id(0) // 2, own_ref, got_ref)
-
-        out = ((2, rows, 4 * columns), full, pl.BlockSpec((1, rows, columns), lambda g, core: (layer, 0, g)))
-        return picked(body, core, (4,), ins, [out], "finish_up", aliases)
-
-    def body(core_ref, own_ref, got_ref, *rest):
-        qkv_ref, out_ref = rest[-2:]
-        values = chosen(core_ref, pl.program_id(0) // 2, own_ref, got_ref)
-
-        @pl.when(pl.program_id(0) < 3)
-        def _():
-            qkv_ref[0] = values
-
-        @pl.when(pl.program_id(0) == 3)
-        def _():
-            out_ref[0] = values
-
+        outs = [((2, rows, 4 * columns), full, pl.BlockSpec((1, rows, columns), lambda g, core: (layer, 0, block(g))))]
+        return picked(body, core, (steps,), ins, outs, "finish_columns", 3, aliases)
     outs = [
-        ((2, rows, 3 * columns), full, pl.BlockSpec((1, rows, columns), lambda g, core: (layer, 0, jnp.minimum(g, 2)))),
+        (
+            (2, rows, 3 * columns),
+            full,
+            pl.BlockSpec((1, rows, columns), lambda g, core: (layer, 0, jnp.minimum(block(g), 2))),
+        ),
         ((2, rows, columns), full, pl.BlockSpec((1, rows, columns), lambda g, core: (layer, 0, 0))),
     ]
-    return picked(body, core, (4,), ins, outs, "finish_qkv_out", aliases)
+    return picked(body, core, (steps,), ins, outs, "finish_qkv_out", 3, aliases)
 
 
 def after(value, *earlier):
@@ -725,68 +787,102 @@
     def __init__(self):
         self.last = ()
 
-    def run(self, function, *arrays, **named):
+    def run(self, function, *arrays):
         held = lax.optimization_barrier(tuple(arrays) + self.last)[: len(arrays)]
-        out = function(*held, **named)
+        out = function(*held)
         self.last = (jax.tree.leaves(out)[0],)
         return out
 
 
+def place_bit(axis, mask):
+    return ((lax.axis_index(axis) & mask) // mask).astype(jnp.int32).reshape(1)
+
+
+class Term:
+    def __init__(self, kind, layer, half, kept, got, core):
+        self.kind, self.layer, self.half, self.kept, self.got, self.core = kind, layer, half, kept, got, core
+
+
+def terms_of(order, kind, layer, function, *arrays):
+    core = place_bit("wide", 1)
+    sent = order.run(lambda *x: function(*x, 1 - core), *arrays)
+    got = jax.tree.map(lambda each: swap(each, "wide", 1), sent)
+    kept = order.run(lambda *x: function(*x, core), *arrays)
+    if isinstance(kept, (tuple, list)):
+        return [Term(kind, layer, place, kept[place], got[place], core) for place in range(len(kept))]
+    return [Term(kind, layer, None, kept, got, core)]
+
+
 class Reduce:
-    def __init__(self, order, kind, term, *arrays):
-        self.order, self.kind = order, kind
-        place = lax.axis_index("wide")
-        self.core = (place & 1).astype(jnp.int32).reshape(1)
-        self.sent = order.run(term, *arrays, 1 - self.core)
-        self.got = swap(self.sent, "wide", 1)
-        self.kept = order.run(term, *arrays, self.core)
-        self.columns = self.kept.shape[-1]
-        stages = [("narrow", mask) for mask in reversed(masks("narrow"))]
-        stages += [("wide", mask) for mask in masks("wide")[1:]]
-        self.down = list(stages)
-        self.up = [stage for stage in reversed(stages) if stage[0] == "wide"]
-        self.joining = None
-
-    def bit(self, axis, mask):
-        return ((lax.axis_index(axis) & mask) // mask).astype(jnp.int32).reshape(1)
+    def __init__(self, order, terms, first=()):
+        self.order, self.terms = order, terms
+        wide = [("wide", mask) for mask in masks("wide")[1:]]
+        narrow = [("narrow", mask) for mask in reversed(masks("narrow"))]
+        early = [stage for stage in wide if stage[1] in first]
+        late = [stage for stage in wide if stage[1] not in first]
+        self.early, self.down, self.up = early + narrow, late, list(reversed(early))
+        self.pieces = 2 ** len(early)
+        self.columns = terms[0].kept.shape[-1]
+        self.passed = [0] * len(terms)
+        self.parts = [(term.kept, term.got) for term in terms]
+        self.joining, self.lengths, self.closed = None, None, False
+
+    def halve(self, axis, mask, lead, pairs):
+        shaped = [array.reshape(lead, 2, -1, self.columns) for pair in pairs for array in pair]
+        bit = place_bit(axis, mask)
+        sent, kept = self.order.run(lambda *x: add_halve(bit, *x), *shaped)
+        return kept, swap(sent, axis, mask)
+
+    def apart(self, place=0):
+        axis, mask = self.early[self.passed[place]]
+        self.passed[place] += 1
+        lead = lax.axis_size("narrow") if axis == "wide" else 1
+        self.parts[place] = self.halve(axis, mask, lead, [self.parts[place]])
+        if axis == "narrow" and self.passed[place] < len(self.early):
+            self.apart(place)
 
     def step(self):
         if self.down:
             axis, mask = self.down.pop(0)
-            shape = (2, -1, self.columns)
-            kept, got = self.kept.reshape(shape), self.got.reshape(shape)
-            self.sent, self.kept = self.order.run(add_halve, kept, got, self.bit(axis, mask))
-            self.got = swap(self.sent, axis, mask)
+            rows = [kept.size // self.columns for kept, _ in self.parts]
+            even = all(each % 32 == 0 for each in rows)
+            if self.lengths is None:
+                self.lengths = [each // 2 for each in rows] if even else rows
+                self.pieces *= 2 if even else 1
+                if not even:
+                    flat = [[side.reshape(-1, self.columns) for side in pair] for pair in self.parts]
+                    self.parts = [tuple(jnp.concatenate(sides) for sides in zip(*flat))]
+            if even:
+                self.up.insert(0, (axis, mask))
+                self.parts = [self.halve(axis, mask, 1, self.parts)]
+            else:
+                total = self.order.run(add, *self.parts[0])
+                self.parts = [(total, swap(total, axis, mask))]
             return
+        kept, got = [array.reshape(-1, self.columns) for array in self.parts[0]]
         if self.joining is None:
-            total = self.order.run(lambda one, two: (one.astype(full) + two.astype(full)).astype(low), self.kept, self.got)
+            total = self.order.run(add, kept, got)
         else:
-            total = self.order.run(pair_up, self.kept, self.got, self.bit(*self.joining))
-            total = total.reshape(-1, self.columns)
-        self.kept = total
+            bit = place_bit(*self.joining)
+            total = self.order.run(lambda *x: pair_up(*x, bit), kept, got).reshape(-1, self.columns)
         if self.up:
             self.joining = self.up.pop(0)
-            self.got = swap(total, *self.joining)
+            self.parts = [(total, swap(total, *self.joining))]
         else:
-            self.got = swap(total, "wide", 1)
-
-    def steps_left(self):
-        return len(self.down) + 1 + len([1 for _ in self.up])
-
-    def finish(self, layer, targets=()):
-        scale = 1.0 / lax.axis_size("wide")
-
-        def last(own, got, core, *targets):
-            return finish(self.kind, own, got, core, scale, layer, targets)
-
-        return self.order.run(last, self.kept, self.got, self.core, *targets)
-
-
-def sum_all(values):
-    for axis in ("wide", "narrow"):
-        for mask in masks(axis):
-            values = values + swap(values, axis, mask)
-    return values
+            self.parts = [(total, swap(total, "wide", 1))]
+            self.closed = True
+
+    def finish(self, done):
+        own, got = [array.reshape(self.pieces, -1, self.columns) for array in self.parts[0]]
+        begin = 0
+        for term, length in zip(self.terms, self.lengths):
+            targets = done.get(term.kind, ())
+
+            def last(own, got, core, *targets, term=term, begin=begin, length=length):
+                return finish(term.kind, term.half, own, got, begin, length, core, term.layer, targets)
+
+            done[term.kind] = self.order.run(last, own, got, term.core, *targets)
+            begin += length
 
 
 def on_device(
@@ -808,10 +904,6 @@
 ):
     items, seq_rows, width = tokens.shape
     rows = items * seq_rows
-    lengths = PATCHES + 1 + CAPTION * flags
-    valid = lax.broadcasted_iota(jnp.int32, (items, seq_rows), 1) < lengths[:, None]
-    keep = valid.reshape(rows, 1).astype(full)
-    every = jnp.ones((rows, 1), full)
     me = lax.axis_index("narrow")
     shares = lax.axis_size("narrow")
     spots = jnp.stack([me, lax.axis_index("wide")]).astype(jnp.int32)
@@ -822,8 +914,12 @@
     qkv1, out1, up1, down1 = [Weight(weight, 1, width, spots) for weight in weights]
     join = Weight(skip_weight, None, width, spots)
 
+    qkv0.fetch()
+    out0.fetch(qkv0.sent)
+    up0.fetch(out0.sent)
+    down0.fetch(up0.sent)
     small = (norm_gains, norm_biases, out_bias, up_bias, down_bias, skip_bias)
-    held = jnp.concatenate([piece.reshape(-1) for piece in small])[None]
+    held = after(jnp.concatenate([piece.reshape(-1) for piece in small]), down0.sent)[None]
     for mask in masks("narrow"):
         held = jnp.concatenate([held, swap(held, "narrow", mask)])
     parts = [lax.dynamic_index_in_dim(held, me ^ place, 0, keepdims=False) for place in range(shares)]
@@ -839,23 +935,23 @@
         return values.reshape(1, -1)
 
     tokens_flat, skip_flat, cotangent_flat = [array.reshape(rows, width) for array in (tokens, skip, cotangent)]
-
-    qkv0.fetch()
-    out0.fetch()
-    up0.fetch()
-    down0.fetch()
+    lengths = PATCHES + 1 + CAPTION * flags
+    valid = lax.broadcasted_iota(jnp.int32, (items, seq_rows), 1) < lengths[:, None]
+    keep = valid.reshape(rows, 1).astype(full)
+    dz1 = jnp.where(keep > 0, cotangent_flat, 0)
+
     qkv0.share(1)
-    out0.share(1)
     qkv0.share(0)
-    out0.share(0)
-    up0.share(1)
     a0, packed0 = order.run(lambda *x: project_qkv(*x, qkv0), tokens_flat, line(gains[0, 0]), line(shifts[0, 0]))
+    out0.share(1, a0)
+    up0.share(1, a0)
     down0.share(1, a0)
-    up0.share(0, a0)
     join.fetch(a0)
     qkv1.fetch(a0)
     packed0 = packed0.reshape(3, items, seq_rows, width)
     mixed0, totals0 = order.run(lambda *x: attend(*x, items, seq_rows), packed0, lengths)
+    out0.share(0, mixed0)
+    up0.share(0, mixed0)
     down0.share(0, mixed0)
     join.share(1, mixed0)
     qkv1.share(1, mixed0)
@@ -863,7 +959,7 @@
     up1.fetch(mixed0)
     mixed0 = mixed0.reshape(rows, width)
     m0, second0, hidden0, slope0, middle = order.run(
-        lambda x, o, ob, g, s, ub, db: feed_forward(x, o, out0, ob, g, s, up0, ub, down0, db, every),
+        lambda x, o, ob, g, s, ub, db: feed_forward(x, o, out0, ob, g, s, up0, ub, down0, db),
         tokens_flat, mixed0, line(out_biases[0]), line(gains[0, 1]), line(shifts[0, 1]), line(up_biases[0]),
         line(down_biases[0]),
     )
@@ -884,68 +980,66 @@
     mixed1 = mixed1.reshape(rows, width)
     down1.share(0, mixed1)
     m1, second1, hidden1, slope1, output = order.run(
-        lambda x, o, ob, g, s, ub, db: feed_forward(x, o, out1, ob, g, s, up1, ub, down1, db, keep),
+        lambda x, o, ob, g, s, ub, db, k: feed_forward(x, o, out1, ob, g, s, up1, ub, down1, db, k),
         entry, mixed1, line(out_biases[1]), line(gains[1, 1]), line(shifts[1, 1]), line(up_biases[1]),
-        line(down_biases[1]),
-    )
-
-    dz1 = jnp.where(keep > 0, cotangent_flat, 0)
-    reduce_down1 = Reduce(order, "down", down_term, hidden1, dz1)
-    reduce_down1.step()
-    du, dm, db, do, dz, sums1, usum1 = order.run(
-        lambda y, s, m, g: feed_forward_back(y, s, down1, up1, m, g, out1, keep),
-        cotangent_flat, slope1, m1, line(gains[1, 1]),
-    )
-    reduce_up1 = Reduce(order, "up", up_term, second1, du)
-    reduce_up1.step()
-    reduce_down1.step()
+        line(down_biases[1]), keep,
+    )
+
+    down1_term = terms_of(order, "down", 1, down_term, hidden1, dz1)
+    pending = Reduce(order, down1_term)
+    pending.apart()
+    du, dm, db, do, sums1, usum1 = order.run(
+        lambda y, z, s, m, g: feed_forward_back(y, z, s, down1, up1, m, g, out1),
+        dz1, dz1, slope1, m1, line(gains[1, 1]),
+    )
+    up1_term = terms_of(order, "up", 1, up_term, second1, du)
+    first = Reduce(order, down1_term + up1_term)
+    first.parts[0], first.passed[0] = pending.parts[0], pending.passed[0]
+    first.apart(1)
     dpacked = order.run(
         lambda *x: attend_back(*x, items, seq_rows), packed1, do.reshape(items, seq_rows, width), totals1, lengths
     )
     flat_packed = dpacked.reshape(3, rows, width)
-    reduce_qkv1 = Reduce(order, "qkv", qkv_out_term, a1, flat_packed, mixed1, db)
-    reduce_qkv1.step()
-    reduce_down1.step()
-    reduce_up1.step()
-    dentry, dmiddle, skip_grad, sums3 = order.run(
+    qkv1_terms = terms_of(order, "qkv", 1, qkv_out_term, a1, flat_packed, mixed1, db)
+    pending = Reduce(order, qkv1_terms)
+    pending.apart(0)
+    pending.apart(1)
+    dentry, dmiddle, dz0, skip_grad, sums3 = order.run(
         lambda gp, x, g, dm: project_back(gp, qkv1, x, g, dm, join), flat_packed, entry, line(gains[1, 0]), dm
     )
-    reduce_join = Reduce(order, "join", join_term, middle, skip_flat, dentry)
-    reduce_down1.step()
-    reduce_up1.step()
-    reduce_join.step()
-    reduce_qkv1.step()
-
-    dz0 = dmiddle.astype(low)
-    reduce_down0 = Reduce(order, "down", down_term, hidden0, dz0)
-    reduce_down0.step()
-    reduce_down1.step()
-    reduce_up1.step()
-    reduce_qkv1.step()
-    reduce_join.step()
-    du, dm, db, do, dz, sums0, usum0 = order.run(
-        lambda y, s, m, g: feed_forward_back(y, s, down0, up0, m, g, out0, every),
-        dmiddle, slope0, m0, line(gains[0, 1]),
-    )
-    reduce_up0 = Reduce(order, "up", up_term, second0, du)
-    reduce_up0.step()
-    reduce_down1.step()
-    reduce_up1.step()
-    reduce_qkv1.step()
-    reduce_join.step()
-    reduce_down0.step()
+    join_terms = terms_of(order, "join", 1, join_term, middle, skip_flat, dentry)
+    first.step()
+    second = Reduce(order, qkv1_terms + join_terms)
+    second.parts[:2], second.passed[:2] = pending.parts, pending.passed
+    second.apart(2)
+
+    down0_term = terms_of(order, "down", 0, down_term, hidden0, dz0)
+    pending = Reduce(order, down0_term, (4,))
+    pending.apart()
+    du, dm, db, do, sums0, usum0 = order.run(
+        lambda y, z, s, m, g: feed_forward_back(y, z, s, down0, up0, m, g, out0),
+        dmiddle, dz0, slope0, m0, line(gains[0, 1]),
+    )
+    up0_term = terms_of(order, "up", 0, up_term, second0, du)
+    third = Reduce(order, down0_term + up0_term, (4,))
+    third.parts[0], third.passed[0] = pending.parts[0], pending.passed[0]
+    first.step()
+    third.apart(1)
+    third.apart(0)
+    second.step()
     dpacked = order.run(
         lambda *x: attend_back(*x, items, seq_rows), packed0, do.reshape(items, seq_rows, width), totals0, lengths
     )
     flat_packed = dpacked.reshape(3, rows, width)
-    reduce_qkv0 = Reduce(order, "qkv", qkv_out_term, a0, flat_packed, mixed0, db)
-    reduce_qkv0.step()
-    reduce_down1.step()
-    reduce_up1.step()
-    reduce_qkv1.step()
-    reduce_join.step()
-    reduce_down0.step()
-    reduce_up0.step()
+    qkv0_terms = terms_of(order, "qkv", 0, qkv_out_term, a0, flat_packed, mixed0, db)
+    first.step()
+    second.step()
+    third.apart(1)
+    fourth = Reduce(order, qkv0_terms[:1])
+    fifth = Reduce(order, qkv0_terms[1:], (4,))
+    fourth.apart()
+    fifth.apart()
+    first.step()
     tokens_grad, sums2 = order.run(
         lambda gp, x, g, dm: project_back(gp, qkv0, x, g, dm), flat_packed, tokens_flat, line(gains[0, 0]), dm
     )
@@ -962,23 +1056,58 @@
         sums3[2],
     ]
     split = [jnp.moveaxis(piece.reshape(piece.shape[:-1] + (shares, -1)), -2, 0) for piece in minor]
-    packed_minor = jnp.concatenate([piece.reshape(shares, -1) for piece in split], axis=1)
-    owned = lax.dynamic_index_in_dim(sum_all(packed_minor), me, 0, keepdims=False) * (1.0 / lax.axis_size("wide"))
-
-    running = [reduce_down1, reduce_up1, reduce_qkv1, reduce_join, reduce_down0, reduce_up0, reduce_qkv0]
+    minor_sum = jnp.concatenate([piece.reshape(shares, -1) for piece in split], axis=1)
+    minor_stages = [("wide", mask) for mask in masks("wide")] + [("narrow", mask) for mask in masks("narrow")]
+    minor_got = swap(minor_sum, *minor_stages[0])
+
+    def minor_step():
+        nonlocal minor_sum, minor_got
+        if minor_stages:
+            minor_stages.pop(0)
+            minor_sum = order.run(lambda one, two: one + two, minor_sum, minor_got)
+            if minor_stages:
+                minor_got = swap(minor_sum, *minor_stages[0])
+
     done = {}
-    while running:
-        for each in list(running):
-            if each.up or each.down or (each.joining is None):
+    first.step()
+    second.step()
+    third.step()
+    minor_step()
+    fifth.apart()
+    first.step()
+    second.step()
+    fourth.step()
+    minor_step()
+    third.step()
+    fifth.step()
+    second.step()
+    first.step()
+    fourth.step()
+    minor_step()
+    third.step()
+    fifth.step()
+    first.finish(done)
+    second.step()
+    fourth.step()
+    minor_step()
+    third.step()
+    fifth.step()
+    second.step()
+    fourth.step()
+    minor_step()
+    third.step()
+    fifth.step()
+    second.finish(done)
+    for stage in range(9):
+        minor_step()
+        for each in (fourth, third, fifth):
+            if not each.closed:
                 each.step()
-            elif not getattr(each, "closed", False):
-                each.step()
-                each.closed = True
-            else:
-                running.remove(each)
-                layer = 0 if each in (reduce_down0, reduce_up0, reduce_qkv0) else 1
-                done[each.kind] = each.finish(layer, done.get(each.kind, ()))
-
+            elif each.parts:
+                each.finish(done)
+                each.parts = None
+
+    owned = lax.dynamic_index_in_dim(minor_sum, me, 0, keepdims=False) * (1.0 / lax.axis_size("wide"))
     minor_sums, begin = [], 0
     for piece in split:
         end = begin + piece.size // shares
@@ -997,7 +1126,7 @@
         minor_sums[3],
         done["down"][0],
         minor_sums[4],
-        done["join"][0],
+        done["join"][0][0],
         minor_sums[5],
     )
 

time: 721 us -> 695 us (0.964)
  starting transfers between devices: 121 us -> 88.2 us
    ppermute x105 -> x96, starting transfers between devices: 121 us -> 88.2 us  [swap(): lax.ppermute(values, axis, [(source, source ^ mask) for source in range(s...]
    unnamed x144 -> x202, local copies, waits for them, and re-layouts: 13.2 us -> 30.1 us
    slice x4 -> x0, local copies, waits for them, and re-layouts: 12.5 us -> none  [__init__(): shard = array if layer is None else array[layer]]
    pallas_call x70 -> x63, Pallas kernels: 98.5 us -> 101 us  [picked(): pl.pallas_call(body, grid_spec=pltpu.PrefetchScalarGridSpec(num_scalar_pr...]
    ppermute x105 -> x96, waiting for transfers between devices: 222 us -> 223 us  [swap(): lax.ppermute(values, axis, [(source, source ^ mask) for source in range(s...]
  transfers between devices with their start and end apart: 105 -> 96, of which waited for: 49 -> 31; matrix products, arithmetic and copies ran while one was open for 7% -> 6% of each run, Pallas kernels for 20% -> 27%
where the time goes in v3:
time: 695 us; the launch traced here: 683 us
  Pallas kernels  300 us (43%)
  waiting for transfers between devices  223 us (32%)
  starting transfers between devices  88.2 us (13%)
  local copies, waits for them, and re-layouts  60.2 us (9%)
  other arithmetic  8.7 us (1%)
    ppermute x96, waiting for transfers between devices, swap(): lax.ppermute(values, axis, [(source, source ^ mask) for source in range(s...  223 us
    pallas_call x12, Pallas kernels, call(): pl.pallas_call(body, grid=grid, in_specs=[spec for _, spec in ins], out_s...  199 us
    pallas_call x63, Pallas kernels, picked(): pl.pallas_call(body, grid_spec=pltpu.PrefetchScalarGridSpec(num_scalar_pr...  101 us
    ppermute x96, starting transfers between devices, swap(): lax.ppermute(values, axis, [(source, source ^ mask) for source in range(s...  88.2 us
    unnamed x202, local copies, waits for them, and re-layouts  30.1 us
  transfers between devices with their start and end apart: 96, of which 31 were waited for; matrix products, arithmetic and copies ran while one was open for 6% of the time, Pallas kernels for 27%

profile of v3, /device:TPU:1, one launch (start us, length us, event | category | flops | bytes accessed | tf_op | source)
XLA Modules:
  0.0 683.2 jit_solution(13715368627205186095)
XLA Ops:
  13.0 30.0 %collective-permute-done.4 = bf16[1,8064]{1,0:T(2,128)(2,1)S(1)} collective-permute-done((bf16[1,8064]{1,0:T(2,128)(2,1)S(1)}, bf16[1,8064]{1,0:T(2,128)(2,1)S(1)}, u32[]{:S(2)}, u32[]{:S(2)}) %collective-permute-start.4) | collective-permute-done | bytes 16160 | tf_op jit(solution)/shard_map/ppermute | solution.py:779
  47.9 7.3 %collective-permute-done.1.refs_3_ = bf16[1,96,2304]{2,1,0:T(8,128)(2,1)S(1)} collective-permute-done((bf16[1,96,2304]{2,1,0:T(8,128)(2,1)S(1)}, bf16[1,96,2304]{2,1,0:T(8,128)(2,1)S(1)}, u32[]{:S(2)}, u32[]{:S(2)}) %collective-permute-start.1) | collective-permute-done | bytes 442400 | tf_op jit(solution)/shard_map/ppermute | solution.py:779
  59.6 6.6 project_qkv.1
  68.9 13.6 %attend.2 = (bf16[2,336,768]{2,1,0:T(8,128)(2,1)}, f32[2,6,8,336]{3,2,1,0:T(8,128)}) custom-call(s32[2]{0:T(128)} %multiply_add_fusion.length_ref, bf16[3,2,336,768]{3,2,1,0:T(8,128)(2,1)} %bitcast.260, bf16[3,2,336,768]{3,2,1,0:T(8,128)(2,1)} %bitcast.261, bf16[3,2,336,768]{3,2,1,0:T(8,128)(2,1)} %bitcast.262), custom_call_target="tpu_custom_call" | custom-call | flops 12999999488 | bytes 100000 | tf_op jit(solution)/shard_map/attend/pallas_call | solution.py:54
  88.1 5.5 collective-permute-done.11.refs_8_
  99.0 4.0 collective-permute-done.23.refs_7_.refs_2_
  109.3 24.7 %feed_forward.2 = (f32[672,768]{1,0:T(8,128)}, bf16[672,768]{1,0:T(8,128)(2,1)}, bf16[672,3072]{1,0:T(8,128)(2,1)}, bf16[672,3072]{1,0:T(8,128)(2,1)}, bf16[672,768]{1,0:T(8,128)(2,1)}) custom-call(s32[2]{0:T(128)} %pad_add_fusion.refs_0_, bf16[2,384,768]{2,1,0:T(8,128)(2,1)} %refs_11_.7, bf16[1,96,768]{2,1,0:T(8,128)(2,1)} %collective-permute-done.6.refs_2_.refs_12_, ...), custom_call_target="tpu_custom_call" | custom-call | flops 23000000512 | bytes 100000 | tf_op jit(solution)/shard_map/feed_forward/pallas_call | solution.py:54
  138.7 3.2 collective-permute-done.5.refs_2_.refs_12_
  145.2 11.4 %join_qkv.1 = (f32[672,768]{1,0:T(8,128)}, bf16[672,768]{1,0:T(8,128)(2,1)}, bf16[3,672,768]{2,1,0:T(8,128)(2,1)}) custom-call(s32[2]{0:T(128)} %pad_add_fusion.refs_0_, bf16[768,768]{1,0:T(8,128)(2,1)} %refs_6_.10, bf16[1,192,768]{2,1,0:T(8,128)(2,1)} %copy-done.87, bf16[1,192,768]{2,1,0:T(8,128)(2,1)} %copy-done.88, bf16[1,192,768]{2,1,0:T(8,128)(2,1)} %copy-done.90, ...), custom_call_target="tpu_custom_call" | custom-call | flops 11000000512 | bytes 100000 | tf_op jit(solution)/shard_map/join_qkv/pallas_call | solution.py:54
  159.1 13.6 %attend.3 = (bf16[2,336,768]{2,1,0:T(8,128)(2,1)}, f32[2,6,8,336]{3,2,1,0:T(8,128)}) custom-call(s32[2]{0:T(128)} %multiply_add_fusion.length_ref, bf16[3,2,336,768]{3,2,1,0:T(8,128)(2,1)} %bitcast.266, bf16[3,2,336,768]{3,2,1,0:T(8,128)(2,1)} %bitcast.267, bf16[3,2,336,768]{3,2,1,0:T(8,128)(2,1)} %bitcast.268), custom_call_target="tpu_custom_call" | custom-call | flops 12999999488 | bytes 100000 | tf_op jit(solution)/shard_map/attend/pallas_call | solution.py:54
  179.1 25.2 %feed_forward.3 = (f32[672,768]{1,0:T(8,128)}, bf16[672,768]{1,0:T(8,128)(2,1)}, bf16[672,3072]{1,0:T(8,128)(2,1)}, bf16[672,3072]{1,0:T(8,128)(2,1)}, bf16[672,768]{1,0:T(8,128)(2,1)}) custom-call(s32[2]{0:T(128)} %pad_add_fusion.refs_0_, bf16[2,384,768]{2,1,0:T(8,128)(2,1)} %refs_11_.7, bf16[1,96,768]{2,1,0:T(8,128)(2,1)} %collective-permute-done.5.refs_2_.refs_12_, ...), custom_call_target="tpu_custom_call" | custom-call | flops 23000000512 | bytes 100000 | tf_op jit(solution)/shard_map/feed_forward/pallas_call | solution.py:54
  204.3 3.5 down_term.4
  208.0 3.5 down_term.5
  215.6 23.1 %feed_forward_back.2 = (bf16[672,3072]{1,0:T(8,128)(2,1)}, f32[672,768]{1,0:T(8,128)}, bf16[672,768]{1,0:T(8,128)(2,1)}, bf16[672,768]{1,0:T(8,128)(2,1)}, f32[8,768]{1,0:T(8,128)}, /*index=5*/f32[1,3072]{1,0:T(1,128)}) custom-call(s32[2]{0:T(128)} %pad_add_fusion.refs_0_, bf16[2,1536,768]{2,1,0:T(8,128)(2,1)} %refs_1_.14, bf16[1,384,768]{2,1,0:T(8,128)(2,1)} %copy-done.77, ...), custom_call_target="tpu_custom_call" | custom-call | flops 20999999488 | bytes 100000 | tf_op jit(solution)/shard_map/feed_forward_back/pallas_call | solution.py:54
  238.7 3.7 up_term.4
  242.5 3.6 up_term.5
  251.4 17.3 %attend_back.2 = bf16[3,2,336,768]{3,2,1,0:T(8,128)(2,1)} custom-call(s32[2]{0:T(128)} %multiply_add_fusion.length_ref, bf16[3,2,336,768]{3,2,1,0:T(8,128)(2,1)} %bitcast.269, bf16[3,2,336,768]{3,2,1,0:T(8,128)(2,1)} %bitcast.270, bf16[3,2,336,768]{3,2,1,0:T(8,128)(2,1)} %bitcast.271, bf16[2,336,768]{2,1,0:T(8,128)(2,1)} %bitcast.283, ...), custom_call_target="tpu_custom_call" | custom-call | flops 16999999488 | bytes 100000 | tf_op jit(solution)/shard_map/attend_back/pallas_call | solution.py:54
  268.8 3.9 qkv_out_term.4
  274.8 3.7 qkv_out_term.5
  281.0 13.7 %project_back.2 = (bf16[672,768]{1,0:T(8,128)(2,1)}, f32[672,768]{1,0:T(8,128)}, bf16[672,768]{1,0:T(8,128)(2,1)}, f32[672,768]{1,0:T(8,128)}, f32[8,768]{1,0:T(8,128)}) custom-call(s32[2]{0:T(128)} %pad_add_fusion.refs_0_, bf16[2,384,2304]{2,1,0:T(8,128)(2,1)} %refs_1_.15, bf16[1,96,2304]{2,1,0:T(8,128)(2,1)} %copy-done.83, ...), custom_call_target="tpu_custom_call" | custom-call | flops 12999999488 | bytes 100000 | tf_op jit(solution)/shard_map/project_back/pallas_call | solution.py:54
  300.8 25.4 %collective-permute-done.43 = bf16[1,768,768]{2,1,0:T(8,128)(2,1)} collective-permute-done((bf16[1,768,768]{2,1,0:T(8,128)(2,1)S(1)}, bf16[1,768,768]{2,1,0:T(8,128)(2,1)}, u32[]{:S(2)}, u32[]{:S(2)}) %collective-permute-start.43) | collective-permute-done | bytes 1179680 | tf_op jit(solution)/shard_map/ppermute | solution.py:779
  335.9 3.9 down_term.6
  342.0 3.5 down_term.7
  349.7 22.8 %feed_forward_back.3 = (bf16[672,3072]{1,0:T(8,128)(2,1)}, f32[672,768]{1,0:T(8,128)}, bf16[672,768]{1,0:T(8,128)(2,1)}, bf16[672,768]{1,0:T(8,128)(2,1)}, f32[8,768]{1,0:T(8,128)}, /*index=5*/f32[1,3072]{1,0:T(1,128)}) custom-call(s32[2]{0:T(128)} %pad_add_fusion.refs_0_, bf16[2,1536,768]{2,1,0:T(8,128)(2,1)} %refs_1_.14, bf16[1,384,768]{2,1,0:T(8,128)(2,1)} %copy-done.71, ...), custom_call_target="tpu_custom_call" | custom-call | flops 20999999488 | bytes 100000 | tf_op jit(solution)/shard_map/feed_forward_back/pallas_call | solution.py:54
  372.5 3.7 up_term.6
  385.7 17.8 %collective-permute-done.50 = bf16[1,768,768]{2,1,0:T(8,128)(2,1)} collective-permute-done((bf16[1,768,768]{2,1,0:T(8,128)(2,1)S(1)}, bf16[1,768,768]{2,1,0:T(8,128)(2,1)}, u32[]{:S(2)}, u32[]{:S(2)}) %collective-permute-start.50) | collective-permute-done | bytes 1179680 | tf_op jit(solution)/shard_map/ppermute | solution.py:779
  409.6 3.7 up_term.7.refs_0_
  420.3 2.7 add_halve.35
  425.1 17.3 %attend_back.3 = bf16[3,2,336,768]{3,2,1,0:T(8,128)(2,1)} custom-call(s32[2]{0:T(128)} %multiply_add_fusion.length_ref, bf16[3,2,336,768]{3,2,1,0:T(8,128)(2,1)} %bitcast.263, bf16[3,2,336,768]{3,2,1,0:T(8,128)(2,1)} %bitcast.264, bf16[3,2,336,768]{3,2,1,0:T(8,128)(2,1)} %bitcast.265, bf16[2,336,768]{2,1,0:T(8,128)(2,1)} %bitcast.282, ...), custom_call_target="tpu_custom_call" | custom-call | flops 16999999488 | bytes 100000 | tf_op jit(solution)/shard_map/attend_back/pallas_call | solution.py:54
  442.4 4.8 qkv_out_term.6
  457.2 3.9 qkv_out_term.7
  474.3 3.6 collective-permute-done.52
  478.0 9.8 %project_back.3 = (f32[672,768]{1,0:T(8,128)}, f32[8,768]{1,0:T(8,128)}) custom-call(s32[2]{0:T(128)} %pad_add_fusion.refs_0_, bf16[2,384,2304]{2,1,0:T(8,128)(2,1)} %refs_1_.15, bf16[1,96,2304]{2,1,0:T(8,128)(2,1)} %copy-done.79, bf16[1,96,2304]{2,1,0:T(8,128)(2,1)} %copy-done.80, bf16[1,96,2304]{2,1,0:T(8,128)(2,1)} %copy-done.81, ...), custom_call_target="tpu_custom_call" | custom-call | flops 8999999488 | bytes 100000 | tf_op jit(solution)/shard_map/project_back/pallas_call | solution.py:54
  496.0 3.0 collective-permute-done.61.got_ref
  508.3 6.9 %collective-permute-done.65.got_ref = bf16[384,768]{1,0:T(8,128)(2,1)S(1)} collective-permute-done((bf16[384,768]{1,0:T(8,128)(2,1)S(1)}, bf16[384,768]{1,0:T(8,128)(2,1)S(1)}, u32[]{:S(2)}, u32[]{:S(2)}) %collective-permute-start.65) | collective-permute-done | bytes 589856 | tf_op jit(solution)/shard_map/ppermute | solution.py:779
  517.2 11.1 %collective-permute-done.64 = bf16[1,144,768]{2,1,0:T(8,128)(2,1)S(1)} collective-permute-done((bf16[1,144,768]{2,1,0:T(8,128)(2,1)S(1)}, bf16[1,144,768]{2,1,0:T(8,128)(2,1)S(1)}, u32[]{:S(2)}, u32[]{:S(2)}) %collective-permute-start.64) | collective-permute-done | bytes 221216 | tf_op jit(solution)/shard_map/ppermute | solution.py:779
  529.8 25.4 %collective-permute-done.62 = f32[2,8064]{1,0:T(2,128)S(1)} collective-permute-done((f32[2,8064]{1,0:T(2,128)S(1)}, f32[2,8064]{1,0:T(2,128)S(1)}, u32[]{:S(2)}, u32[]{:S(2)}) %collective-permute-start.62) | collective-permute-done | bytes 64544 | tf_op jit(solution)/shard_map/ppermute | solution.py:779
  562.2 4.7 collective-permute-done.68
  567.0 7.5 %collective-permute-done.78 = bf16[1,192,768]{2,1,0:T(8,128)(2,1)S(1)} collective-permute-done((bf16[1,192,768]{2,1,0:T(8,128)(2,1)S(1)}, bf16[1,192,768]{2,1,0:T(8,128)(2,1)S(1)}, u32[]{:S(2)}, u32[]{:S(2)}) %collective-permute-start.78) | collective-permute-done | bytes 294944 | tf_op jit(solution)/shard_map/ppermute | solution.py:779
  577.2 2.8 finish_columns.2.rest_0_
  580.0 3.9 collective-permute-done.75.got_ref
  589.3 3.0 collective-permute-done.74
  592.4 12.1 %collective-permute-done.73 = f32[2,8064]{1,0:T(2,128)S(1)} collective-permute-done((f32[2,8064]{1,0:T(2,128)S(1)}, f32[2,8064]{1,0:T(2,128)S(1)}, u32[]{:S(2)}, u32[]{:S(2)}) %collective-permute-start.73) | collective-permute-done | bytes 64544 | tf_op jit(solution)/shard_map/ppermute | solution.py:779
  609.6 4.3 collective-permute-done.80
  614.0 8.9 %collective-permute-done.87.got_ref = bf16[384,768]{1,0:T(8,128)(2,1)S(1)} collective-permute-done((bf16[384,768]{1,0:T(8,128)(2,1)S(1)}, bf16[384,768]{1,0:T(8,128)(2,1)S(1)}, u32[]{:S(2)}, u32[]{:S(2)}) %collective-permute-start.87) | collective-permute-done | bytes 589856 | tf_op jit(solution)/shard_map/ppermute | solution.py:779
  625.5 23.9 %collective-permute-done.86.got_ref = bf16[48,768]{1,0:T(8,128)(2,1)S(1)} collective-permute-done((bf16[48,768]{1,0:T(8,128)(2,1)S(1)}, bf16[48,768]{1,0:T(8,128)(2,1)S(1)}, u32[]{:S(2)}, u32[]{:S(2)}) %collective-permute-start.86) | collective-permute-done | bytes 73760 | tf_op jit(solution)/shard_map/ppermute | solution.py:779
  661.0 2.7 collective-permute-done.89.got_ref
  669.1 2.8 finish_columns.3
  (514 shorter events, 214.2 us)
Async XLA Ops:
  1.8 42.9 %collective-permute-start = (bf16[1,96,2304]{2,1,0:T(8,128)(2,1)S(1)}, bf16[1,96,2304]{2,1,0:T(8,128)(2,1)S(1)}, u32[]{:S(2)}, u32[]{:S(2)}) collective-permute-start(bf16[1,96,2304]{2,1,0:T(8,128)(2,1)S(1)} %constant_dynamic-slice_fusion.7), channel_id=1, source_target_pairs={{0,1},{1,0},{2,3},{3,2},{4,5},{5,4},{6,7},{7,6},{8,9},{9,8},{10,11... | collective-permute-start | bytes 1327112 | tf_op jit(solution)/shard_map/ppermute | solution.py:779
  4.8 62.9 %collective-permute-start.6 = (bf16[1,96,768]{2,1,0:T(8,128)(2,1)S(1)}, bf16[1,96,768]{2,1,0:T(8,128)(2,1)}, u32[]{:S(2)}, u32[]{:S(2)}) collective-permute-start(bf16[1,96,768]{2,1,0:T(8,128)(2,1)S(1)} %constant_dynamic-slice_fusion.6), channel_id=1, source_target_pairs={{0,1},{1,0},{2,3},{3,2},{4,5},{5,4},{6,7},{7,6},{8,9},{9,8},{10,11... | collective-permute-start | bytes 442376 | tf_op jit(solution)/shard_map/ppermute | solution.py:779
  6.0 61.4 %collective-permute-start.10 = (bf16[1,96,3072]{2,1,0:T(8,128)(2,1)S(1)}, bf16[1,96,3072]{2,1,0:T(8,128)(2,1)S(1)}, u32[]{:S(2)}, u32[]{:S(2)}) collective-permute-start(bf16[1,96,3072]{2,1,0:T(8,128)(2,1)S(1)} %constant_dynamic-slice_fusion.5), channel_id=1, source_target_pairs={{0,1},{1,0},{2,3},{3,2},{4,5},{5,4},{6,7},{7,6},{8,9},{9,8},{10,11... | collective-permute-start | bytes 1769480 | tf_op jit(solution)/shard_map/ppermute | solution.py:779
  8.6 57.6 %collective-permute-start.14 = (bf16[1,384,768]{2,1,0:T(8,128)(2,1)S(1)}, bf16[1,384,768]{2,1,0:T(8,128)(2,1)S(1)}, u32[]{:S(2)}, u32[]{:S(2)}) collective-permute-start(bf16[1,384,768]{2,1,0:T(8,128)(2,1)S(1)} %constant_dynamic-slice_fusion.4), channel_id=1, source_target_pairs={{0,1},{1,0},{2,3},{3,2},{4,5},{5,4},{6,7},{7,6},{8,9},{9,8},{10,11... | collective-permute-start | bytes 1769480 | tf_op jit(solution)/shard_map/ppermute | solution.py:779
  10.4 32.6 %collective-permute-start.4 = (bf16[1,8064]{1,0:T(2,128)(2,1)S(1)}, bf16[1,8064]{1,0:T(2,128)(2,1)S(1)}, u32[]{:S(2)}, u32[]{:S(2)}) collective-permute-start(bf16[1,8064]{1,0:T(2,128)(2,1)S(1)} %broadcast_in_dim.16), channel_id=1, source_target_pairs={{0,1},{1,0},{2,3},{3,2},{4,5},{5,4},{6,7},{7,6},{8,9},{9,8},{10,11... | collective-permute-start | bytes 48392 | tf_op jit(solution)/shard_map/ppermute | solution.py:779
  66.2 20.9 %collective-permute-start.15 = (bf16[1,384,768]{2,1,0:T(8,128)(2,1)S(1)}, bf16[1,384,768]{2,1,0:T(8,128)(2,1)S(1)}, u32[]{:S(2)}, u32[]{:S(2)}) collective-permute-start(bf16[1,384,768]{2,1,0:T(8,128)(2,1)S(1)} %collective-permute-done.14.refs_12_.refs_2_), channel_id=1, source_target_pairs={{0,4},{2,6},{4,0},{6,2},{8,12},{10,14},{12,8},{14,10},{16,20},{18,... | collective-permute-start | bytes 1769480 | tf_op jit(solution)/shard_map/ppermute | solution.py:779
  67.5 26.1 %collective-permute-start.11 = (bf16[1,96,3072]{2,1,0:T(8,128)(2,1)S(1)}, bf16[1,96,3072]{2,1,0:T(8,128)(2,1)}, u32[]{:S(2)}, u32[]{:S(2)}) collective-permute-start(bf16[1,96,3072]{2,1,0:T(8,128)(2,1)S(1)} %collective-permute-done.10.refs_7_), channel_id=1, source_target_pairs={{0,4},{2,6},{4,0},{6,2},{8,12},{10,14},{12,8},{14,10},{16,20},{18,... | collective-permute-start | bytes 1769480 | tf_op jit(solution)/shard_map/ppermute | solution.py:779
  67.8 28.9 %collective-permute-start.7 = (bf16[1,96,768]{2,1,0:T(8,128)(2,1)}, bf16[1,96,768]{2,1,0:T(8,128)(2,1)S(1)}, u32[]{:S(2)}, u32[]{:S(2)}) collective-permute-start(bf16[1,96,768]{2,1,0:T(8,128)(2,1)} %collective-permute-done.6.refs_2_.refs_12_), channel_id=1, source_target_pairs={{0,4},{2,6},{4,0},{6,2},{8,12},{10,14},{12,8},{14,10},{16,20},{18,... | collective-permute-start | bytes 442376 | tf_op jit(solution)/shard_map/ppermute | solution.py:779
  104.9 31.9 %collective-permute-start.29 = (bf16[1,96,3072]{2,1,0:T(8,128)(2,1)S(1)}, bf16[1,96,3072]{2,1,0:T(8,128)(2,1)}, u32[]{:S(2)}, u32[]{:S(2)}) collective-permute-start(bf16[1,96,3072]{2,1,0:T(8,128)(2,1)S(1)} %constant_dynamic-slice_fusion.1), channel_id=1, source_target_pairs={{0,1},{1,0},{2,3},{3,2},{4,5},{5,4},{6,7},{7,6},{8,9},{9,8},{10,11... | collective-permute-start | bytes 1769480 | tf_op jit(solution)/shard_map/ppermute | solution.py:779
  106.1 29.1 %collective-permute-start.20 = (bf16[1,192,768]{2,1,0:T(8,128)(2,1)S(1)}, bf16[1,192,768]{2,1,0:T(8,128)(2,1)S(1)}, u32[]{:S(2)}, u32[]{:S(2)}) collective-permute-start(bf16[1,192,768]{2,1,0:T(8,128)(2,1)S(1)} %collective-permute-done.19.refs_2_.refs_7_), channel_id=1, source_target_pairs={{0,4},{2,6},{4,0},{6,2},{8,12},{10,14},{12,8},{14,10},{16,20},{18,... | collective-permute-start | bytes 884744 | tf_op jit(solution)/shard_map/ppermute | solution.py:779
  106.4 27.6 %collective-permute-start.24 = (bf16[1,96,2304]{2,1,0:T(8,128)(2,1)S(1)}, bf16[1,96,2304]{2,1,0:T(8,128)(2,1)S(1)}, u32[]{:S(2)}, u32[]{:S(2)}) collective-permute-start(bf16[1,96,2304]{2,1,0:T(8,128)(2,1)S(1)} %collective-permute-done.23.refs_7_.refs_2_), channel_id=1, source_target_pairs={{0,4},{2,6},{4,0},{6,2},{8,12},{10,14},{12,8},{14,10},{16,20},{18,... | collective-permute-start | bytes 1327112 | tf_op jit(solution)/shard_map/ppermute | solution.py:779
  142.2 31.0 %collective-permute-start.30 = (bf16[1,96,3072]{2,1,0:T(8,128)(2,1)}, bf16[1,96,3072]{2,1,0:T(8,128)(2,1)S(1)}, u32[]{:S(2)}, u32[]{:S(2)}) collective-permute-start(bf16[1,96,3072]{2,1,0:T(8,128)(2,1)} %collective-permute-done.29.refs_7_), channel_id=1, source_target_pairs={{0,4},{2,6},{4,0},{6,2},{8,12},{10,14},{12,8},{14,10},{16,20},{18,... | collective-permute-start | bytes 1769480 | tf_op jit(solution)/shard_map/ppermute | solution.py:779
  142.5 32.2 %collective-permute-start.18 = (bf16[1,96,768]{2,1,0:T(8,128)(2,1)}, bf16[1,96,768]{2,1,0:T(8,128)(2,1)S(1)}, u32[]{:S(2)}, u32[]{:S(2)}) collective-permute-start(bf16[1,96,768]{2,1,0:T(8,128)(2,1)} %collective-permute-done.5.refs_2_.refs_12_), channel_id=1, source_target_pairs={{0,4},{2,6},{4,0},{6,2},{8,12},{10,14},{12,8},{14,10},{16,20},{18,... | collective-permute-start | bytes 442376 | tf_op jit(solution)/shard_map/ppermute | solution.py:779
  156.6 22.5 %collective-permute-start.31 = (bf16[1,96,3072]{2,1,0:T(8,128)(2,1)}, bf16[1,96,3072]{2,1,0:T(8,128)(2,1)}, u32[]{:S(2)}, u32[]{:S(2)}) collective-permute-start(bf16[1,96,3072]{2,1,0:T(8,128)(2,1)} %collective-permute-done.29.refs_7_), channel_id=1, source_target_pairs={{0,2},{2,0},{4,6},{6,4},{8,10},{10,8},{12,14},{14,12},{16,18},{18,... | collective-permute-start | bytes 1769480 | tf_op jit(solution)/shard_map/ppermute | solution.py:779
  273.3 27.5 %collective-permute-start.42 = (bf16[1,768,768]{2,1,0:T(8,128)(2,1)S(1)}, bf16[1,768,768]{2,1,0:T(8,128)(2,1)S(1)}, u32[]{:S(2)}, u32[]{:S(2)}) collective-permute-start(bf16[1,768,768]{2,1,0:T(8,128)(2,1)S(1)} %get-tuple-element.464), channel_id=1, source_target_pairs={{0,1},{1,0},{2,3},{3,2},{4,5},{5,4},{6,7},{7,6},{8,9},{9,8},{10,11... | collective-permute-start | bytes 3538952 | tf_op jit(solution)/shard_map/ppermute | solution.py:779
  274.4 51.8 %collective-permute-start.43 = (bf16[1,768,768]{2,1,0:T(8,128)(2,1)S(1)}, bf16[1,768,768]{2,1,0:T(8,128)(2,1)}, u32[]{:S(2)}, u32[]{:S(2)}) collective-permute-start(bf16[1,768,768]{2,1,0:T(8,128)(2,1)S(1)} %get-tuple-element.480), channel_id=1, source_target_pairs={{0,1},{1,0},{2,3},{3,2},{4,5},{5,4},{6,7},{7,6},{8,9},{9,8},{10,11... | collective-permute-start | bytes 3538952 | tf_op jit(solution)/shard_map/ppermute | solution.py:779
  299.3 35.0 %collective-permute-start.41 = (bf16[2,384,768]{2,1,0:T(8,128)(2,1)}, bf16[2,384,768]{2,1,0:T(8,128)(2,1)}, u32[]{:S(2)}, u32[]{:S(2)}) collective-permute-start(bf16[2,384,768]{2,1,0:T(8,128)(2,1)} %bitcast.34), channel_id=1, source_target_pairs={{0,2},{2,0},{4,6},{6,4},{8,10},{10,8},{12,14},{14,12},{16,18},{18,... | collective-permute-start | bytes 3538952 | tf_op jit(solution)/shard_map/ppermute | solution.py:779
  376.2 37.1 %collective-permute-start.49 = (bf16[2,768,768]{2,1,0:T(8,128)(2,1)S(1)}, bf16[2,768,768]{2,1,0:T(8,128)(2,1)}, u32[]{:S(2)}, u32[]{:S(2)}) collective-permute-start(bf16[2,768,768]{2,1,0:T(8,128)(2,1)S(1)} %bitcast.171), channel_id=1, source_target_pairs={{0,2},{2,0},{4,6},{6,4},{8,10},{10,8},{12,14},{14,12},{16,18},{18,... | collective-permute-start | bytes 7077896 | tf_op jit(solution)/shard_map/ppermute | solution.py:779
  376.3 27.3 %collective-permute-start.50 = (bf16[1,768,768]{2,1,0:T(8,128)(2,1)S(1)}, bf16[1,768,768]{2,1,0:T(8,128)(2,1)}, u32[]{:S(2)}, u32[]{:S(2)}) collective-permute-start(bf16[1,768,768]{2,1,0:T(8,128)(2,1)S(1)} %get-tuple-element.526), channel_id=1, source_target_pairs={{0,4},{2,6},{4,0},{6,2},{8,12},{10,14},{12,8},{14,10},{16,20},{18,... | collective-permute-start | bytes 3538952 | tf_op jit(solution)/shard_map/ppermute | solution.py:779
  379.0 41.2 %collective-permute-start.46 = (bf16[1,384,768]{2,1,0:T(8,128)(2,1)}, bf16[1,384,768]{2,1,0:T(8,128)(2,1)}, u32[]{:S(2)}, u32[]{:S(2)}) collective-permute-start(bf16[1,384,768]{2,1,0:T(8,128)(2,1)} %copy-done.5), channel_id=1, source_target_pairs={{0,1},{1,0},{2,3},{3,2},{4,5},{5,4},{6,7},{7,6},{8,9},{9,8},{10,11... | collective-permute-start | bytes 1769480 | tf_op jit(solution)/shard_map/ppermute | solution.py:779
  380.2 40.0 %collective-permute-start.45 = (bf16[1,384,768]{2,1,0:T(8,128)(2,1)}, bf16[1,384,768]{2,1,0:T(8,128)(2,1)}, u32[]{:S(2)}, u32[]{:S(2)}) collective-permute-start(bf16[1,384,768]{2,1,0:T(8,128)(2,1)} %copy-done.4), channel_id=1, source_target_pairs={{0,1},{1,0},{2,3},{3,2},{4,5},{5,4},{6,7},{7,6},{8,9},{9,8},{10,11... | collective-permute-start | bytes 1769480 | tf_op jit(solution)/shard_map/ppermute | solution.py:779
  381.9 35.9 %collective-permute-start.48 = (bf16[2,384,768]{2,1,0:T(8,128)(2,1)}, bf16[2,384,768]{2,1,0:T(8,128)(2,1)}, u32[]{:S(2)}, u32[]{:S(2)}) collective-permute-start(bf16[2,384,768]{2,1,0:T(8,128)(2,1)} %copy-done.1), channel_id=1, source_target_pairs={{0,8},{2,10},{4,12},{6,14},{8,0},{10,2},{12,4},{14,6},{16,24},{18,... | collective-permute-start | bytes 3538952 | tf_op jit(solution)/shard_map/ppermute | solution.py:779
  413.3 47.8 %collective-permute-start.51 = (bf16[1,384,768]{2,1,0:T(8,128)(2,1)}, bf16[1,384,768]{2,1,0:T(8,128)(2,1)}, u32[]{:S(2)}, u32[]{:S(2)}) collective-permute-start(bf16[1,384,768]{2,1,0:T(8,128)(2,1)} %get-tuple-element.557), channel_id=1, source_target_pairs={{0,8},{2,10},{4,12},{6,14},{8,0},{10,2},{12,4},{14,6},{16,24},{18,... | collective-permute-start | bytes 1769480 | tf_op jit(solution)/shard_map/ppermute | solution.py:779
  417.8 49.3 %collective-permute-start.55 = (bf16[2,384,768]{2,1,0:T(8,128)(2,1)S(1)}, bf16[2,384,768]{2,1,0:T(8,128)(2,1)S(1)}, u32[]{:S(2)}, u32[]{:S(2)}) collective-permute-start(bf16[2,384,768]{2,1,0:T(8,128)(2,1)S(1)} %get-tuple-element.560), channel_id=1, source_target_pairs={{0,8},{2,10},{4,12},{6,14},{8,0},{10,2},{12,4},{14,6},{16,24},{18,... | collective-permute-start | bytes 3538952 | tf_op jit(solution)/shard_map/ppermute | solution.py:779
  423.8 38.8 %collective-permute-start.56 = (bf16[1,576,768]{2,1,0:T(8,128)(2,1)}, bf16[1,576,768]{2,1,0:T(8,128)(2,1)}, u32[]{:S(2)}, u32[]{:S(2)}) collective-permute-start(bf16[1,576,768]{2,1,0:T(8,128)(2,1)} %get-tuple-element.570), channel_id=1, source_target_pairs={{0,4},{2,6},{4,0},{6,2},{8,12},{10,14},{12,8},{14,10},{16,20},{18,... | collective-permute-start | bytes 2654216 | tf_op jit(solution)/shard_map/ppermute | solution.py:779
  447.2 22.3 %collective-permute-start.54 = (bf16[2,384,768]{2,1,0:T(8,128)(2,1)}, bf16[2,384,768]{2,1,0:T(8,128)(2,1)}, u32[]{:S(2)}, u32[]{:S(2)}) collective-permute-start(bf16[2,384,768]{2,1,0:T(8,128)(2,1)} %get-tuple-element.582), channel_id=1, source_target_pairs={{0,2},{2,0},{4,6},{6,4},{8,10},{10,8},{12,14},{14,12},{16,18},{18,... | collective-permute-start | bytes 3538952 | tf_op jit(solution)/shard_map/ppermute | solution.py:779
  451.5 20.8 %collective-permute-start.53 = (bf16[2,384,768]{2,1,0:T(8,128)(2,1)S(1)}, bf16[2,384,768]{2,1,0:T(8,128)(2,1)}, u32[]{:S(2)}, u32[]{:S(2)}) collective-permute-start(bf16[2,384,768]{2,1,0:T(8,128)(2,1)S(1)} %get-tuple-element.593), channel_id=1, source_target_pairs={{0,2},{2,0},{4,6},{6,4},{8,10},{10,8},{12,14},{14,12},{16,18},{18,... | collective-permute-start | bytes 3538952 | tf_op jit(solution)/shard_map/ppermute | solution.py:779
  461.1 43.2 %collective-permute-start.58 = (bf16[1,384,768]{2,1,0:T(8,128)(2,1)}, bf16[1,384,768]{2,1,0:T(8,128)(2,1)}, u32[]{:S(2)}, u32[]{:S(2)}) collective-permute-start(bf16[1,384,768]{2,1,0:T(8,128)(2,1)} %get-tuple-element.563), channel_id=1, source_target_pairs={{0,1},{1,0},{2,3},{3,2},{4,5},{5,4},{6,7},{7,6},{8,9},{9,8},{10,11... | collective-permute-start | bytes 1769480 | tf_op jit(solution)/shard_map/ppermute | solution.py:779
  467.1 34.8 %collective-permute-start.60 = (bf16[1,288,768]{2,1,0:T(8,128)(2,1)}, bf16[1,288,768]{2,1,0:T(8,128)(2,1)}, u32[]{:S(2)}, u32[]{:S(2)}) collective-permute-start(bf16[1,288,768]{2,1,0:T(8,128)(2,1)} %get-tuple-element.598), channel_id=1, source_target_pairs={{0,8},{2,10},{4,12},{6,14},{8,0},{10,2},{12,4},{14,6},{16,24},{18,... | collective-permute-start | bytes 1327112 | tf_op jit(solution)/shard_map/ppermute | solution.py:779
  469.5 37.2 %collective-permute-start.59 = (bf16[1,384,768]{2,1,0:T(8,128)(2,1)}, bf16[1,384,768]{2,1,0:T(8,128)(2,1)S(1)}, u32[]{:S(2)}, u32[]{:S(2)}) collective-permute-start(bf16[1,384,768]{2,1,0:T(8,128)(2,1)} %get-tuple-element.601), channel_id=1, source_target_pairs={{0,1},{1,0},{2,3},{3,2},{4,5},{5,4},{6,7},{7,6},{8,9},{9,8},{10,11... | collective-permute-start | bytes 1769480 | tf_op jit(solution)/shard_map/ppermute | solution.py:779
  474.1 34.1 %collective-permute-start.66 = (bf16[2,192,768]{2,1,0:T(8,128)(2,1)S(1)}, bf16[2,192,768]{2,1,0:T(8,128)(2,1)S(1)}, u32[]{:S(2)}, u32[]{:S(2)}) collective-permute-start(bf16[2,192,768]{2,1,0:T(8,128)(2,1)S(1)} %get-tuple-element.607), channel_id=1, source_target_pairs={{0,8},{2,10},{4,12},{6,14},{8,0},{10,2},{12,4},{14,6},{16,24},{18,... | collective-permute-start | bytes 1769480 | tf_op jit(solution)/shard_map/ppermute | solution.py:779
  477.9 21.0 %collective-permute-start.61 = (bf16[192,768]{1,0:T(8,128)(2,1)S(1)}, bf16[192,768]{1,0:T(8,128)(2,1)S(1)}, u32[]{:S(2)}, u32[]{:S(2)}) collective-permute-start(bf16[192,768]{1,0:T(8,128)(2,1)S(1)} %add_convert_fusion.1.own_ref), channel_id=1, source_target_pairs={{0,16},{2,18},{4,20},{6,22},{8,24},{10,26},{12,28},{14,30},{16,0},... | collective-permute-start | bytes 884744 | tf_op jit(solution)/shard_map/ppermute | solution.py:779
  501.9 27.7 %collective-permute-start.63 = (bf16[1,384,768]{2,1,0:T(8,128)(2,1)S(1)}, bf16[1,384,768]{2,1,0:T(8,128)(2,1)S(1)}, u32[]{:S(2)}, u32[]{:S(2)}) collective-permute-start(bf16[1,384,768]{2,1,0:T(8,128)(2,1)S(1)} %get-tuple-element.604), channel_id=1, source_target_pairs={{0,1},{1,0},{2,3},{3,2},{4,5},{5,4},{6,7},{7,6},{8,9},{9,8},{10,11... | collective-permute-start | bytes 1769480 | tf_op jit(solution)/shard_map/ppermute | solution.py:779
  515.2 40.4 %collective-permute-start.69 = (bf16[768,768]{1,0:T(8,128)(2,1)S(1)}, bf16[768,768]{1,0:T(8,128)(2,1)S(1)}, u32[]{:S(2)}, u32[]{:S(2)}) collective-permute-start(bf16[768,768]{1,0:T(8,128)(2,1)S(1)} %bitcast.162), channel_id=1, source_target_pairs={{0,4},{2,6},{4,0},{6,2},{8,12},{10,14},{12,8},{14,10},{16,20},{18,... | collective-permute-start | bytes 3538952 | tf_op jit(solution)/shard_map/ppermute | solution.py:779
  515.7 39.6 %collective-permute-start.72 = (bf16[1,384,768]{2,1,0:T(8,128)(2,1)S(1)}, bf16[1,384,768]{2,1,0:T(8,128)(2,1)S(1)}, u32[]{:S(2)}, u32[]{:S(2)}) collective-permute-start(bf16[1,384,768]{2,1,0:T(8,128)(2,1)S(1)} %get-tuple-element.634), channel_id=1, source_target_pairs={{0,4},{2,6},{4,0},{6,2},{8,12},{10,14},{12,8},{14,10},{16,20},{18,... | collective-permute-start | bytes 1769480 | tf_op jit(solution)/shard_map/ppermute | solution.py:779
  517.0 38.3 %collective-permute-start.62 = (f32[2,8064]{1,0:T(2,128)S(1)}, f32[2,8064]{1,0:T(2,128)S(1)}, u32[]{:S(2)}, u32[]{:S(2)}) collective-permute-start(f32[2,8064]{1,0:T(2,128)S(1)} %add.69), channel_id=1, source_target_pairs={{0,4},{2,6},{4,0},{6,2},{8,12},{10,14},{12,8},{14,10},{16,20},{18,... | collective-permute-start | bytes 193544 | tf_op jit(solution)/shard_map/ppermute | solution.py:779
  528.3 27.2 %collective-permute-start.71 = (bf16[1,192,768]{2,1,0:T(8,128)(2,1)S(1)}, bf16[1,192,768]{2,1,0:T(8,128)(2,1)S(1)}, u32[]{:S(2)}, u32[]{:S(2)}) collective-permute-start(bf16[1,192,768]{2,1,0:T(8,128)(2,1)S(1)} %get-tuple-element.642), channel_id=1, source_target_pairs={{0,1},{1,0},{2,3},{3,2},{4,5},{5,4},{6,7},{7,6},{8,9},{9,8},{10,11... | collective-permute-start | bytes 884744 | tf_op jit(solution)/shard_map/ppermute | solution.py:779
  529.6 26.0 %collective-permute-start.70 = (bf16[144,768]{1,0:T(8,128)(2,1)S(1)}, bf16[144,768]{1,0:T(8,128)(2,1)S(1)}, u32[]{:S(2)}, u32[]{:S(2)}) collective-permute-start(bf16[144,768]{1,0:T(8,128)(2,1)S(1)} %add_convert_fusion.2.own_ref), channel_id=1, source_target_pairs={{0,16},{2,18},{4,20},{6,22},{8,24},{10,26},{12,28},{14,30},{16,0},... | collective-permute-start | bytes 663560 | tf_op jit(solution)/shard_map/ppermute | solution.py:779
  555.8 18.9 %collective-permute-start.76 = (bf16[1536,768]{1,0:T(8,128)(2,1)S(1)}, bf16[1536,768]{1,0:T(8,128)(2,1)S(1)}, u32[]{:S(2)}, u32[]{:S(2)}) collective-permute-start(bf16[1536,768]{1,0:T(8,128)(2,1)S(1)} %bitcast.153), channel_id=1, source_target_pairs={{0,2},{2,0},{4,6},{6,4},{8,10},{10,8},{12,14},{14,12},{16,18},{18,... | collective-permute-start | bytes 7077896 | tf_op jit(solution)/shard_map/ppermute | solution.py:779
  566.9 17.0 %collective-permute-start.75 = (bf16[288,768]{1,0:T(8,128)(2,1)S(1)}, bf16[288,768]{1,0:T(8,128)(2,1)S(1)}, u32[]{:S(2)}, u32[]{:S(2)}) collective-permute-start(bf16[288,768]{1,0:T(8,128)(2,1)S(1)} %bitcast.198), channel_id=1, source_target_pairs={{0,8},{2,10},{4,12},{6,14},{8,0},{10,2},{12,4},{14,6},{16,24},{18,... | collective-permute-start | bytes 1327112 | tf_op jit(solution)/shard_map/ppermute | solution.py:779
  584.0 22.1 %collective-permute-start.81 = (bf16[576,768]{1,0:T(8,128)(2,1)S(1)}, bf16[576,768]{1,0:T(8,128)(2,1)S(1)}, u32[]{:S(2)}, u32[]{:S(2)}) collective-permute-start(bf16[576,768]{1,0:T(8,128)(2,1)S(1)} %bitcast.182), channel_id=1, source_target_pairs={{0,4},{2,6},{4,0},{6,2},{8,12},{10,14},{12,8},{14,10},{16,20},{18,... | collective-permute-start | bytes 2654216 | tf_op jit(solution)/shard_map/ppermute | solution.py:779
  585.1 19.4 %collective-permute-start.83 = (bf16[192,768]{1,0:T(8,128)(2,1)S(1)}, bf16[192,768]{1,0:T(8,128)(2,1)S(1)}, u32[]{:S(2)}, u32[]{:S(2)}) collective-permute-start(bf16[192,768]{1,0:T(8,128)(2,1)S(1)} %add_convert_fusion.own_ref), channel_id=1, source_target_pairs={{0,16},{2,18},{4,20},{6,22},{8,24},{10,26},{12,28},{14,30},{16,0},... | collective-permute-start | bytes 884744 | tf_op jit(solution)/shard_map/ppermute | solution.py:779
  587.0 17.5 %collective-permute-start.73 = (f32[2,8064]{1,0:T(2,128)S(1)}, f32[2,8064]{1,0:T(2,128)S(1)}, u32[]{:S(2)}, u32[]{:S(2)}) collective-permute-start(f32[2,8064]{1,0:T(2,128)S(1)} %add.72), channel_id=1, source_target_pairs={{0,16},{2,18},{4,20},{6,22},{8,24},{10,26},{12,28},{14,30},{16,0},... | collective-permute-start | bytes 193544 | tf_op jit(solution)/shard_map/ppermute | solution.py:779
  587.5 18.5 %collective-permute-start.82 = (bf16[1,48,768]{2,1,0:T(8,128)(2,1)S(1)}, bf16[1,48,768]{2,1,0:T(8,128)(2,1)S(1)}, u32[]{:S(2)}, u32[]{:S(2)}) collective-permute-start(bf16[1,48,768]{2,1,0:T(8,128)(2,1)S(1)} %get-tuple-element.677), channel_id=1, source_target_pairs={{0,16},{2,18},{4,20},{6,22},{8,24},{10,26},{12,28},{14,30},{16,0},... | collective-permute-start | bytes 221192 | tf_op jit(solution)/shard_map/ppermute | solution.py:779
  606.2 43.2 %collective-permute-start.85 = (bf16[1152,768]{1,0:T(8,128)(2,1)S(1)}, bf16[1152,768]{1,0:T(8,128)(2,1)S(1)}, u32[]{:S(2)}, u32[]{:S(2)}) collective-permute-start(bf16[1152,768]{1,0:T(8,128)(2,1)S(1)} %bitcast.158), channel_id=1, source_target_pairs={{0,2},{2,0},{4,6},{6,4},{8,10},{10,8},{12,14},{14,12},{16,18},{18,... | collective-permute-start | bytes 5308424 | tf_op jit(solution)/shard_map/ppermute | solution.py:779
  623.0 32.8 %collective-permute-start.90 = (bf16[768,768]{1,0:T(8,128)(2,1)S(1)}, bf16[768,768]{1,0:T(8,128)(2,1)S(1)}, u32[]{:S(2)}, u32[]{:S(2)}) collective-permute-start(bf16[768,768]{1,0:T(8,128)(2,1)S(1)} %bitcast.164), channel_id=1, source_target_pairs={{0,8},{2,10},{4,12},{6,14},{8,0},{10,2},{12,4},{14,6},{16,24},{18,... | collective-permute-start | bytes 3538952 | tf_op jit(solution)/shard_map/ppermute | solution.py:779
  623.1 26.3 %collective-permute-start.86 = (bf16[48,768]{1,0:T(8,128)(2,1)S(1)}, bf16[48,768]{1,0:T(8,128)(2,1)S(1)}, u32[]{:S(2)}, u32[]{:S(2)}) collective-permute-start(bf16[48,768]{1,0:T(8,128)(2,1)S(1)} %add_convert_fusion.4.own_ref), channel_id=1, source_target_pairs={{0,16},{2,18},{4,20},{6,22},{8,24},{10,26},{12,28},{14,30},{16,0},... | collective-permute-start | bytes 221192 | tf_op jit(solution)/shard_map/ppermute | solution.py:779
  624.9 30.9 %collective-permute-start.84 = (bf16[48,768]{1,0:T(8,128)(2,1)S(1)}, bf16[48,768]{1,0:T(8,128)(2,1)S(1)}, u32[]{:S(2)}, u32[]{:S(2)}) collective-permute-start(bf16[48,768]{1,0:T(8,128)(2,1)S(1)} %add_convert_fusion.3.own_ref), channel_id=1, source_target_pairs={{0,16},{2,18},{4,20},{6,22},{8,24},{10,26},{12,28},{14,30},{16,0},... | collective-permute-start | bytes 221192 | tf_op jit(solution)/shard_map/ppermute | solution.py:779
  (144 other events, 1121.0 us)

commit v4 on v3

--- a/solution.py
+++ b/solution.py
@@ -47,7 +47,7 @@
 
 
 def cost(micros):
-    return pl.CostEstimate(flops=int(micros * 10**9), bytes_accessed=10**5, transcendentals=0)
+    return pl.CostEstimate(flops=int(micros * 3 * 10**8), bytes_accessed=0, transcendentals=0)
 
 
 def call(body, grid, ins, outs, name, micros, scratch=(), limit=56):
@@ -539,13 +539,24 @@
     )(which, *[array for array, _ in ins])
 
 
+def quarters(rows, width, narrow_rows):
+    shape = (lax.axis_size("narrow") // 2 * narrow_rows, width)
+    return [(shape, low, pl.BlockSpec(shape, lambda g, core: (0, 0)))] * 4
+
+
 def up_term(left, right, core):
     rows, width = left.shape
-    shares = lax.axis_size("narrow")
-    part = width // shares
-
-    def body(core_ref, l_ref, r_ref, out_ref):
-        out_ref[...] = dot(l_ref[...], r_ref[...], (0, 0)).astype(low).reshape(shares, 1, part, width)
+    part = width // lax.axis_size("narrow")
+    half = width // 2
+
+    def body(core_ref, l_ref, r_ref, *outs):
+        value = dot(l_ref[...], r_ref[...], (0, 0)).astype(low)
+        for block in range(2):
+
+            @pl.when(pl.program_id(0) == block)
+            def _():
+                outs[block][...] = value[:half]
+                outs[2 + block][...] = value[half:]
 
     return picked(
         body,
@@ -555,39 +566,39 @@
             (left, pl.BlockSpec((rows, width), lambda g, core: (0, 0))),
             (right, pl.BlockSpec((rows, width), lambda g, core: (0, core[0] * 2 + g))),
         ],
-        [((shares, 2, part, width), low, pl.BlockSpec((shares, 1, part, width), lambda g, core: (0, g, 0, 0)))],
+        quarters(rows, width, part),
         "up_term",
         3.5,
-    )[0].reshape(shares, 2 * part, width)
+    )
 
 
 def qkv_out_term(first, packed, mixed, branch, core):
     rows, width = first.shape
-    shares = lax.axis_size("narrow")
-    part = width // shares
-
-    def body(core_ref, l_ref, r_ref, o_ref, b_ref, one_ref, two_ref):
+    part = width // lax.axis_size("narrow")
+    half = width // 2
+
+    def body(core_ref, l_ref, r_ref, o_ref, b_ref, *outs):
         step = pl.program_id(0)
         last = core_ref[0] * 2 + step == 3
 
+        def put(block, value):
+            outs[block][...] = value[:half]
+            outs[2 + block][...] = value[half:]
+
         @pl.when(last)
         def _():
-            two_ref[...] = dot(o_ref[...], b_ref[...], (0, 0)).astype(low).reshape(shares, part, width)
+            put(1, dot(o_ref[...], b_ref[...], (0, 0)).astype(low))
 
         @pl.when(jnp.logical_not(last))
         def _():
-            value = dot(l_ref[...], r_ref[0], (0, 0)).astype(low).reshape(shares, part, width)
-
-            @pl.when(step == 0)
-            def _():
-                one_ref[...] = value
-
-            @pl.when(step == 1)
-            def _():
-                two_ref[...] = value
+            value = dot(l_ref[...], r_ref[0], (0, 0)).astype(low)
+            for block in range(2):
+
+                @pl.when(step == block)
+                def _():
+                    put(block, value)
 
     flat = pl.BlockSpec((rows, width), lambda g, core: (0, 0))
-    out = ((shares, part, width), low, pl.BlockSpec((shares, part, width), lambda g, core: (0, 0, 0)))
     return picked(
         body,
         core,
@@ -598,7 +609,7 @@
             (mixed, flat),
             (branch, flat),
         ],
-        [out, out],
+        quarters(rows, width, part),
         "qkv_out_term",
         3.5,
     )
@@ -610,25 +621,32 @@
     part = left.shape[1] // (2 * shares)
     direct = part == width
     if not direct:
-        left = left.reshape(rows, shares, 2, part)
-        left = lax.dynamic_index_in_dim(left, core[0], 2, keepdims=False).reshape(rows, shares * part)
-    steps = shares * part // width
-
-    def body(core_ref, l_ref, r_ref, out_ref):
-        out_ref[...] = dot(l_ref[...], r_ref[...], (0, 0)).astype(low)
+        left = left.reshape(rows, shares, 2, 2, part // 2)
+        left = lax.dynamic_index_in_dim(left, core[0], 2, keepdims=False)
+        left = left.reshape(rows, 2, shares // 2, 2, part // 2).swapaxes(2, 3).reshape(rows, 2 * width)
+    half = width // 2
+
+    def body(core_ref, l_ref, r_ref, *outs):
+        value = dot(l_ref[...], r_ref[...], (0, 0)).astype(low)
+        for owner in range(2):
+
+            @pl.when(pl.program_id(0) == owner)
+            def _():
+                outs[2 * owner][...] = value[:half]
+                outs[2 * owner + 1][...] = value[half:]
 
     return picked(
         body,
         core,
-        (steps,),
+        (2,),
         [
             (left, pl.BlockSpec((rows, width), lambda g, core: (0, g * 2 + core[0] if direct else g))),
             (right, pl.BlockSpec((rows, width), lambda g, core: (0, 0))),
         ],
-        [((shares * part, width), low, pl.BlockSpec((width, width), lambda g, core: (g, 0)))],
+        quarters(rows, width, part // 2),
         "down_term",
         3.5,
-    )[0].reshape(shares, part, width)
+    )
 
 
 def join_term(middle, skip, right, core):
@@ -637,13 +655,16 @@
     part = width // shares
     half = width // 2
     if part != half:
-        left = jnp.concatenate([middle, skip], axis=1).reshape(rows, shares, 2, part)
-        left = lax.dynamic_index_in_dim(left, core[0], 2, keepdims=False).reshape(rows, shares * part)
+        left = jnp.concatenate([middle, skip], axis=1).reshape(rows, shares, 2, 2, part // 2)
+        left = lax.dynamic_index_in_dim(left, core[0], 2, keepdims=False)
+        left = left.reshape(rows, 2, shares // 2, 2, part // 2).swapaxes(2, 3).reshape(rows, width)
         middle, skip = left[:, :half], left[:, half:]
 
-    def body(core_ref, m_ref, s_ref, r_ref, out_ref):
-        out_ref[:half] = dot(m_ref[...], r_ref[...], (0, 0)).astype(low)
-        out_ref[half:] = dot(s_ref[...], r_ref[...], (0, 0)).astype(low)
+    def body(core_ref, m_ref, s_ref, r_ref, *outs):
+        for owner, left_ref in enumerate((m_ref, s_ref)):
+            value = dot(left_ref[...], r_ref[...], (0, 0)).astype(low)
+            outs[2 * owner][...] = value[: half // 2]
+            outs[2 * owner + 1][...] = value[half // 2 :]
 
     side = pl.BlockSpec((rows, half), lambda g, core: (0, core[0] if part == half else 0))
     return picked(
@@ -651,10 +672,35 @@
         core,
         (1,),
         [(middle, side), (skip, side), (right, pl.BlockSpec((rows, width), lambda g, core: (0, 0)))],
-        [((width, width), low, pl.BlockSpec((width, width), lambda g, core: (0, 0)))],
+        quarters(rows, width, part // 2),
         "join_term",
         2,
-    )[0].reshape(shares, part, width)
+    )
+
+
+def cross(bit, *pieces):
+    kept, got = pieces[:4], pieces[4:]
+    rows, columns = kept[0].shape
+    steps = 2 if rows % 32 == 0 else 1
+
+    def body(bit_ref, *refs):
+        sent_ref, left_ref = refs[8:]
+
+        def put(target, owner):
+            for block in range(2):
+                one, two = refs[2 * owner + block], refs[4 + 2 * owner + block]
+                target[block] = (one[...].astype(full) + two[...].astype(full)).astype(low)
+
+        for mine in range(2):
+
+            @pl.when(bit_ref[0] == mine)
+            def _():
+                put(sent_ref, 1 - mine)
+                put(left_ref, mine)
+
+    ins = [(piece, pl.BlockSpec((rows // steps, columns), lambda g, bit: (g, 0))) for piece in kept + got]
+    out = ((2, rows, columns), low, pl.BlockSpec((2, rows // steps, columns), lambda g, bit: (0, g, 0)))
+    return picked(body, bit, (steps,), ins, [out, out], "cross", 2.5)
 
 
 def add_halve(bit, *pairs):
@@ -793,84 +839,107 @@
         self.last = (jax.tree.leaves(out)[0],)
         return out
 
+    def hold(self, *arrays):
+        self.last += arrays
+
 
 def place_bit(axis, mask):
     return ((lax.axis_index(axis) & mask) // mask).astype(jnp.int32).reshape(1)
 
 
 class Term:
-    def __init__(self, kind, layer, half, kept, got, core):
-        self.kind, self.layer, self.half, self.kept, self.got, self.core = kind, layer, half, kept, got, core
-
-
-def terms_of(order, kind, layer, function, *arrays):
-    core = place_bit("wide", 1)
-    sent = order.run(lambda *x: function(*x, 1 - core), *arrays)
-    got = jax.tree.map(lambda each: swap(each, "wide", 1), sent)
-    kept = order.run(lambda *x: function(*x, core), *arrays)
-    if isinstance(kept, (tuple, list)):
-        return [Term(kind, layer, place, kept[place], got[place], core) for place in range(len(kept))]
-    return [Term(kind, layer, None, kept, got, core)]
+    def __init__(self, order, kind, layer, function, *arrays):
+        self.order, self.kind, self.layer = order, kind, layer
+        self.core = place_bit("wide", 1)
+        sent = order.run(lambda *x: function(*x, 1 - self.core), *arrays)
+        self.got = [swap(each, "wide", 1) for each in sent]
+        self.columns = sent[0].shape[-1]
+        self.keep = lambda: order.run(lambda *x: function(*x, self.core), *arrays)
+
+    def stay(self):
+        self.kept, self.keep = self.keep(), None
+
+    def pass_narrow(self):
+        stages = list(reversed(masks("narrow")))
+        if self.keep:
+            self.stay()
+        bit = place_bit("narrow", stages[0])
+        sent, self.kept = self.order.run(lambda *x: cross(bit, *x), *self.kept, *self.got)
+        self.got = swap(sent, "narrow", stages[0])
+        for mask in stages[1:]:
+            self.kept, self.got = halve(self.order, "narrow", mask, 2, [(self.kept, self.got)], self.columns)
+
+
+    def pass_wide(self, mask):
+        self.kept, self.got = halve(self.order, "wide", mask, 1, [(self.kept, self.got)], self.columns)
+
+
+def halve(order, axis, mask, lead, pairs, columns):
+    shaped = [array.reshape(lead, 2, -1, columns) for pair in pairs for array in pair]
+    bit = place_bit(axis, mask)
+    sent, kept = order.run(lambda *x: add_halve(bit, *x), *shaped)
+    return kept, swap(sent, axis, mask)
 
 
 class Reduce:
-    def __init__(self, order, terms, first=()):
+    def __init__(self, order, terms, passed=()):
         self.order, self.terms = order, terms
-        wide = [("wide", mask) for mask in masks("wide")[1:]]
-        narrow = [("narrow", mask) for mask in reversed(masks("narrow"))]
-        early = [stage for stage in wide if stage[1] in first]
-        late = [stage for stage in wide if stage[1] not in first]
-        self.early, self.down, self.up = early + narrow, late, list(reversed(early))
-        self.pieces = 2 ** len(early)
-        self.columns = terms[0].kept.shape[-1]
-        self.passed = [0] * len(terms)
+        self.down = [mask for mask in masks("wide")[1:] if mask not in passed]
+        self.up = list(reversed(passed))
+        self.pieces, self.columns = 2 ** len(passed), terms[0].columns
         self.parts = [(term.kept, term.got) for term in terms]
-        self.joining, self.lengths, self.closed = None, None, False
-
-    def halve(self, axis, mask, lead, pairs):
-        shaped = [array.reshape(lead, 2, -1, self.columns) for pair in pairs for array in pair]
-        bit = place_bit(axis, mask)
-        sent, kept = self.order.run(lambda *x: add_halve(bit, *x), *shaped)
-        return kept, swap(sent, axis, mask)
-
-    def apart(self, place=0):
-        axis, mask = self.early[self.passed[place]]
-        self.passed[place] += 1
-        lead = lax.axis_size("narrow") if axis == "wide" else 1
-        self.parts[place] = self.halve(axis, mask, lead, [self.parts[place]])
-        if axis == "narrow" and self.passed[place] < len(self.early):
-            self.apart(place)
+        self.lengths, self.first = [each.size // self.columns for each, _ in self.parts], True
+        self.joining, self.closed = None, False
 
     def step(self):
+        if self.closed:
+            return
         if self.down:
-            axis, mask = self.down.pop(0)
+            mask = self.down.pop(0)
             rows = [kept.size // self.columns for kept, _ in self.parts]
             even = all(each % 32 == 0 for each in rows)
-            if self.lengths is None:
-                self.lengths = [each // 2 for each in rows] if even else rows
-                self.pieces *= 2 if even else 1
-                if not even:
-                    flat = [[side.reshape(-1, self.columns) for side in pair] for pair in self.parts]
-                    self.parts = [tuple(jnp.concatenate(sides) for sides in zip(*flat))]
+            if self.first and even:
+                self.pieces, self.lengths = 2 * self.pieces, [each // 2 for each in rows]
+            self.first = False
             if even:
-                self.up.insert(0, (axis, mask))
-                self.parts = [self.halve(axis, mask, 1, self.parts)]
+                self.up.insert(0, mask)
+                self.parts = [halve(self.order, "wide", mask, 1, self.parts, self.columns)]
             else:
-                total = self.order.run(add, *self.parts[0])
-                self.parts = [(total, swap(total, axis, mask))]
+                flat = [[side.reshape(-1, self.columns) for side in pair] for pair in self.parts]
+                pair = [jnp.concatenate(sides) for sides in zip(*flat)]
+                total = self.order.run(add, *pair)
+                self.parts = [(total, swap(total, "wide", mask))]
             return
         kept, got = [array.reshape(-1, self.columns) for array in self.parts[0]]
         if self.joining is None:
             total = self.order.run(add, kept, got)
         else:
-            bit = place_bit(*self.joining)
+            bit = place_bit("wide", self.joining)
             total = self.order.run(lambda *x: pair_up(*x, bit), kept, got).reshape(-1, self.columns)
         if self.up:
             self.joining = self.up.pop(0)
-            self.parts = [(total, swap(total, *self.joining))]
+            self.parts = [(total, swap(total, "wide", self.joining))]
         else:
             self.parts = [(total, swap(total, "wide", 1))]
             self.closed = True
+
+    def sum_rest(self):
+        rows = [kept.size // self.columns for kept, _ in self.parts]
+        flat = [[side.reshape(-1, self.columns) for side in pair] for pair in self.parts]
+        self.lengths, self.pieces = [each // 2 for each in rows], 2
+        flat = [[side.reshape(2, -1, self.columns) for side in pair] for pair in self.parts]
+        pair = [jnp.concatenate(sides, axis=1) for sides in zip(*flat)]
+        total = self.order.run(add, *pair)
+        size = lax.axis_size("wide")
+        groups = [[device + core for device in range(0, size, 2)] for core in range(2)]
+        total = lax.psum(total, "wide", axis_index_groups=groups)
+        self.parts, self.down, self.up, self.joining = [(total,)], [], [], 0
+
+    def close(self):
+        total = self.parts[0][0].reshape(-1, self.columns)
+        total = self.order.run(lambda x: x, total) if False else total
+        self.parts = [(total, swap(total, "wide", 1))]
+        self.closed = True
 
     def finish(self, done):
         own, got = [array.reshape(self.pieces, -1, self.columns) for array in self.parts[0]]
@@ -879,7 +948,7 @@
             targets = done.get(term.kind, ())
 
             def last(own, got, core, *targets, term=term, begin=begin, length=length):
-                return finish(term.kind, term.half, own, got, begin, length, core, term.layer, targets)
+                return finish(term.kind, None, own, got, begin, length, core, term.layer, targets)
 
             done[term.kind] = self.order.run(last, own, got, term.core, *targets)
             begin += length
@@ -985,64 +1054,58 @@
         line(down_biases[1]), keep,
     )
 
-    down1_term = terms_of(order, "down", 1, down_term, hidden1, dz1)
-    pending = Reduce(order, down1_term)
-    pending.apart()
+    term_down1 = Term(order, "down", 1, down_term, hidden1, dz1)
+    term_down1.pass_narrow()
     du, dm, db, do, sums1, usum1 = order.run(
         lambda y, z, s, m, g: feed_forward_back(y, z, s, down1, up1, m, g, out1),
         dz1, dz1, slope1, m1, line(gains[1, 1]),
     )
-    up1_term = terms_of(order, "up", 1, up_term, second1, du)
-    first = Reduce(order, down1_term + up1_term)
-    first.parts[0], first.passed[0] = pending.parts[0], pending.passed[0]
-    first.apart(1)
+    term_up1 = Term(order, "up", 1, up_term, second1, du)
+    term_up1.pass_narrow()
+    order.hold(term_down1.got)
     dpacked = order.run(
         lambda *x: attend_back(*x, items, seq_rows), packed1, do.reshape(items, seq_rows, width), totals1, lengths
     )
     flat_packed = dpacked.reshape(3, rows, width)
-    qkv1_terms = terms_of(order, "qkv", 1, qkv_out_term, a1, flat_packed, mixed1, db)
-    pending = Reduce(order, qkv1_terms)
-    pending.apart(0)
-    pending.apart(1)
+    term_qkv1 = Term(order, "qkv", 1, qkv_out_term, a1, flat_packed, mixed1, db)
+    term_qkv1.pass_narrow()
+    first = Reduce(order, [term_down1, term_up1])
+    first.sum_rest()
     dentry, dmiddle, dz0, skip_grad, sums3 = order.run(
         lambda gp, x, g, dm: project_back(gp, qkv1, x, g, dm, join), flat_packed, entry, line(gains[1, 0]), dm
     )
-    join_terms = terms_of(order, "join", 1, join_term, middle, skip_flat, dentry)
-    first.step()
-    second = Reduce(order, qkv1_terms + join_terms)
-    second.parts[:2], second.passed[:2] = pending.parts, pending.passed
-    second.apart(2)
-
-    down0_term = terms_of(order, "down", 0, down_term, hidden0, dz0)
-    pending = Reduce(order, down0_term, (4,))
-    pending.apart()
+    term_down0 = Term(order, "down", 0, down_term, hidden0, dz0)
+    term_down0.stay()
+    term_qkv1.pass_wide(2)
+    term_down0.pass_narrow()
+    term_join = Term(order, "join", 1, join_term, middle, skip_flat, dentry)
+    term_join.pass_narrow()
+
     du, dm, db, do, sums0, usum0 = order.run(
         lambda y, z, s, m, g: feed_forward_back(y, z, s, down0, up0, m, g, out0),
         dmiddle, dz0, slope0, m0, line(gains[0, 1]),
     )
-    up0_term = terms_of(order, "up", 0, up_term, second0, du)
-    third = Reduce(order, down0_term + up0_term, (4,))
-    third.parts[0], third.passed[0] = pending.parts[0], pending.passed[0]
-    first.step()
-    third.apart(1)
-    third.apart(0)
-    second.step()
+    term_up0 = Term(order, "up", 0, up_term, second0, du)
+    term_up0.stay()
+    term_down0.pass_wide(2)
+    term_up0.pass_narrow()
+    term_join.pass_wide(2)
     dpacked = order.run(
         lambda *x: attend_back(*x, items, seq_rows), packed0, do.reshape(items, seq_rows, width), totals0, lengths
     )
+    second = Reduce(order, [term_qkv1, term_join], (2,))
+    second.step()
     flat_packed = dpacked.reshape(3, rows, width)
-    qkv0_terms = terms_of(order, "qkv", 0, qkv_out_term, a0, flat_packed, mixed0, db)
-    first.step()
+    term_qkv0 = Term(order, "qkv", 0, qkv_out_term, a0, flat_packed, mixed0, db)
+    term_qkv0.stay()
+    term_up0.pass_wide(2)
     second.step()
-    third.apart(1)
-    fourth = Reduce(order, qkv0_terms[:1])
-    fifth = Reduce(order, qkv0_terms[1:], (4,))
-    fourth.apart()
-    fifth.apart()
-    first.step()
+    term_qkv0.pass_narrow()
     tokens_grad, sums2 = order.run(
         lambda gp, x, g, dm: project_back(gp, qkv0, x, g, dm), flat_packed, tokens_flat, line(gains[0, 0]), dm
     )
+    fourth = Reduce(order, [term_qkv0])
+    third = Reduce(order, [term_down0, term_up0], (2,))
 
     def norm_terms(place):
         return jnp.stack([jnp.stack([sums2[place], sums0[1 + place]]), jnp.stack([sums3[place], sums1[1 + place]])])
@@ -1069,43 +1132,38 @@
                 minor_got = swap(minor_sum, *minor_stages[0])
 
     done = {}
-    first.step()
     second.step()
     third.step()
     minor_step()
-    fifth.apart()
-    first.step()
+    fourth.step()
+    second.step()
+    minor_step()
+    third.step()
     second.step()
     fourth.step()
     minor_step()
     third.step()
-    fifth.step()
-    second.step()
-    first.step()
-    fourth.step()
-    minor_step()
-    third.step()
-    fifth.step()
-    first.finish(done)
+    first.close()
     second.step()
     fourth.step()
     minor_step()
     third.step()
-    fifth.step()
-    second.step()
+    first.finish(done)
     fourth.step()
+    second.finish(done)
     minor_step()
     third.step()
-    fifth.step()
-    second.finish(done)
-    for stage in range(9):
+    fourth.step()
+    third.step()
+    fourth.step()
+    third.finish(done)
+    fourth.step()
+    for each in (second, third, fourth):
+        while not each.closed:
+            each.step()
+    while minor_stages:
         minor_step()
-        for each in (fourth, third, fifth):
-            if not each.closed:
-                each.step()
-            elif each.parts:
-                each.finish(done)
-                each.parts = None
+    fourth.finish(done)
 
     owned = lax.dynamic_index_in_dim(minor_sum, me, 0, keepdims=False) * (1.0 / lax.axis_size("wide"))
     minor_sums, begin = [], 0

time: 695 us -> 667 us (0.960)
  waiting for transfers between devices: 223 us -> 161 us
  between operations: 2.26 us -> 15.7 us
  local copies, waits for them, and re-layouts: 60.2 us -> 70.9 us
  other arithmetic: 8.7 us -> 17.8 us
    ppermute x96 -> x101, waiting for transfers between devices: 223 us -> 141 us  [swap(): lax.ppermute(values, axis, [(source, source ^ mask) for source in range(s...]
    psum x0 -> x1, waiting for transfers between devices: none -> 20.1 us  [sum_rest(): total = lax.psum(total, 'wide', axis_index_groups=groups)]
    reshape x10, local copies, waits for them, and re-layouts: 0.15 us -> 8.35 us  [on_device(): both = [part[begin:end].reshape(piece.shape) for part in parts]]
    unnamed x202 -> x160, local copies, waits for them, and re-layouts: 30.1 us -> 23.1 us
    ppermute x96 -> x101, starting transfers between devices: 88.2 us -> 89.3 us  [swap(): lax.ppermute(values, axis, [(source, source ^ mask) for source in range(s...]
    pallas_call x63 -> x48, Pallas kernels: 101 us -> 102 us  [picked(): pl.pallas_call(body, grid_spec=pltpu.PrefetchScalarGridSpec(num_scalar_pr...]
  transfers between devices with their start and end apart: 96 -> 102, of which waited for: 31 -> 25; matrix products, arithmetic and copies ran while one was open for 6% -> 11% of each run, Pallas kernels for 27% -> 39%
where the time goes in v4:
time: 667 us; the launch traced here: 654 us
  Pallas kernels  300 us (45%)
  waiting for transfers between devices  161 us (24%)
  starting transfers between devices  89.3 us (13%)
  local copies, waits for them, and re-layouts  70.9 us (11%)
  other arithmetic  17.8 us (3%)
  between operations  15.7 us (2%)
    pallas_call x12, Pallas kernels, call(): pl.pallas_call(body, grid=grid, in_specs=[spec for _, spec in ins], out_s...  198 us
    ppermute x101, waiting for transfers between devices, swap(): lax.ppermute(values, axis, [(source, source ^ mask) for source in range(s...  141 us
    pallas_call x48, Pallas kernels, picked(): pl.pallas_call(body, grid_spec=pltpu.PrefetchScalarGridSpec(num_scalar_pr...  102 us
    ppermute x101, starting transfers between devices, swap(): lax.ppermute(values, axis, [(source, source ^ mask) for source in range(s...  89.3 us
    unnamed x160, local copies, waits for them, and re-layouts  23.1 us
    psum x1, waiting for transfers between devices, sum_rest(): total = lax.psum(total, 'wide', axis_index_groups=groups)  20.1 us
  transfers between devices with their start and end apart: 102, of which 25 were waited for; matrix products, arithmetic and copies ran while one was open for 11% of the time, Pallas kernels for 39%

profile of v4, /device:TPU:1, one launch (start us, length us, event | category | flops | bytes accessed | tf_op | source)
XLA Modules:
  0.0 654.4 jit_solution(8438492338347303135)
XLA Ops:
  31.8 17.6 %collective-permute-done.4 = bf16[1,8064]{1,0:T(2,128)(2,1)} collective-permute-done((bf16[1,8064]{1,0:T(2,128)(2,1)}, bf16[1,8064]{1,0:T(2,128)(2,1)}, u32[]{:S(2)}, u32[]{:S(2)}) %collective-permute-start.4) | collective-permute-done | bytes 16160 | tf_op jit(solution)/shard_map/ppermute | solution.py:825
  64.1 4.6 collective-permute-done.1.refs_3_
  75.5 6.6 %project_qkv.1 = (bf16[672,768]{1,0:T(8,128)(2,1)}, bf16[3,672,768]{2,1,0:T(8,128)(2,1)}) custom-call(s32[2]{0:T(128)} %pad_add_fusion.refs_0_, bf16[2,384,2304]{2,1,0:T(8,128)(2,1)} %refs_1_.15, bf16[1,96,2304]{2,1,0:T(8,128)(2,1)} %copy-done.49, bf16[1,96,2304]{2,1,0:T(8,128)(2,1)} %copy-done.50, bf16[1,96,2304]{2,1,0:T(8,128)(2,1)} %collective-permute-done.2.refs_4_, ...), custom_call_target="tpu_custom_call" | custom-call | flops 2100000000 | tf_op jit(solution)/shard_map/project_qkv/pallas_call | solution.py:54
  84.9 13.6 %attend.2 = (bf16[2,336,768]{2,1,0:T(8,128)(2,1)}, f32[2,6,8,336]{3,2,1,0:T(8,128)}) custom-call(s32[2]{0:T(128)} %multiply_add_fusion.length_ref, bf16[3,2,336,768]{3,2,1,0:T(8,128)(2,1)} %bitcast.184, bf16[3,2,336,768]{3,2,1,0:T(8,128)(2,1)} %bitcast.185, bf16[3,2,336,768]{3,2,1,0:T(8,128)(2,1)} %bitcast.186), custom_call_target="tpu_custom_call" | custom-call | flops 3900000000 | tf_op jit(solution)/shard_map/attend/pallas_call | solution.py:54
  103.7 6.1 collective-permute-done.11.refs_8_
  114.9 3.8 collective-permute-done.23.refs_7_.refs_2_
  125.1 24.7 %feed_forward.2 = (f32[672,768]{1,0:T(8,128)}, bf16[672,768]{1,0:T(8,128)(2,1)}, bf16[672,3072]{1,0:T(8,128)(2,1)}, bf16[672,3072]{1,0:T(8,128)(2,1)}, bf16[672,768]{1,0:T(8,128)(2,1)}) custom-call(s32[2]{0:T(128)} %pad_add_fusion.refs_0_, bf16[2,384,768]{2,1,0:T(8,128)(2,1)} %refs_11_.7, bf16[1,96,768]{2,1,0:T(8,128)(2,1)} %copy-done.57, ...), custom_call_target="tpu_custom_call" | custom-call | flops 6899999744 | tf_op jit(solution)/shard_map/feed_forward/pallas_call | solution.py:54
  156.8 11.3 %join_qkv.1 = (f32[672,768]{1,0:T(8,128)}, bf16[672,768]{1,0:T(8,128)(2,1)}, bf16[3,672,768]{2,1,0:T(8,128)(2,1)}) custom-call(s32[2]{0:T(128)} %pad_add_fusion.refs_0_, bf16[768,768]{1,0:T(8,128)(2,1)} %refs_6_.10, bf16[1,192,768]{2,1,0:T(8,128)(2,1)} %collective-permute-done.19.refs_2_.refs_7_, bf16[1,192,768]{2,1,0:T(8,128)(2,1)} %copy-done.54, ...), custom_call_target="tpu_custom_call" | custom-call | flops 3300000000 | tf_op jit(solution)/shard_map/join_qkv/pallas_call | solution.py:54
  171.6 3.2 collective-permute-done.5.refs_2_.refs_12_
  177.4 13.6 %attend.3 = (bf16[2,336,768]{2,1,0:T(8,128)(2,1)}, f32[2,6,8,336]{3,2,1,0:T(8,128)}) custom-call(s32[2]{0:T(128)} %multiply_add_fusion.length_ref, bf16[3,2,336,768]{3,2,1,0:T(8,128)(2,1)} %bitcast.190, bf16[3,2,336,768]{3,2,1,0:T(8,128)(2,1)} %bitcast.191, bf16[3,2,336,768]{3,2,1,0:T(8,128)(2,1)} %bitcast.192), custom_call_target="tpu_custom_call" | custom-call | flops 3900000000 | tf_op jit(solution)/shard_map/attend/pallas_call | solution.py:54
  196.4 25.2 %feed_forward.3 = (f32[672,768]{1,0:T(8,128)}, bf16[672,768]{1,0:T(8,128)(2,1)}, bf16[672,3072]{1,0:T(8,128)(2,1)}, bf16[672,3072]{1,0:T(8,128)(2,1)}, bf16[672,768]{1,0:T(8,128)(2,1)}) custom-call(s32[2]{0:T(128)} %pad_add_fusion.refs_0_, bf16[2,384,768]{2,1,0:T(8,128)(2,1)} %refs_11_.7, bf16[1,96,768]{2,1,0:T(8,128)(2,1)} %copy-done.61, ...), custom_call_target="tpu_custom_call" | custom-call | flops 6899999744 | tf_op jit(solution)/shard_map/feed_forward/pallas_call | solution.py:54
  221.6 5.2 down_term.4
  227.8 3.7 down_term.5
  234.4 22.6 %feed_forward_back.2 = (bf16[672,3072]{1,0:T(8,128)(2,1)}, f32[672,768]{1,0:T(8,128)}, bf16[672,768]{1,0:T(8,128)(2,1)}, bf16[672,768]{1,0:T(8,128)(2,1)}, f32[8,768]{1,0:T(8,128)}, /*index=5*/f32[1,3072]{1,0:T(1,128)}) custom-call(s32[2]{0:T(128)} %pad_add_fusion.refs_0_, bf16[2,1536,768]{2,1,0:T(8,128)(2,1)} %refs_1_.14, bf16[1,384,768]{2,1,0:T(8,128)(2,1)} %copy-done.48, ...), custom_call_target="tpu_custom_call" | custom-call | flops 6300000256 | tf_op jit(solution)/shard_map/feed_forward_back/pallas_call | solution.py:54
  257.0 3.8 up_term.4
  262.0 3.7 up_term.5
  267.6 17.3 %attend_back.2 = bf16[3,2,336,768]{3,2,1,0:T(8,128)(2,1)} custom-call(s32[2]{0:T(128)} %multiply_add_fusion.length_ref, bf16[3,2,336,768]{3,2,1,0:T(8,128)(2,1)} %bitcast.193, bf16[3,2,336,768]{3,2,1,0:T(8,128)(2,1)} %bitcast.194, bf16[3,2,336,768]{3,2,1,0:T(8,128)(2,1)} %bitcast.195, bf16[2,336,768]{2,1,0:T(8,128)(2,1)} %bitcast.183, ...), custom_call_target="tpu_custom_call" | custom-call | flops 5100000256 | tf_op jit(solution)/shard_map/attend_back/pallas_call | solution.py:54
  285.0 3.9 qkv_out_term.4
  290.3 4.1 qkv_out_term.5
  300.8 13.4 %project_back.2 = (bf16[672,768]{1,0:T(8,128)(2,1)}, f32[672,768]{1,0:T(8,128)}, bf16[672,768]{1,0:T(8,128)(2,1)}, f32[672,768]{1,0:T(8,128)}, f32[8,768]{1,0:T(8,128)}) custom-call(s32[2]{0:T(128)} %pad_add_fusion.refs_0_, bf16[2,384,2304]{2,1,0:T(8,128)(2,1)} %refs_1_.15, bf16[1,96,2304]{2,1,0:T(8,128)(2,1)} %collective-permute-done.23.refs_7_.refs_2_, ...), custom_call_target="tpu_custom_call" | custom-call | flops 3900000000 | tf_op jit(solution)/shard_map/project_back/pallas_call | solution.py:54
  315.5 5.3 down_term.6
  322.1 3.9 down_term.7
  343.9 22.6 %feed_forward_back.3 = (bf16[672,3072]{1,0:T(8,128)(2,1)}, f32[672,768]{1,0:T(8,128)}, bf16[672,768]{1,0:T(8,128)(2,1)}, bf16[672,768]{1,0:T(8,128)(2,1)}, f32[8,768]{1,0:T(8,128)}, /*index=5*/f32[1,3072]{1,0:T(1,128)}) custom-call(s32[2]{0:T(128)} %pad_add_fusion.refs_0_, bf16[2,1536,768]{2,1,0:T(8,128)(2,1)} %refs_1_.14, bf16[1,384,768]{2,1,0:T(8,128)(2,1)} %copy-done.40, ...), custom_call_target="tpu_custom_call" | custom-call | flops 6300000256 | tf_op jit(solution)/shard_map/feed_forward_back/pallas_call | solution.py:54
  366.5 5.2 up_term.6
  375.0 3.8 up_term.7
  389.8 3.9 collective-permute-done.60
  395.1 17.5 %attend_back.3 = bf16[3,2,336,768]{3,2,1,0:T(8,128)(2,1)} custom-call(s32[2]{0:T(128)} %multiply_add_fusion.length_ref, bf16[3,2,336,768]{3,2,1,0:T(8,128)(2,1)} %bitcast.187, bf16[3,2,336,768]{3,2,1,0:T(8,128)(2,1)} %bitcast.188, bf16[3,2,336,768]{3,2,1,0:T(8,128)(2,1)} %bitcast.189, bf16[2,336,768]{2,1,0:T(8,128)(2,1)} %bitcast.182, ...), custom_call_target="tpu_custom_call" | custom-call | flops 5100000256 | tf_op jit(solution)/shard_map/attend_back/pallas_call | solution.py:54
  416.8 5.2 qkv_out_term.6
  428.5 3.8 qkv_out_term.7
  439.7 2.9 cross.13
  443.3 9.8 %project_back.3 = (f32[672,768]{1,0:T(8,128)}, f32[8,768]{1,0:T(8,128)}) custom-call(s32[2]{0:T(128)} %pad_add_fusion.refs_0_, bf16[2,384,2304]{2,1,0:T(8,128)(2,1)} %refs_1_.15, bf16[1,96,2304]{2,1,0:T(8,128)(2,1)} %copy-done.49, bf16[1,96,2304]{2,1,0:T(8,128)(2,1)} %copy-done.50, bf16[1,96,2304]{2,1,0:T(8,128)(2,1)} %collective-permute-done.2.refs_4_, ...), custom_call_target="tpu_custom_call" | custom-call | flops 2700000000 | tf_op jit(solution)/shard_map/project_back/pallas_call | solution.py:54
  462.5 8.3 %collective-permute-done.76 = bf16[1,384,768]{2,1,0:T(8,128)(2,1)} collective-permute-done((bf16[1,384,768]{2,1,0:T(8,128)(2,1)}, bf16[1,384,768]{2,1,0:T(8,128)(2,1)}, u32[]{:S(2)}, u32[]{:S(2)}) %collective-permute-start.76) | collective-permute-done | bytes 589856 | tf_op jit(solution)/shard_map/ppermute | solution.py:825
  478.1 7.8 %collective-permute-done.79.got_ref = bf16[144,768]{1,0:T(8,128)(2,1)S(1)} collective-permute-done((bf16[144,768]{1,0:T(8,128)(2,1)S(1)}, bf16[144,768]{1,0:T(8,128)(2,1)S(1)}, u32[]{:S(2)}, u32[]{:S(2)}) %collective-permute-start.79) | collective-permute-done | bytes 221216 | tf_op jit(solution)/shard_map/ppermute | solution.py:825
  486.1 20.1 %all-reduce.2.cloned.1.call-done.own_ref = bf16[2,768,768]{2,1,0:T(8,128)(2,1)} async-done(((bf16[2,768,768]{2,1,0:T(8,128)(2,1)}), bf16[2,768,768]{2,1,0:T(8,128)(2,1)}) %all-reduce.2.cloned.1.call-update) | async-done | bytes 2359312 | tf_op jit(solution)/shard_map/psum | solution.py:935
  512.7 3.4 collective-permute-done.83.got_ref
  525.8 7.6 %collective-permute-done.88 = bf16[1,192,768]{2,1,0:T(8,128)(2,1)S(1)} collective-permute-done((bf16[1,192,768]{2,1,0:T(8,128)(2,1)S(1)}, bf16[1,192,768]{2,1,0:T(8,128)(2,1)S(1)}, u32[]{:S(2)}, u32[]{:S(2)}) %collective-permute-start.88) | collective-permute-done | bytes 294944 | tf_op jit(solution)/shard_map/ppermute | solution.py:825
  533.5 9.0 %collective-permute-done.87.got_ref = bf16[576,768]{1,0:T(8,128)(2,1)S(1)} collective-permute-done((bf16[576,768]{1,0:T(8,128)(2,1)S(1)}, bf16[576,768]{1,0:T(8,128)(2,1)S(1)}, u32[]{:S(2)}, u32[]{:S(2)}) %collective-permute-start.87) | collective-permute-done | bytes 884768 | tf_op jit(solution)/shard_map/ppermute | solution.py:825
  548.2 11.5 %collective-permute-done.86 = bf16[1,192,768]{2,1,0:T(8,128)(2,1)S(1)} collective-permute-done((bf16[1,192,768]{2,1,0:T(8,128)(2,1)S(1)}, bf16[1,192,768]{2,1,0:T(8,128)(2,1)S(1)}, u32[]{:S(2)}, u32[]{:S(2)}) %collective-permute-start.86) | collective-permute-done | bytes 294944 | tf_op jit(solution)/shard_map/ppermute | solution.py:825
  559.8 4.3 collective-permute-done.85
  572.0 3.0 finish_columns.2.rest_0_
  575.0 4.1 collective-permute-done.91
  579.2 3.5 finish_qkv_out.2
  585.9 3.1 collective-permute-start.94
  591.6 18.5 %collective-permute-done.97.got_ref = bf16[768,768]{1,0:T(8,128)(2,1)S(1)} collective-permute-done((bf16[768,768]{1,0:T(8,128)(2,1)S(1)}, bf16[768,768]{1,0:T(8,128)(2,1)S(1)}, u32[]{:S(2)}, u32[]{:S(2)}) %collective-permute-start.97) | collective-permute-done | bytes 1179680 | tf_op jit(solution)/shard_map/ppermute | solution.py:825
  613.1 3.7 collective-permute-start.96
  616.8 7.3 %collective-permute-done.96.got_ref = bf16[192,768]{1,0:T(8,128)(2,1)S(1)} collective-permute-done((bf16[192,768]{1,0:T(8,128)(2,1)S(1)}, bf16[192,768]{1,0:T(8,128)(2,1)S(1)}, u32[]{:S(2)}, u32[]{:S(2)}) %collective-permute-start.96) | collective-permute-done | bytes 294944 | tf_op jit(solution)/shard_map/ppermute | solution.py:825
  630.9 7.4 %collective-permute-done.98.got_ref = bf16[384,768]{1,0:T(8,128)(2,1)S(1)} collective-permute-done((bf16[384,768]{1,0:T(8,128)(2,1)S(1)}, bf16[384,768]{1,0:T(8,128)(2,1)S(1)}, u32[]{:S(2)}, u32[]{:S(2)}) %collective-permute-start.98) | collective-permute-done | bytes 589856 | tf_op jit(solution)/shard_map/ppermute | solution.py:825
  643.8 3.3 finish_qkv_out.3
  (471 shorter events, 220.9 us)
Async XLA Ops:
  7.2 499.0 %all-reduce.2.cloned.1.call-start = ((), (), s32[]{:S(2)}) async-start(), calls=%async_computation | async-start | bytes 4718592 | tf_op jit(solution)/shard_map/psum | solution.py:935
  8.3 50.1 %collective-permute-start = (bf16[1,96,2304]{2,1,0:T(8,128)(2,1)S(1)}, bf16[1,96,2304]{2,1,0:T(8,128)(2,1)S(1)}, u32[]{:S(2)}, u32[]{:S(2)}) collective-permute-start(bf16[1,96,2304]{2,1,0:T(8,128)(2,1)S(1)} %constant_dynamic-slice_fusion.7), channel_id=1, source_target_pairs={{0,1},{1,0},{2,3},{3,2},{4,5},{5,4},{6,7},{7,6},{8,9},{9,8},{10,11... | collective-permute-start | bytes 1327112 | tf_op jit(solution)/shard_map/ppermute | solution.py:825
  11.3 72.4 %collective-permute-start.6 = (bf16[1,96,768]{2,1,0:T(8,128)(2,1)S(1)}, bf16[1,96,768]{2,1,0:T(8,128)(2,1)S(1)}, u32[]{:S(2)}, u32[]{:S(2)}) collective-permute-start(bf16[1,96,768]{2,1,0:T(8,128)(2,1)S(1)} %constant_dynamic-slice_fusion.6), channel_id=1, source_target_pairs={{0,1},{1,0},{2,3},{3,2},{4,5},{5,4},{6,7},{7,6},{8,9},{9,8},{10,11... | collective-permute-start | bytes 442376 | tf_op jit(solution)/shard_map/ppermute | solution.py:825
  12.5 70.9 %collective-permute-start.10 = (bf16[1,96,3072]{2,1,0:T(8,128)(2,1)S(1)}, bf16[1,96,3072]{2,1,0:T(8,128)(2,1)S(1)}, u32[]{:S(2)}, u32[]{:S(2)}) collective-permute-start(bf16[1,96,3072]{2,1,0:T(8,128)(2,1)S(1)} %constant_dynamic-slice_fusion.5), channel_id=1, source_target_pairs={{0,1},{1,0},{2,3},{3,2},{4,5},{5,4},{6,7},{7,6},{8,9},{9,8},{10,11... | collective-permute-start | bytes 1769480 | tf_op jit(solution)/shard_map/ppermute | solution.py:825
  15.1 67.0 %collective-permute-start.14 = (bf16[1,384,768]{2,1,0:T(8,128)(2,1)S(1)}, bf16[1,384,768]{2,1,0:T(8,128)(2,1)S(1)}, u32[]{:S(2)}, u32[]{:S(2)}) collective-permute-start(bf16[1,384,768]{2,1,0:T(8,128)(2,1)S(1)} %constant_dynamic-slice_fusion.4), channel_id=1, source_target_pairs={{0,1},{1,0},{2,3},{3,2},{4,5},{5,4},{6,7},{7,6},{8,9},{9,8},{10,11... | collective-permute-start | bytes 1769480 | tf_op jit(solution)/shard_map/ppermute | solution.py:825
  28.4 21.0 %collective-permute-start.4 = (bf16[1,8064]{1,0:T(2,128)(2,1)}, bf16[1,8064]{1,0:T(2,128)(2,1)}, u32[]{:S(2)}, u32[]{:S(2)}) collective-permute-start(bf16[1,8064]{1,0:T(2,128)(2,1)} %broadcast_in_dim.16), channel_id=1, source_target_pairs={{0,1},{1,0},{2,3},{3,2},{4,5},{5,4},{6,7},{7,6},{8,9},{9,8},{10,11... | collective-permute-start | bytes 48392 | tf_op jit(solution)/shard_map/ppermute | solution.py:825
  82.2 20.6 %collective-permute-start.15 = (bf16[1,384,768]{2,1,0:T(8,128)(2,1)S(1)}, bf16[1,384,768]{2,1,0:T(8,128)(2,1)S(1)}, u32[]{:S(2)}, u32[]{:S(2)}) collective-permute-start(bf16[1,384,768]{2,1,0:T(8,128)(2,1)S(1)} %collective-permute-done.14.refs_12_.refs_2_), channel_id=1, source_target_pairs={{0,4},{2,6},{4,0},{6,2},{8,12},{10,14},{12,8},{14,10},{16,20},{18,... | collective-permute-start | bytes 1769480 | tf_op jit(solution)/shard_map/ppermute | solution.py:825
  83.4 26.5 %collective-permute-start.11 = (bf16[1,96,3072]{2,1,0:T(8,128)(2,1)S(1)}, bf16[1,96,3072]{2,1,0:T(8,128)(2,1)S(1)}, u32[]{:S(2)}, u32[]{:S(2)}) collective-permute-start(bf16[1,96,3072]{2,1,0:T(8,128)(2,1)S(1)} %collective-permute-done.10.refs_7_), channel_id=1, source_target_pairs={{0,4},{2,6},{4,0},{6,2},{8,12},{10,14},{12,8},{14,10},{16,20},{18,... | collective-permute-start | bytes 1769480 | tf_op jit(solution)/shard_map/ppermute | solution.py:825
  83.7 29.3 %collective-permute-start.7 = (bf16[1,96,768]{2,1,0:T(8,128)(2,1)S(1)}, bf16[1,96,768]{2,1,0:T(8,128)(2,1)S(1)}, u32[]{:S(2)}, u32[]{:S(2)}) collective-permute-start(bf16[1,96,768]{2,1,0:T(8,128)(2,1)S(1)} %collective-permute-done.6.refs_2_.refs_12_), channel_id=1, source_target_pairs={{0,4},{2,6},{4,0},{6,2},{8,12},{10,14},{12,8},{14,10},{16,20},{18,... | collective-permute-start | bytes 442376 | tf_op jit(solution)/shard_map/ppermute | solution.py:825
  98.5 15.3 %collective-permute-start.8 = (bf16[1,96,768]{2,1,0:T(8,128)(2,1)S(1)}, bf16[1,96,768]{2,1,0:T(8,128)(2,1)S(1)}, u32[]{:S(2)}, u32[]{:S(2)}) collective-permute-start(bf16[1,96,768]{2,1,0:T(8,128)(2,1)S(1)} %collective-permute-done.6.refs_2_.refs_12_), channel_id=1, source_target_pairs={{0,2},{2,0},{4,6},{6,4},{8,10},{10,8},{12,14},{14,12},{16,18},{18,... | collective-permute-start | bytes 442376 | tf_op jit(solution)/shard_map/ppermute | solution.py:825
  102.8 15.9 %collective-permute-start.23 = (bf16[1,96,2304]{2,1,0:T(8,128)(2,1)S(1)}, bf16[1,96,2304]{2,1,0:T(8,128)(2,1)}, u32[]{:S(2)}, u32[]{:S(2)}) collective-permute-start(bf16[1,96,2304]{2,1,0:T(8,128)(2,1)S(1)} %constant_dynamic-slice_fusion.2), channel_id=1, source_target_pairs={{0,1},{1,0},{2,3},{3,2},{4,5},{5,4},{6,7},{7,6},{8,9},{9,8},{10,11... | collective-permute-start | bytes 1327112 | tf_op jit(solution)/shard_map/ppermute | solution.py:825
  120.6 32.0 %collective-permute-start.29 = (bf16[1,96,3072]{2,1,0:T(8,128)(2,1)S(1)}, bf16[1,96,3072]{2,1,0:T(8,128)(2,1)S(1)}, u32[]{:S(2)}, u32[]{:S(2)}) collective-permute-start(bf16[1,96,3072]{2,1,0:T(8,128)(2,1)S(1)} %constant_dynamic-slice_fusion.1), channel_id=1, source_target_pairs={{0,1},{1,0},{2,3},{3,2},{4,5},{5,4},{6,7},{7,6},{8,9},{9,8},{10,11... | collective-permute-start | bytes 1769480 | tf_op jit(solution)/shard_map/ppermute | solution.py:825
  121.9 29.1 %collective-permute-start.20 = (bf16[1,192,768]{2,1,0:T(8,128)(2,1)}, bf16[1,192,768]{2,1,0:T(8,128)(2,1)S(1)}, u32[]{:S(2)}, u32[]{:S(2)}) collective-permute-start(bf16[1,192,768]{2,1,0:T(8,128)(2,1)} %collective-permute-done.19.refs_2_.refs_7_), channel_id=1, source_target_pairs={{0,4},{2,6},{4,0},{6,2},{8,12},{10,14},{12,8},{14,10},{16,20},{18,... | collective-permute-start | bytes 884744 | tf_op jit(solution)/shard_map/ppermute | solution.py:825
  122.1 27.6 %collective-permute-start.24 = (bf16[1,96,2304]{2,1,0:T(8,128)(2,1)}, bf16[1,96,2304]{2,1,0:T(8,128)(2,1)S(1)}, u32[]{:S(2)}, u32[]{:S(2)}) collective-permute-start(bf16[1,96,2304]{2,1,0:T(8,128)(2,1)} %collective-permute-done.23.refs_7_.refs_2_), channel_id=1, source_target_pairs={{0,4},{2,6},{4,0},{6,2},{8,12},{10,14},{12,8},{14,10},{16,20},{18,... | collective-permute-start | bytes 1327112 | tf_op jit(solution)/shard_map/ppermute | solution.py:825
  152.6 15.5 %collective-permute-start.33 = (bf16[1,384,768]{2,1,0:T(8,128)(2,1)S(1)}, bf16[1,384,768]{2,1,0:T(8,128)(2,1)S(1)}, u32[]{:S(2)}, u32[]{:S(2)}) collective-permute-start(bf16[1,384,768]{2,1,0:T(8,128)(2,1)S(1)} %constant_dynamic-slice_fusion), channel_id=1, source_target_pairs={{0,1},{1,0},{2,3},{3,2},{4,5},{5,4},{6,7},{7,6},{8,9},{9,8},{10,11... | collective-permute-start | bytes 1769480 | tf_op jit(solution)/shard_map/ppermute | solution.py:825
  154.9 36.3 %collective-permute-start.30 = (bf16[1,96,3072]{2,1,0:T(8,128)(2,1)S(1)}, bf16[1,96,3072]{2,1,0:T(8,128)(2,1)}, u32[]{:S(2)}, u32[]{:S(2)}) collective-permute-start(bf16[1,96,3072]{2,1,0:T(8,128)(2,1)S(1)} %collective-permute-done.29.refs_7_), channel_id=1, source_target_pairs={{0,4},{2,6},{4,0},{6,2},{8,12},{10,14},{12,8},{14,10},{16,20},{18,... | collective-permute-start | bytes 1769480 | tf_op jit(solution)/shard_map/ppermute | solution.py:825
  168.1 23.4 %collective-permute-start.34 = (bf16[1,384,768]{2,1,0:T(8,128)(2,1)S(1)}, bf16[1,384,768]{2,1,0:T(8,128)(2,1)}, u32[]{:S(2)}, u32[]{:S(2)}) collective-permute-start(bf16[1,384,768]{2,1,0:T(8,128)(2,1)S(1)} %collective-permute-done.33.refs_12_.refs_2_), channel_id=1, source_target_pairs={{0,4},{2,6},{4,0},{6,2},{8,12},{10,14},{12,8},{14,10},{16,20},{18,... | collective-permute-start | bytes 1769480 | tf_op jit(solution)/shard_map/ppermute | solution.py:825
  174.8 16.9 %collective-permute-start.18 = (bf16[1,96,768]{2,1,0:T(8,128)(2,1)S(1)}, bf16[1,96,768]{2,1,0:T(8,128)(2,1)S(1)}, u32[]{:S(2)}, u32[]{:S(2)}) collective-permute-start(bf16[1,96,768]{2,1,0:T(8,128)(2,1)S(1)} %collective-permute-done.5.refs_2_.refs_12_), channel_id=1, source_target_pairs={{0,4},{2,6},{4,0},{6,2},{8,12},{10,14},{12,8},{14,10},{16,20},{18,... | collective-permute-start | bytes 442376 | tf_op jit(solution)/shard_map/ppermute | solution.py:825
  175.1 21.3 %collective-permute-start.31 = (bf16[1,96,3072]{2,1,0:T(8,128)(2,1)S(1)}, bf16[1,96,3072]{2,1,0:T(8,128)(2,1)}, u32[]{:S(2)}, u32[]{:S(2)}) collective-permute-start(bf16[1,96,3072]{2,1,0:T(8,128)(2,1)S(1)} %collective-permute-done.29.refs_7_), channel_id=1, source_target_pairs={{0,2},{2,0},{4,6},{6,4},{8,10},{10,8},{12,14},{14,12},{16,18},{18,... | collective-permute-start | bytes 1769480 | tf_op jit(solution)/shard_map/ppermute | solution.py:825
  233.3 34.3 %collective-permute-start.45 = (bf16[2,384,768]{2,1,0:T(8,128)(2,1)S(1)}, bf16[2,384,768]{2,1,0:T(8,128)(2,1)S(1)}, u32[]{:S(2)}, u32[]{:S(2)}) collective-permute-start(bf16[2,384,768]{2,1,0:T(8,128)(2,1)S(1)} %get-tuple-element.508), channel_id=1, source_target_pairs={{0,1},{1,0},{2,3},{3,2},{4,5},{5,4},{6,7},{7,6},{8,9},{9,8},{10,11... | collective-permute-start | bytes 3538952 | tf_op jit(solution)/shard_map/ppermute | solution.py:825
  267.3 27.2 %collective-permute-start.46 = (bf16[2,384,768]{2,1,0:T(8,128)(2,1)S(1)}, bf16[2,384,768]{2,1,0:T(8,128)(2,1)}, u32[]{:S(2)}, u32[]{:S(2)}) collective-permute-start(bf16[2,384,768]{2,1,0:T(8,128)(2,1)S(1)} %get-tuple-element.538), channel_id=1, source_target_pairs={{0,1},{1,0},{2,3},{3,2},{4,5},{5,4},{6,7},{7,6},{8,9},{9,8},{10,11... | collective-permute-start | bytes 3538952 | tf_op jit(solution)/shard_map/ppermute | solution.py:825
  297.7 28.2 %collective-permute-start.55 = (bf16[2,384,768]{2,1,0:T(8,128)(2,1)}, bf16[2,384,768]{2,1,0:T(8,128)(2,1)S(1)}, u32[]{:S(2)}, u32[]{:S(2)}) collective-permute-start(bf16[2,384,768]{2,1,0:T(8,128)(2,1)} %get-tuple-element.571), channel_id=1, source_target_pairs={{0,1},{1,0},{2,3},{3,2},{4,5},{5,4},{6,7},{7,6},{8,9},{9,8},{10,11... | collective-permute-start | bytes 3538952 | tf_op jit(solution)/shard_map/ppermute | solution.py:825
  338.6 40.3 %collective-permute-start.65 = (bf16[2,384,768]{2,1,0:T(8,128)(2,1)}, bf16[2,384,768]{2,1,0:T(8,128)(2,1)}, u32[]{:S(2)}, u32[]{:S(2)}) collective-permute-start(bf16[2,384,768]{2,1,0:T(8,128)(2,1)} %copy-done.26), channel_id=1, source_target_pairs={{0,1},{1,0},{2,3},{3,2},{4,5},{5,4},{6,7},{7,6},{8,9},{9,8},{10,11... | collective-permute-start | bytes 3538952 | tf_op jit(solution)/shard_map/ppermute | solution.py:825
  383.8 41.4 %collective-permute-start.73 = (bf16[2,384,768]{2,1,0:T(8,128)(2,1)}, bf16[2,384,768]{2,1,0:T(8,128)(2,1)}, u32[]{:S(2)}, u32[]{:S(2)}) collective-permute-start(bf16[2,384,768]{2,1,0:T(8,128)(2,1)} %get-tuple-element.665), channel_id=1, source_target_pairs={{0,1},{1,0},{2,3},{3,2},{4,5},{5,4},{6,7},{7,6},{8,9},{9,8},{10,11... | collective-permute-start | bytes 3538952 | tf_op jit(solution)/shard_map/ppermute | solution.py:825
  387.0 25.6 %collective-permute-start.66 = (bf16[1,384,768]{2,1,0:T(8,128)(2,1)}, bf16[1,384,768]{2,1,0:T(8,128)(2,1)}, u32[]{:S(2)}, u32[]{:S(2)}) collective-permute-start(bf16[1,384,768]{2,1,0:T(8,128)(2,1)} %get-tuple-element.598), channel_id=1, source_target_pairs={{0,4},{2,6},{4,0},{6,2},{8,12},{10,14},{12,8},{14,10},{16,20},{18,... | collective-permute-start | bytes 1769480 | tf_op jit(solution)/shard_map/ppermute | solution.py:825
  393.8 18.8 %collective-permute-start.67 = (bf16[1,192,768]{2,1,0:T(8,128)(2,1)S(1)}, bf16[1,192,768]{2,1,0:T(8,128)(2,1)S(1)}, u32[]{:S(2)}, u32[]{:S(2)}) collective-permute-start(bf16[1,192,768]{2,1,0:T(8,128)(2,1)S(1)} %get-tuple-element.668), channel_id=1, source_target_pairs={{0,4},{2,6},{4,0},{6,2},{8,12},{10,14},{12,8},{14,10},{16,20},{18,... | collective-permute-start | bytes 884744 | tf_op jit(solution)/shard_map/ppermute | solution.py:825
  415.5 18.9 %collective-permute-start.72 = (bf16[1,288,768]{2,1,0:T(8,128)(2,1)}, bf16[1,288,768]{2,1,0:T(8,128)(2,1)S(1)}, u32[]{:S(2)}, u32[]{:S(2)}) collective-permute-start(bf16[1,288,768]{2,1,0:T(8,128)(2,1)} %get-tuple-element.681), channel_id=1, source_target_pairs={{0,8},{2,10},{4,12},{6,14},{8,0},{10,2},{12,4},{14,6},{16,24},{18,... | collective-permute-start | bytes 1327112 | tf_op jit(solution)/shard_map/ppermute | solution.py:825
  424.7 15.0 %collective-permute-start.70 = (bf16[384,768]{1,0:T(8,128)(2,1)}, bf16[384,768]{1,0:T(8,128)(2,1)}, u32[]{:S(2)}, u32[]{:S(2)}) collective-permute-start(bf16[384,768]{1,0:T(8,128)(2,1)} %get-tuple-element.696), channel_id=1, source_target_pairs={{0,2},{2,0},{4,6},{6,4},{8,10},{10,8},{12,14},{14,12},{16,18},{18,... | collective-permute-start | bytes 1769480 | tf_op jit(solution)/shard_map/ppermute | solution.py:825
  434.5 28.1 %collective-permute-start.75 = (bf16[1,384,768]{2,1,0:T(8,128)(2,1)}, bf16[1,384,768]{2,1,0:T(8,128)(2,1)}, u32[]{:S(2)}, u32[]{:S(2)}) collective-permute-start(bf16[1,384,768]{2,1,0:T(8,128)(2,1)} %get-tuple-element.656), channel_id=1, source_target_pairs={{0,4},{2,6},{4,0},{6,2},{8,12},{10,14},{12,8},{14,10},{16,20},{18,... | collective-permute-start | bytes 1769480 | tf_op jit(solution)/shard_map/ppermute | solution.py:825
  436.1 34.7 %collective-permute-start.76 = (bf16[1,384,768]{2,1,0:T(8,128)(2,1)}, bf16[1,384,768]{2,1,0:T(8,128)(2,1)}, u32[]{:S(2)}, u32[]{:S(2)}) collective-permute-start(bf16[1,384,768]{2,1,0:T(8,128)(2,1)} %get-tuple-element.702), channel_id=1, source_target_pairs={{0,4},{2,6},{4,0},{6,2},{8,12},{10,14},{12,8},{14,10},{16,20},{18,... | collective-permute-start | bytes 1769480 | tf_op jit(solution)/shard_map/ppermute | solution.py:825
  437.4 23.9 %collective-permute-start.77 = (bf16[1,144,768]{2,1,0:T(8,128)(2,1)}, bf16[1,144,768]{2,1,0:T(8,128)(2,1)}, u32[]{:S(2)}, u32[]{:S(2)}) collective-permute-start(bf16[1,144,768]{2,1,0:T(8,128)(2,1)} %get-tuple-element.705), channel_id=1, source_target_pairs={{0,16},{2,18},{4,20},{6,22},{8,24},{10,26},{12,28},{14,30},{16,0},... | collective-permute-start | bytes 663560 | tf_op jit(solution)/shard_map/ppermute | solution.py:825
  442.6 34.2 %collective-permute-start.80 = (bf16[2,384,768]{2,1,0:T(8,128)(2,1)}, bf16[2,384,768]{2,1,0:T(8,128)(2,1)S(1)}, u32[]{:S(2)}, u32[]{:S(2)}) collective-permute-start(bf16[2,384,768]{2,1,0:T(8,128)(2,1)} %get-tuple-element.714), channel_id=1, source_target_pairs={{0,1},{1,0},{2,3},{3,2},{4,5},{5,4},{6,7},{7,6},{8,9},{9,8},{10,11... | collective-permute-start | bytes 3538952 | tf_op jit(solution)/shard_map/ppermute | solution.py:825
  462.4 23.5 %collective-permute-start.79 = (bf16[144,768]{1,0:T(8,128)(2,1)S(1)}, bf16[144,768]{1,0:T(8,128)(2,1)S(1)}, u32[]{:S(2)}, u32[]{:S(2)}) collective-permute-start(bf16[144,768]{1,0:T(8,128)(2,1)S(1)} %add_convert_fusion.2.own_ref), channel_id=1, source_target_pairs={{0,16},{2,18},{4,20},{6,22},{8,24},{10,26},{12,28},{14,30},{16,0},... | collective-permute-start | bytes 663560 | tf_op jit(solution)/shard_map/ppermute | solution.py:825
  473.1 37.3 %collective-permute-start.84 = (bf16[1,384,768]{2,1,0:T(8,128)(2,1)}, bf16[1,384,768]{2,1,0:T(8,128)(2,1)}, u32[]{:S(2)}, u32[]{:S(2)}) collective-permute-start(bf16[1,384,768]{2,1,0:T(8,128)(2,1)} %get-tuple-element.736), channel_id=1, source_target_pairs={{0,8},{2,10},{4,12},{6,14},{8,0},{10,2},{12,4},{14,6},{16,24},{18,... | collective-permute-start | bytes 1769480 | tf_op jit(solution)/shard_map/ppermute | solution.py:825
  486.0 30.1 %collective-permute-start.83 = (bf16[288,768]{1,0:T(8,128)(2,1)S(1)}, bf16[288,768]{1,0:T(8,128)(2,1)S(1)}, u32[]{:S(2)}, u32[]{:S(2)}) collective-permute-start(bf16[288,768]{1,0:T(8,128)(2,1)S(1)} %bitcast.144), channel_id=1, source_target_pairs={{0,8},{2,10},{4,12},{6,14},{8,0},{10,2},{12,4},{14,6},{16,24},{18,... | collective-permute-start | bytes 1327112 | tf_op jit(solution)/shard_map/ppermute | solution.py:825
  486.1 23.5 %collective-permute-start.78 = (f32[2,8064]{1,0:T(2,128)}, f32[2,8064]{1,0:T(2,128)S(1)}, u32[]{:S(2)}, u32[]{:S(2)}) collective-permute-start(f32[2,8064]{1,0:T(2,128)} %add.69), channel_id=1, source_target_pairs={{0,4},{2,6},{4,0},{6,2},{8,12},{10,14},{12,8},{14,10},{16,20},{18,... | collective-permute-start | bytes 193544 | tf_op jit(solution)/shard_map/ppermute | solution.py:825
  506.2 63.2 %collective-permute-start.92 = (bf16[1536,768]{1,0:T(8,128)(2,1)}, bf16[1536,768]{1,0:T(8,128)(2,1)S(1)}, u32[]{:S(2)}, u32[]{:S(2)}) collective-permute-start(bf16[1536,768]{1,0:T(8,128)(2,1)} %bitcast.112), channel_id=1, source_target_pairs={{0,2},{2,0},{4,6},{6,4},{8,10},{10,8},{12,14},{14,12},{16,18},{18,... | collective-permute-start | bytes 7077896 | tf_op jit(solution)/shard_map/ppermute | solution.py:825
  506.9 16.6 %collective-permute-start.82 = (bf16[1,384,768]{2,1,0:T(8,128)(2,1)}, bf16[1,384,768]{2,1,0:T(8,128)(2,1)S(1)}, u32[]{:S(2)}, u32[]{:S(2)}) collective-permute-start(bf16[1,384,768]{2,1,0:T(8,128)(2,1)} %copy-done.31), channel_id=1, source_target_pairs={{0,4},{2,6},{4,0},{6,2},{8,12},{10,14},{12,8},{14,10},{16,20},{18,... | collective-permute-start | bytes 1769480 | tf_op jit(solution)/shard_map/ppermute | solution.py:825
  516.2 26.3 %collective-permute-start.87 = (bf16[576,768]{1,0:T(8,128)(2,1)S(1)}, bf16[576,768]{1,0:T(8,128)(2,1)S(1)}, u32[]{:S(2)}, u32[]{:S(2)}) collective-permute-start(bf16[576,768]{1,0:T(8,128)(2,1)S(1)} %bitcast.129), channel_id=1, source_target_pairs={{0,4},{2,6},{4,0},{6,2},{8,12},{10,14},{12,8},{14,10},{16,20},{18,... | collective-permute-start | bytes 2654216 | tf_op jit(solution)/shard_map/ppermute | solution.py:825
  517.8 15.6 %collective-permute-start.88 = (bf16[1,192,768]{2,1,0:T(8,128)(2,1)S(1)}, bf16[1,192,768]{2,1,0:T(8,128)(2,1)S(1)}, u32[]{:S(2)}, u32[]{:S(2)}) collective-permute-start(bf16[1,192,768]{2,1,0:T(8,128)(2,1)S(1)} %get-tuple-element.751), channel_id=1, source_target_pairs={{0,16},{2,18},{4,20},{6,22},{8,24},{10,26},{12,28},{14,30},{16,0},... | collective-permute-start | bytes 884744 | tf_op jit(solution)/shard_map/ppermute | solution.py:825
  542.6 36.6 %collective-permute-start.90 = (bf16[1152,768]{1,0:T(8,128)(2,1)S(1)}, bf16[1152,768]{1,0:T(8,128)(2,1)S(1)}, u32[]{:S(2)}, u32[]{:S(2)}) collective-permute-start(bf16[1152,768]{1,0:T(8,128)(2,1)S(1)} %bitcast.107), channel_id=1, source_target_pairs={{0,2},{2,0},{4,6},{6,4},{8,10},{10,8},{12,14},{14,12},{16,18},{18,... | collective-permute-start | bytes 5308424 | tf_op jit(solution)/shard_map/ppermute | solution.py:825
  543.2 16.5 %collective-permute-start.86 = (bf16[1,192,768]{2,1,0:T(8,128)(2,1)S(1)}, bf16[1,192,768]{2,1,0:T(8,128)(2,1)S(1)}, u32[]{:S(2)}, u32[]{:S(2)}) collective-permute-start(bf16[1,192,768]{2,1,0:T(8,128)(2,1)S(1)} %get-tuple-element.756), channel_id=1, source_target_pairs={{0,8},{2,10},{4,12},{6,14},{8,0},{10,2},{12,4},{14,6},{16,24},{18,... | collective-permute-start | bytes 884744 | tf_op jit(solution)/shard_map/ppermute | solution.py:825
  545.8 18.3 %collective-permute-start.93 = (bf16[192,768]{1,0:T(8,128)(2,1)S(1)}, bf16[192,768]{1,0:T(8,128)(2,1)S(1)}, u32[]{:S(2)}, u32[]{:S(2)}) collective-permute-start(bf16[192,768]{1,0:T(8,128)(2,1)S(1)} %add_convert_fusion.1.own_ref), channel_id=1, source_target_pairs={{0,16},{2,18},{4,20},{6,22},{8,24},{10,26},{12,28},{14,30},{16,0},... | collective-permute-start | bytes 884744 | tf_op jit(solution)/shard_map/ppermute | solution.py:825
  547.2 16.9 %collective-permute-start.85 = (f32[2,8064]{1,0:T(2,128)S(1)}, f32[2,8064]{1,0:T(2,128)S(1)}, u32[]{:S(2)}, u32[]{:S(2)}) collective-permute-start(f32[2,8064]{1,0:T(2,128)S(1)} %add.71), channel_id=1, source_target_pairs={{0,16},{2,18},{4,20},{6,22},{8,24},{10,26},{12,28},{14,30},{16,0},... | collective-permute-start | bytes 193544 | tf_op jit(solution)/shard_map/ppermute | solution.py:825
  564.2 20.1 %collective-permute-start.95 = (bf16[384,768]{1,0:T(8,128)(2,1)S(1)}, bf16[384,768]{1,0:T(8,128)(2,1)S(1)}, u32[]{:S(2)}, u32[]{:S(2)}) collective-permute-start(bf16[384,768]{1,0:T(8,128)(2,1)S(1)} %bitcast.131), channel_id=1, source_target_pairs={{0,8},{2,10},{4,12},{6,14},{8,0},{10,2},{12,4},{14,6},{16,24},{18,... | collective-permute-start | bytes 1769480 | tf_op jit(solution)/shard_map/ppermute | solution.py:825
  567.2 17.1 %collective-permute-start.89 = (f32[2,8064]{1,0:T(2,128)S(1)}, f32[2,8064]{1,0:T(2,128)S(1)}, u32[]{:S(2)}, u32[]{:S(2)}) collective-permute-start(f32[2,8064]{1,0:T(2,128)S(1)} %add.73), channel_id=1, source_target_pairs={{0,1},{1,0},{2,3},{3,2},{4,5},{5,4},{6,7},{7,6},{8,9},{9,8},{10,11... | collective-permute-start | bytes 193544 | tf_op jit(solution)/shard_map/ppermute | solution.py:825
  584.4 25.7 %collective-permute-start.97 = (bf16[768,768]{1,0:T(8,128)(2,1)S(1)}, bf16[768,768]{1,0:T(8,128)(2,1)S(1)}, u32[]{:S(2)}, u32[]{:S(2)}) collective-permute-start(bf16[768,768]{1,0:T(8,128)(2,1)S(1)} %bitcast.118), channel_id=1, source_target_pairs={{0,4},{2,6},{4,0},{6,2},{8,12},{10,14},{12,8},{14,10},{16,20},{18,... | collective-permute-start | bytes 3538952 | tf_op jit(solution)/shard_map/ppermute | solution.py:825
  610.2 15.4 %collective-permute-start.99 = (bf16[1536,768]{1,0:T(8,128)(2,1)S(1)}, bf16[1536,768]{1,0:T(8,128)(2,1)S(1)}, u32[]{:S(2)}, u32[]{:S(2)}) collective-permute-start(bf16[1536,768]{1,0:T(8,128)(2,1)S(1)} %bitcast.104), channel_id=1, source_target_pairs={{0,2},{2,0},{4,6},{6,4},{8,10},{10,8},{12,14},{14,12},{16,18},{18,... | collective-permute-start | bytes 7077896 | tf_op jit(solution)/shard_map/ppermute | solution.py:825
  (129 other events, 1074.6 us)
Sparse Core Ops, SparseCore 0:
  373.7 132.5 all-reduce.1
